TPU v7x, 32 devices: a whole 2x2x4 slice. The times are simulated.
32 devices in a mesh: shard: 8 (over z, x), grp: 4 (over y, core).
Axes of the slice: x: 2, y: 2, z: 4, core: 2. Of those that a mesh axis runs over, the one named last changes fastest.
Arguments:
- embeddings: bfloat16 [8192, 1024], P('shard', 'grp')
- clusters: int32 [8192], P('shard'), may hold values from 0 to 3, as said below
- blocks: int32 [32, 4], P('shard'), may hold values from 0 to 31, as said below
- counts: int32 [32], P('shard'), may hold values from 1 to 4
- seed_mask: int32 [8192], P(('shard', 'grp')), may hold values 0 or 1
- prior: bfloat16 [8192, 256], P(('shard', 'grp')), may hold values from 0 to 1
Outputs:
- labels: bfloat16 [8192, 256], P(('shard', 'grp'))
Inputs may be any that keep to these rules, and one draw needn't show every extreme that they name: `blocks`: slot 0 of row tile r is r itself; the other slots hold distinct tiles of the same shard or of the first 2 tiles of the next shard, never past the last tile; slots at or past counts hold such tiles too but carry no affinity. `clusters`: images 2m and 2m + 1 share a cluster.
All inputs are finite; a program needn't handle non-finite values. No bound on the sum of `seed_mask` on one device may be relied on, other than what follows from the above.
Results may differ from a plain program's by a relative error of at most 0.0038.
Values may be sent and summed in bfloat16 or wider, within the bound.
No kernel may reach another device: no remote copies, remote signals or barrier semaphores. Data moves between devices by JAX's collectives and lax.ppermute only.
A program may use at most 64 MiB of HBM per device.

v0:
```python
import jax
import jax.numpy as jnp
from jax import lax
from jax.sharding import PartitionSpec as P

TILE = 256
K = 4
SPILL = 2
STEPS = 2


kernel_width = 0.06
spread_weight = 0.6


def passed_along(block, axis, distance):
    devices = range(lax.axis_size(axis))
    route = [(i - distance, i) for i in devices if i - distance in devices]
    return lax.ppermute(block, axis, route)


def local(embeddings, clusters, blocks, counts, seed_mask, prior):
    groups = lax.axis_size("grp")
    member = lax.axis_index("grp")
    shard_base = lax.axis_index("shard") * groups
    spill_rows = SPILL * TILE
    wtiles = groups + SPILL
    width = embeddings.shape[1]
    next_x, next_c = passed_along((embeddings[:spill_rows], clusters[:spill_rows]), "shard", -1)
    window_x = jnp.concatenate([embeddings, next_x], axis=0)
    window_c = jnp.concatenate([clusters, next_c], axis=0).reshape(wtiles, TILE)
    local_ids = blocks - shard_base
    own_ids = lax.dynamic_index_in_dim(local_ids, member, 0, keepdims=False)
    tiles_x = window_x.reshape(wtiles, TILE, width)
    tile_norms = jnp.sum(jnp.square(tiles_x.astype(jnp.float32)), axis=-1)
    ntiles = TILE * lax.axis_size("grp") // TILE
    first = jnp.int32(0) // TILE
    rows_x = lax.dynamic_slice_in_dim(tiles_x, first, ntiles, 0)
    rows_n = lax.dynamic_slice_in_dim(tile_norms, first, ntiles, 0)
    cols_x = tiles_x[local_ids]
    cols_n = tile_norms[local_ids]
    dots = jnp.einsum("rif,rkjf->rikj", rows_x, cols_x, preferred_element_type=jnp.float32)
    term = rows_n[:, :, None, None] + cols_n[:, None, :, :] - 2.0 * dots
    dist = lax.psum_scatter(
        term.reshape(TILE * lax.axis_size("grp"), K * TILE), "grp", scatter_dimension=0, tiled=True
    ).reshape(TILE, K, TILE)
    own_c = lax.dynamic_index_in_dim(window_c, member, 0, keepdims=False)
    col_c = window_c[own_ids]
    slot_index = jnp.arange(K, dtype=jnp.int32)
    image_index = jnp.arange(TILE, dtype=jnp.int32)
    live = slot_index < lax.dynamic_index_in_dim(counts, member, 0, keepdims=False)
    same = own_c[:, None, None] == col_c[None, :, :]
    itself = (own_ids[None, :, None] == member) & (
        image_index[:, None, None] == image_index[None, None, :]
    )
    allowed = same & live[None, :, None] & jnp.logical_not(itself)
    logits = -dist / kernel_width
    top = jnp.max(jnp.where(allowed, logits, jnp.float32(-1e30)), axis=(1, 2), keepdims=True)
    weights = jnp.where(allowed, jnp.exp(logits - top), jnp.float32(0.0))
    total = jnp.sum(weights, axis=(1, 2), keepdims=True)
    affinity = (weights / total).astype(jnp.bfloat16)
    seeds = seed_mask.astype(jnp.float32)[:, None] * prior.astype(jnp.float32)
    labels = seeds.astype(jnp.bfloat16)
    for step in range(STEPS):
        shard_labels = lax.all_gather(labels, "grp", axis=0, tiled=True)
        spill_labels = passed_along(shard_labels[:spill_rows], "shard", -1)
        window_l = jnp.concatenate([shard_labels, spill_labels], axis=0).reshape(
            wtiles, TILE, labels.shape[1]
        )
        picked = window_l[own_ids]
        spread = jnp.einsum("ikj,kjc->ic", affinity, picked, preferred_element_type=jnp.float32)
        labels = (spread_weight * spread + (1.0 - spread_weight) * seeds).astype(jnp.bfloat16)
    return labels


def solution(mesh):
    in_specs = (
        P("shard", "grp"),
        P("shard"),
        P("shard", None),
        P("shard"),
        P(("shard", "grp")),
        P(("shard", "grp"), None),
    )
    out_specs = P(("shard", "grp"), None)
    return jax.shard_map(local, mesh=mesh, in_specs=in_specs, out_specs=out_specs, check_vma=False)
```

profile of v0, /device:TPU:11, one launch (start us, length us, event | category | flops | bytes accessed | tf_op | source)
XLA Modules:
  0.0 108.8 jit_solution(7340198877987223764)
XLA Ops:
  6.5 0.0 reduce-scatter.2.cloned.1.call-start
  6.5 1.0 slice.21
  7.5 2.2 %collective-permute-start.1 = (bf16[512,256]{1,0:T(8,128)(2,1)S(1)}, bf16[512,256]{1,0:T(8,128)(2,1)S(1)}, u32[]{:S(2)}, u32[]{:S(2)}) collective-permute-start(bf16[512,256]{1,0:T(8,128)(2,1)S(1)} %slice.21), channel_id=1, source_target_pairs={{4,0},{8,4},{12,8},{16,12},{20,16},{24,20},{28,24},{5,1},{9,5},{13... | collective-permute-start | bytes 786440 | tf_op jit(solution)/shard_map/ppermute | solution.py:19
  9.7 0.7 compare_select_fusion
  10.4 0.1 reshape.113
  10.5 1.1 constant_dynamic-update-slice_fusion.1
  11.5 5.9 %collective-permute-done.1 = bf16[512,256]{1,0:T(8,128)(2,1)S(1)} collective-permute-done((bf16[512,256]{1,0:T(8,128)(2,1)S(1)}, bf16[512,256]{1,0:T(8,128)(2,1)S(1)}, u32[]{:S(2)}, u32[]{:S(2)}) %collective-permute-start.1) | collective-permute-done | bytes 262176 | tf_op jit(solution)/shard_map/ppermute | solution.py:19
  17.5 0.3 multiply_reduce_fusion
  17.8 0.0 copy-start
  17.8 0.7 gather_fusion.2
  18.5 0.6 gather_fusion.1
  19.1 0.0 copy-done
  19.1 2.5 %bitcast_subtract_fusion = f32[4,256,4,256]{1,3,2,0:T(8,128)} fusion(bf16[4,4,256,256]{3,2,1,0:T(8,128)(2,1)S(1)} %bitcast.51, bf16[4,256,256,1]{2,1,3,0:T(8,128)(2,1)S(1)} %bitcast.52, f32[4,4,256]{2,1,0:T(4,128)S(1)} %reshape.112, f32[4,256]{1,0:T(4,128)S(1)} %dynamic_slice.24), kind=kOutput, calls=%fused_computation.5 | convolution fusion | flops 540016640 | bytes 6836224 | tf_op jit(solution)/shard_map/rif,rkjf->rikj/dot_general | solution.py:42
  21.6 5.2 %copy.7 = f32[4,256,4,256]{3,2,1,0:T(4,128)} copy(f32[4,256,4,256]{1,3,2,0:T(8,128)} %bitcast_subtract_fusion) | data formatting | bytes 8388608 | tf_op jit(solution)/shard_map/sub | solution.py:43
  26.8 5.2 %copy.15 = f32[128,8,4,256]{3,1,2,0:T(8,128)} copy(f32[128,8,4,256]{3,2,1,0:T(4,128)} %bitcast.49) | data formatting | bytes 8388608
  32.0 0.0 copy-start.2
  32.0 0.0 copy-start.3
  32.0 0.0 copy-start.1
  32.0 0.0 copy-start.4
  32.0 0.0 reduce-scatter.2.cloned.1.call-update
  32.0 0.7 copy-done.2
  32.7 1.9 %collective-permute-start = (s32[512]{0:T(512)S(1)}, s32[512]{0:T(512)S(1)}, u32[]{:S(2)}, u32[]{:S(2)}) collective-permute-start(s32[512]{0:T(512)S(1)} %slice.20), channel_id=1, source_target_pairs={{4,0},{8,4},{12,8},{16,12},{20,16},{24,20},{28,24},{5,1},{9,5},{13... | collective-permute-start | bytes 6152 | tf_op jit(solution)/shard_map/ppermute | solution.py:19
  34.6 0.0 copy-done.3
  34.6 0.0 copy-done.1
  34.6 0.1 fusion.7
  34.7 8.6 %all_gather.6 = bf16[1024,256]{1,0:T(8,128)(2,1)S(1)} all-gather(bf16[256,256]{1,0:T(8,128)(2,1)S(1)} %fusion.7), channel_id=1, replica_groups=mesh['shard'=8,'grp'=4] {'grp'}, dimensions={0}, use_global_device_ids=true | all-gather | bytes 655360 | tf_op jit(solution)/shard_map/all_gather | solution.py:65
  43.4 3.5 %collective-permute-start.2 = (bf16[512,256]{1,0:T(8,128)(2,1)S(1)}, bf16[512,256]{1,0:T(8,128)(2,1)S(1)}, u32[]{:S(2)}, u32[]{:S(2)}) collective-permute-start(bf16[512,256]{1,0:T(8,128)(2,1)S(1)} %slice.34), channel_id=1, source_target_pairs={{4,0},{8,4},{12,8},{16,12},{20,16},{24,20},{28,24},{5,1},{9,5},{13... | collective-permute-start | bytes 786440 | tf_op jit(solution)/shard_map/ppermute | solution.py:19
  46.9 0.0 copy-done.4
  46.9 0.6 dynamic_slice.22
  47.6 0.7 iota_compare_fusion.1
  48.2 0.1 and.60
  48.3 0.4 copy.9
  48.7 0.1 and.67
  48.8 0.1 and.63
  48.9 0.0 collective-permute-done
  48.9 0.6 gather_fusion
  49.5 5.0 %collective-permute-done.2 = bf16[512,256]{1,0:T(8,128)(2,1)S(1)} collective-permute-done((bf16[512,256]{1,0:T(8,128)(2,1)S(1)}, bf16[512,256]{1,0:T(8,128)(2,1)S(1)}, u32[]{:S(2)}, u32[]{:S(2)}) %collective-permute-start.2) | collective-permute-done | bytes 262176 | tf_op jit(solution)/shard_map/ppermute | solution.py:19
  54.5 0.1 pad_maximum_fusion
  54.5 0.6 gather_fusion.3
  55.1 22.6 %reduce-scatter.2.cloned.1.call-done = f32[256,1024]{1,0:T(8,128)} async-done(((f32[1024,1024]{1,0:T(8,128)}), f32[256,1024]{1,0:T(8,128)}) %reduce-scatter.2.cloned.1.call-update) | async-done | bytes 1048592 | tf_op jit(solution)/shard_map/reduce_scatter | solution.py:44
  77.7 1.7 %select_reduce_fusion.1 = f32[256]{0:T(256)S(1)} fusion(f32[256,1024]{1,0:T(8,128)} %reduce-scatter.2.cloned.1.call-done, pred[256,1024]{1,0:T(8,128)(4,1)S(1)} %copy.9, pred[1024]{0:T(1024)(128)(4,1)S(1)} %and.68, pred[1024]{0:T(1024)(128)(4,1)S(1)} %and.64, s32[1024]{0:T(1024)S(1)} %bitcast.57, s32[256]{0:T(256)S(1)} %bitcast.60), kind=kLoop, calls=%fused_computation.17 | loop fusion | flops 2359040 | bytes 1318912 | tf_op jit(solution)/shard_map/reduce_max | solution.py:58
  79.4 1.8 %select_reduce_fusion = (f32[256]{0:T(256)S(1)}, f32[256,1024]{1,0:T(8,128)S(1)}) fusion(f32[256]{0:T(256)S(1)} %select_reduce_fusion.1, f32[256,1024]{1,0:T(8,128)} %reduce-scatter.2.cloned.1.call-done, pred[256,1024]{1,0:T(8,128)(4,1)S(1)} %copy.9, pred[1024]{0:T(1024)(128)(4,1)S(1)} %and.68, pred[1024]{0:T(1024)(128)(4,1)S(1)} %and.64, ...), kind=kLoop, calls=%fused_computation.16 | loop fusion | flops 2621184 | bytes 2368512 | tf_op jit(solution)/shard_map/reduce_sum | solution.py:60
  81.3 0.3 copy.8
  81.6 0.5 divide_convert_fusion
  82.1 0.4 fusion.5
  82.5 7.3 %all_gather.7 = bf16[1024,256]{1,0:T(8,128)(2,1)S(1)} all-gather(bf16[256,256]{1,0:T(8,128)(2,1)S(1)} %fusion.5), channel_id=1, replica_groups=mesh['shard'=8,'grp'=4] {'grp'}, dimensions={0}, use_global_device_ids=true | all-gather | bytes 655360 | tf_op jit(solution)/shard_map/all_gather | solution.py:65
  89.8 2.2 %collective-permute-start.3 = (bf16[512,256]{1,0:T(8,128)(2,1)S(1)}, bf16[512,256]{1,0:T(8,128)(2,1)S(1)}, u32[]{:S(2)}, u32[]{:S(2)}) collective-permute-start(bf16[512,256]{1,0:T(8,128)(2,1)S(1)} %slice.35), channel_id=1, source_target_pairs={{4,0},{8,4},{12,8},{16,12},{20,16},{24,20},{28,24},{5,1},{9,5},{13... | collective-permute-start | bytes 786440 | tf_op jit(solution)/shard_map/ppermute | solution.py:19
  92.0 8.4 %collective-permute-done.3 = bf16[512,256]{1,0:T(8,128)(2,1)S(1)} collective-permute-done((bf16[512,256]{1,0:T(8,128)(2,1)S(1)}, bf16[512,256]{1,0:T(8,128)(2,1)S(1)}, u32[]{:S(2)}, u32[]{:S(2)}) %collective-permute-start.3) | collective-permute-done | bytes 262176 | tf_op jit(solution)/shard_map/ppermute | solution.py:19
  100.3 0.1 pad_maximum_fusion.1
  100.4 0.6 gather_fusion.4
  101.0 1.0 fusion.4
  (20 shorter events, 0.2 us)
Async XLA Ops:
  6.5 71.2 %reduce-scatter.2.cloned.1.call-start = ((), (), s32[]{:S(2)}) async-start(), calls=%async_computation.1 | async-start | bytes 5242880 | tf_op jit(solution)/shard_map/reduce_scatter | solution.py:44
  7.5 10.0 %collective-permute-start.1 = (bf16[512,256]{1,0:T(8,128)(2,1)S(1)}, bf16[512,256]{1,0:T(8,128)(2,1)S(1)}, u32[]{:S(2)}, u32[]{:S(2)}) collective-permute-start(bf16[512,256]{1,0:T(8,128)(2,1)S(1)} %slice.21), channel_id=1, source_target_pairs={{4,0},{8,4},{12,8},{16,12},{20,16},{24,20},{28,24},{5,1},{9,5},{13... | collective-permute-start | bytes 786440 | tf_op jit(solution)/shard_map/ppermute | solution.py:19
  17.8 1.3 %copy-start = (bf16[1024,256]{1,0:T(8,128)(2,1)S(1)}, bf16[1024,256]{1,0:T(8,128)(2,1)}, u32[]{:S(2)}) copy-start(bf16[1024,256]{1,0:T(8,128)(2,1)} %param.6) | copy-start | bytes 1572868
  32.0 0.7 copy-start.2
  32.0 2.6 %copy-start.3 = (s32[256]{0:T(256)S(1)}, s32[256]{0:T(256)}, u32[]{:S(2)}) copy-start(s32[256]{0:T(256)} %param.10) | copy-start | bytes 3076
  32.0 2.6 %copy-start.1 = (bf16[256,256]{1,0:T(8,128)(2,1)S(1)}, bf16[256,256]{1,0:T(8,128)(2,1)}, u32[]{:S(2)}) copy-start(bf16[256,256]{1,0:T(8,128)(2,1)} %param.11) | copy-start | bytes 393220
  32.0 14.9 %copy-start.4 = (s32[4]{0:T(128)S(1)}, s32[4]{0:T(128)}, u32[]{:S(2)}) copy-start(s32[4]{0:T(128)} %param.9) | copy-start | bytes 52
  32.7 16.2 %collective-permute-start = (s32[512]{0:T(512)S(1)}, s32[512]{0:T(512)S(1)}, u32[]{:S(2)}, u32[]{:S(2)}) collective-permute-start(s32[512]{0:T(512)S(1)} %slice.20), channel_id=1, source_target_pairs={{4,0},{8,4},{12,8},{16,12},{20,16},{24,20},{28,24},{5,1},{9,5},{13... | collective-permute-start | bytes 6152 | tf_op jit(solution)/shard_map/ppermute | solution.py:19
  43.4 11.1 %collective-permute-start.2 = (bf16[512,256]{1,0:T(8,128)(2,1)S(1)}, bf16[512,256]{1,0:T(8,128)(2,1)S(1)}, u32[]{:S(2)}, u32[]{:S(2)}) collective-permute-start(bf16[512,256]{1,0:T(8,128)(2,1)S(1)} %slice.34), channel_id=1, source_target_pairs={{4,0},{8,4},{12,8},{16,12},{20,16},{24,20},{28,24},{5,1},{9,5},{13... | collective-permute-start | bytes 786440 | tf_op jit(solution)/shard_map/ppermute | solution.py:19
  89.8 10.5 %collective-permute-start.3 = (bf16[512,256]{1,0:T(8,128)(2,1)S(1)}, bf16[512,256]{1,0:T(8,128)(2,1)S(1)}, u32[]{:S(2)}, u32[]{:S(2)}) collective-permute-start(bf16[512,256]{1,0:T(8,128)(2,1)S(1)} %slice.35), channel_id=1, source_target_pairs={{4,0},{8,4},{12,8},{16,12},{20,16},{24,20},{28,24},{5,1},{9,5},{13... | collective-permute-start | bytes 786440 | tf_op jit(solution)/shard_map/ppermute | solution.py:19
Sparse Core Ops, SparseCore 0:
  32.2 45.5 reduce-scatter.1
where the time goes:
time: 110 us; the launch traced here: 109 us
  waiting for transfers between devices  41.9 us (38%)
  local copies, waits for them, and re-layouts  17.8 us (16%)
  blocking collectives  15.9 us (14%)
  between operations  13.7 us (12%)
  starting transfers between devices  9.74 us (9%)
  other arithmetic  5.96 us (5%)
  matrix products  3.84 us (3%)
    reduce_scatter x1, waiting for transfers between devices, local(): lax.psum_scatter(term.reshape(TILE * lax.axis_size('grp'), K * TILE), 'gr...  22.6 us
    ppermute x4, waiting for transfers between devices, passed_along(): return lax.ppermute(block, axis, route)  19.2 us
    all_gather x2, blocking collectives, local(): shard_labels = lax.all_gather(labels, 'grp', axis=0, tiled=True)  15.9 us
    ppermute x4, starting transfers between devices, passed_along(): return lax.ppermute(block, axis, route)  9.74 us
    unnamed x13, local copies, waits for them, and re-layouts  6.92 us
    sub x1, local copies, waits for them, and re-layouts, local(): term = rows_n[:, :, None, None] + cols_n[:, None, :, :] - 2.0 * dots  5.22 us
    dot_general x1, matrix products, local(): jnp.einsum('rif,rkjf->rikj', rows_x, cols_x, preferred_element_type=jnp.f...  2.48 us
  transfers between devices with their start and end apart: 5, of which 4 were waited for; matrix products, arithmetic and copies ran while one was open for 5% of the time, Pallas kernels for 0%

commit v1 on v0

v1 whole, which is shorter than its diff:
```python
import functools

import jax
import jax.numpy as jnp
from jax import lax
from jax.experimental import pallas as pl
from jax.experimental.pallas import tpu as pltpu
from jax.sharding import PartitionSpec as P

TILE = 256
K = 4
SPILL = 2
ROWS = 32

kernel_width = 0.06
spread_weight = 0.6
MASKED = -1e30

NT = (((1,), (1,)), ((), ()))


def across(block, distance):
    groups = lax.axis_size("grp")
    return lax.ppermute(block, "grp", [(i, i ^ distance) for i in range(groups)])


def from_next(block):
    return lax.ppermute(block, "shard", [(i + 1, i) for i in range(lax.axis_size("shard") - 1)])


def from_next_heads(block, pair):
    groups = lax.axis_size("grp")
    route = [
        ((i + 1) * groups + c, i * groups + 2 * pair + c)
        for i in range(lax.axis_size("shard") - 1)
        for c in range(2)
    ]
    return lax.ppermute(block, ("shard", "grp"), route)


def listed(blocks_ref, counts_ref, groups):
    member = lax.axis_index("grp")
    base = lax.axis_index("shard") * groups
    count = counts_ref[member]
    ids = [blocks_ref[member, k] - base for k in range(K)]
    return [
        sum(jnp.where((ids[k] == w) & (k < count), 1, 0) for k in range(K))
        for w in range(groups + SPILL)
    ]


def spread(aff_ref, own_refs, spill_refs, seed, groups):
    member = lax.axis_index("grp")
    core = lax.rem(member, 2)
    total = jnp.zeros(seed.shape, jnp.float32)
    for m, ref in enumerate(own_refs):
        total += jnp.dot(aff_ref[member ^ m], ref[...], preferred_element_type=jnp.float32)
    for m, ref in enumerate(spill_refs):
        total += jnp.dot(
            aff_ref[groups + (core ^ m)], ref[...], preferred_element_type=jnp.float32
        )
    return (spread_weight * total + (1.0 - spread_weight) * seed.astype(jnp.float32)).astype(
        jnp.bfloat16
    )


def affinity_kernel(groups, blocks_ref, counts_ref, clusters_ref, spill_c_ref, *refs):
    quarters = groups
    half = groups // 2
    wtiles = groups + SPILL
    refs = list(refs)
    own_x = [[refs.pop(0) for _ in range(1 if q < 2 else 2)] for q in range(quarters)]
    spill_x = [refs.pop(0) for _ in range(quarters)]
    own_l = [refs.pop(0) for _ in range(groups)]
    spill_l = [refs.pop(0) for _ in range(SPILL)]
    labels_ref, aff_ref, rows_ref, logit_ref, normi_ref = refs
    member = lax.axis_index("grp")
    mult = listed(blocks_ref, counts_ref, groups)
    spill_rows = SPILL * TILE

    for q in range(quarters):
        if len(own_x[q]) == 1:
            rows_ref[q] = own_x[q][0][pl.ds(pl.multiple_of(member * TILE, TILE), TILE), :]
        else:
            @pl.when(member < SPILL)
            def _(q=q):
                rows_ref[q] = own_x[q][0][pl.ds(pl.multiple_of(member * TILE, TILE), TILE), :]

            @pl.when(member >= SPILL)
            def _(q=q):
                at = pl.multiple_of((member - SPILL) * TILE, TILE)
                rows_ref[q] = own_x[q][1][pl.ds(at, TILE), :]

    def columns(w, q):
        if w >= groups:
            return spill_x[q][(w - groups) * TILE:(w - groups + 1) * TILE, :]
        if len(own_x[q]) == 1:
            return own_x[q][0][w * TILE:(w + 1) * TILE, :]
        if w < SPILL:
            return own_x[q][0][w * TILE:(w + 1) * TILE, :]
        return own_x[q][1][(w - SPILL) * TILE:(w - SPILL + 1) * TILE, :]

    def cluster_row(w):
        if w >= groups:
            return spill_c_ref[:, (w - groups) * TILE:(w - groups + 1) * TILE]
        return clusters_ref[:, w * TILE:(w + 1) * TILE]

    eye = lax.broadcasted_iota(jnp.int32, (TILE, TILE), 0) == lax.broadcasted_iota(
        jnp.int32, (TILE, TILE), 1
    )

    def as_column(row):
        return jnp.sum(jnp.where(eye, row, jnp.zeros_like(row)), axis=1, keepdims=True)

    def norm_row(tiles):
        squares = sum(
            jnp.square(t[:, h * 128:(h + 1) * 128].astype(jnp.float32))
            for t in tiles
            for h in range(t.shape[1] // 128)
        )
        ones = jnp.ones((8, 128), jnp.float32)
        return lax.dot_general(
            ones, squares, NT, precision=lax.Precision.HIGHEST,
            preferred_element_type=jnp.float32,
        )[0:1]

    own_n = norm_row([rows_ref[q] for q in range(quarters)])
    normi = as_column(own_n)
    own_c = clusters_ref[:, pl.ds(pl.multiple_of(member * TILE, TILE), TILE)]
    row_c = as_column(own_c.astype(jnp.float32))

    for w in range(wtiles):
        @pl.when(mult[w] > 0)
        def _(w=w):
            tiles = [columns(w, q) for q in range(quarters)]
            norm = norm_row(tiles)
            dots = sum(
                lax.dot_general(rows_ref[q], tiles[q], NT, preferred_element_type=jnp.float32)
                for q in range(quarters)
            )
            dist = normi + norm - 2.0 * dots
            same = row_c == cluster_row(w).astype(jnp.float32)
            allowed = same & jnp.logical_not(eye & (member == w))
            logit_ref[w] = jnp.where(allowed, dist * (-1.0 / kernel_width), MASKED)

        @pl.when(mult[w] == 0)
        def _(w=w):
            logit_ref[w] = jnp.full((TILE, TILE), MASKED, jnp.float32)

    factors = [m.astype(jnp.float32) for m in mult]

    def softmax(step, carry):
        rows = pl.ds(pl.multiple_of(step * ROWS, ROWS), ROWS)
        logits = [logit_ref[w, rows, :] for w in range(wtiles)]
        top = functools.reduce(jnp.maximum, logits)
        top = jnp.max(top, axis=1, keepdims=True)
        weights = [jnp.exp(logits[w] - top) * factors[w] for w in range(wtiles)]
        total = jnp.sum(functools.reduce(jnp.add, weights), axis=1, keepdims=True)
        scale = 1.0 / total
        for w in range(wtiles):
            aff_ref[w, rows, :] = (weights[w] * scale).astype(jnp.bfloat16)
        return carry

    lax.fori_loop(0, TILE // ROWS, softmax, 0, unroll=True)
    labels_ref[...] = spread(aff_ref, own_l, spill_l, own_l[0][...], groups)


def spread_kernel(groups, aff_ref, seed_ref, *refs):
    own_l = refs[:groups]
    spill_parts = refs[groups:-2]
    out_ref, got_ref = refs[-2:]
    pair = lax.axis_index("grp") // 2
    for k in range(groups // 2):
        @pl.when(pair == k)
        def _(k=k):
            for t in range(SPILL):
                got_ref[t] = spill_parts[k * SPILL + t][...]
    out_ref[...] = spread(
        aff_ref, own_l, [got_ref.at[t] for t in range(SPILL)], seed_ref[...], groups
    )


def local(embeddings, clusters, blocks, counts, seed_mask, prior):
    groups = lax.axis_size("grp")
    member = lax.axis_index("grp")
    spill_rows = SPILL * TILE
    width = prior.shape[1]

    head, tail = embeddings[:spill_rows], embeddings[spill_rows:]
    seeds = seed_mask.astype(jnp.bfloat16)[:, None] * prior

    own_x, spill_x = [], []
    head_far = [across(head, 2 * m) for m in range(1, groups // 2)]
    spill_near = from_next(head)
    spill_c = from_next(clusters[:spill_rows])
    tail_far = [across(tail, 2 * m) for m in range(1, groups // 2)]
    own_sib = across(embeddings, 1)
    spill_far = [from_next(h) for h in head_far]
    labels_far = [across(seeds, 2 * m) for m in range(1, groups // 2)]
    first = seeds
    for m in range(1, groups // 2):
        first = jnp.where(member // 2 == m, labels_far[m - 1], first)
    spill_l0 = from_next(first)

    own_x = [[embeddings], [own_sib]]
    spill_x = [spill_near, across(spill_near, 1)]
    own_l = [seeds, across(seeds, 1)]
    for m in range(groups // 2 - 1):
        own_x += [[head_far[m], tail_far[m]], [across(head_far[m], 1), across(tail_far[m], 1)]]
        spill_x += [spill_far[m], across(spill_far[m], 1)]
        own_l += [labels_far[m], across(labels_far[m], 1)]
    spill_l = [spill_l0, across(spill_l0, 1)]

    arrays = [x for xs in own_x for x in xs] + spill_x + own_l + spill_l
    smem = pl.BlockSpec(memory_space=pltpu.SMEM)
    vmem = pl.BlockSpec(memory_space=pltpu.VMEM)
    wtiles = groups + SPILL
    labels, affinity = pl.pallas_call(
        functools.partial(affinity_kernel, groups),
        out_shape=(
            jax.ShapeDtypeStruct((TILE, width), jnp.bfloat16),
            jax.ShapeDtypeStruct((wtiles, TILE, TILE), jnp.bfloat16),
        ),
        in_specs=[smem, smem] + [vmem] * (2 + len(arrays)),
        out_specs=(vmem, vmem),
        scratch_shapes=[
            pltpu.VMEM((groups, TILE, embeddings.shape[1]), jnp.bfloat16),
            pltpu.VMEM((wtiles, TILE, TILE), jnp.float32),
            pltpu.VMEM((TILE, 1), jnp.float32),
        ],
        compiler_params=pltpu.CompilerParams(vmem_limit_bytes=40 * 1024 * 1024),
        name="affinity",
    )(blocks, counts, clusters.reshape(1, -1), spill_c.reshape(1, -1), *arrays)

    far = [across(labels, 2 * m) for m in range(1, groups // 2)]
    heads = [from_next_heads(labels, m) for m in range(groups // 2)]
    own_l = [labels, across(labels, 1)]
    for f in far:
        own_l += [f, across(f, 1)]
    parts = []
    for h in heads:
        parts += [h, across(h, 1)]
    return pl.pallas_call(
        functools.partial(spread_kernel, groups),
        out_shape=jax.ShapeDtypeStruct((TILE, width), jnp.bfloat16),
        in_specs=[vmem] * (2 + groups + len(parts)),
        out_specs=vmem,
        scratch_shapes=[pltpu.VMEM((SPILL, TILE, width), jnp.bfloat16)],
        compiler_params=pltpu.CompilerParams(vmem_limit_bytes=40 * 1024 * 1024),
        name="spread",
    )(affinity, seeds, *own_l, *parts)


def solution(mesh):
    in_specs = (
        P("shard", "grp"),
        P("shard"),
        P("shard", None),
        P("shard"),
        P(("shard", "grp")),
        P(("shard", "grp"), None),
    )
    out_specs = P(("shard", "grp"), None)
    return jax.shard_map(local, mesh=mesh, in_specs=in_specs, out_specs=out_specs, check_vma=False)
```

time: 110 us -> 49.9 us (0.45)
  waiting for transfers between devices: 41.9 us -> 12.3 us
  starting transfers between devices: 9.74 us -> 29.5 us
  local copies, waits for them, and re-layouts: 17.8 us -> 1.74 us
  blocking collectives: 15.9 us -> 0 us
  between operations: 13.7 us -> 0.15 us
  other arithmetic: 5.96 us -> 1.78 us
  matrix products: 3.84 us -> 0 us
  Pallas kernels: 0 us -> 3.5 us
    reduce_scatter x1 -> x0, waiting for transfers between devices: 22.6 us -> none  [local(): lax.psum_scatter(term.reshape(TILE * lax.axis_size('grp'), K * TILE), 'gr...]
    ppermute x4 -> x22, starting transfers between devices: 9.74 us -> 29.5 us  [the longest x16 13.5 us: across(): lax.ppermute(block, 'grp', [(i, i ^ distance) for i in range(groups)])]
    all_gather x2 -> x0, blocking collectives: 15.9 us -> none  [local(): shard_labels = lax.all_gather(labels, 'grp', axis=0, tiled=True)]
    ppermute x4 -> x22, waiting for transfers between devices: 19.2 us -> 12.3 us  [the longest x4 5.69 us: from_next(): lax.ppermute(block, 'shard', [(i + 1, i) for i in range(lax.axis_size('sh...]
    unnamed x13 -> x10, local copies, waits for them, and re-layouts: 6.92 us -> 0.67 us
    sub x1 -> x0, local copies, waits for them, and re-layouts: 5.22 us -> none  [local(): term = rows_n[:, :, None, None] + cols_n[:, None, :, :] - 2.0 * dots]
    dot_general x3 -> x0, matrix products: 3.84 us -> none  [the longest x1 2.48 us: local(): jnp.einsum('rif,rkjf->rikj', rows_x, cols_x, preferred_element_type=jnp.f...]
    pallas_call x0 -> x2, Pallas kernels: none -> 3.5 us  [the longest x1 2.45 us: local(): pl.pallas_call(functools.partial(affinity_kernel, groups), out_shape=(jax...]
  transfers between devices with their start and end apart: 5 -> 22, of which waited for: 4 -> 7; matrix products, arithmetic and copies ran while one was open for 5% -> 2% of each run, Pallas kernels for 0% -> 0%
where the time goes in v1:
time: 49.9 us; the launch traced here: 49 us
  starting transfers between devices  29.5 us (59%)
  waiting for transfers between devices  12.3 us (25%)
  Pallas kernels  3.5 us (7%)
  other arithmetic  1.78 us (4%)
  local copies, waits for them, and re-layouts  1.74 us (3%)
    ppermute x16, starting transfers between devices, across(): lax.ppermute(block, 'grp', [(i, i ^ distance) for i in range(groups)])  13.5 us
    ppermute x4, starting transfers between devices, from_next(): lax.ppermute(block, 'shard', [(i + 1, i) for i in range(lax.axis_size('sh...  9.55 us
    ppermute x2, starting transfers between devices, from_next_heads(): return lax.ppermute(block, ('shard', 'grp'), route)  6.46 us
    ppermute x4, waiting for transfers between devices, from_next(): lax.ppermute(block, 'shard', [(i + 1, i) for i in range(lax.axis_size('sh...  5.69 us
    ppermute x2, waiting for transfers between devices, from_next_heads(): return lax.ppermute(block, ('shard', 'grp'), route)  3.69 us
    ppermute x16, waiting for transfers between devices, across(): lax.ppermute(block, 'grp', [(i, i ^ distance) for i in range(groups)])  2.96 us
    pallas_call x1, Pallas kernels, local(): pl.pallas_call(functools.partial(affinity_kernel, groups), out_shape=(jax...  2.45 us
    slice x1, local copies, waits for them, and re-layouts, local(): head, tail = (embeddings[:spill_rows], embeddings[spill_rows:])  1.06 us
  transfers between devices with their start and end apart: 22, of which 7 were waited for; matrix products, arithmetic and copies ran while one was open for 2% of the time, Pallas kernels for 0%

profile of v1, /device:TPU:11, one launch (start us, length us, event | category | flops | bytes accessed | tf_op | source)
XLA Modules:
  0.0 49.0 jit_solution(16348857902148896748)
XLA Ops:
  0.0 0.7 %convert_element_type.3 = bf16[256]{0:T(256)(128)(2,1)S(1)} convert(s32[256]{0:T(256)} %param.10) | non-fusion elementwise | flops 256 | bytes 1536 | tf_op jit(solution)/shard_map/convert_element_type | solution.py:190
  0.7 1.0 %broadcast_multiply_fusion.refs_10_.seed_ref = bf16[256,256]{1,0:T(8,128)(2,1)S(1)} fusion(bf16[256,256]{1,0:T(8,128)(2,1)} %param.11, bf16[256]{0:T(256)(128)(2,1)S(1)} %convert_element_type.3), kind=kLoop, calls=%fused_computation.1 | loop fusion | flops 65536 | bytes 262656 | tf_op jit(solution)/shard_map/mul | solution.py:190
  1.7 0.0 copy-start.4
  1.7 0.0 copy-start
  1.7 1.3 %collective-permute-start.11 = (bf16[256,256]{1,0:T(8,128)(2,1)S(1)}, bf16[256,256]{1,0:T(8,128)(2,1)S(1)}, u32[]{:S(2)}, u32[]{:S(2)}) collective-permute-start(bf16[256,256]{1,0:T(8,128)(2,1)S(1)} %broadcast_multiply_fusion.refs_10_.seed_ref), channel_id=1, source_target_pairs={{0,2},{1,3},{2,0},{3,1},{4,6},{5,7},{6,4},{7,5},{8,10},{9,11},{10,... | collective-permute-start | bytes 393224 | tf_op jit(solution)/shard_map/ppermute | solution.py:24
  3.0 1.0 %collective-permute-start.10 = (bf16[256,256]{1,0:T(8,128)(2,1)S(1)}, bf16[256,256]{1,0:T(8,128)(2,1)S(1)}, u32[]{:S(2)}, u32[]{:S(2)}) collective-permute-start(bf16[256,256]{1,0:T(8,128)(2,1)S(1)} %broadcast_multiply_fusion.refs_10_.seed_ref), channel_id=1, source_target_pairs={{0,1},{1,0},{2,3},{3,2},{4,5},{5,4},{6,7},{7,6},{8,9},{9,8},{10,11... | collective-permute-start | bytes 393224 | tf_op jit(solution)/shard_map/ppermute | solution.py:24
  4.0 1.1 %fusion = (bf16[512,256]{1,0:T(8,128)(2,1)S(1)}, bf16[512,256]{1,0:T(8,128)(2,1)S(1)}) fusion(bf16[1024,256]{1,0:T(8,128)(2,1)} %refs_0_.1), kind=kLoop, calls=%fused_computation.2 | loop fusion | bytes 1048576 | tf_op jit(solution)/shard_map/slice | solution.py:189
  5.0 0.3 collective-permute-start.2
  5.3 0.0 copy-start.1
  5.3 0.8 %collective-permute-done.11.refs_12_ = bf16[256,256]{1,0:T(8,128)(2,1)S(1)} collective-permute-done((bf16[256,256]{1,0:T(8,128)(2,1)S(1)}, bf16[256,256]{1,0:T(8,128)(2,1)S(1)}, u32[]{:S(2)}, u32[]{:S(2)}) %collective-permute-start.11) | collective-permute-done | bytes 131104 | tf_op jit(solution)/shard_map/ppermute | solution.py:24
  6.1 0.0 copy-done.4
  6.1 0.1 broadcast_select_fusion
  6.3 2.2 %collective-permute-start.13 = (bf16[256,256]{1,0:T(8,128)(2,1)S(1)}, bf16[256,256]{1,0:T(8,128)(2,1)S(1)}, u32[]{:S(2)}, u32[]{:S(2)}) collective-permute-start(bf16[256,256]{1,0:T(8,128)(2,1)S(1)} %broadcast_select_fusion), channel_id=1, source_target_pairs={{4,0},{8,4},{12,8},{16,12},{20,16},{24,20},{28,24},{5,1},{9,5},{13... | collective-permute-start | bytes 393224 | tf_op jit(solution)/shard_map/ppermute | solution.py:28
  8.4 0.0 copy-done.1
  8.4 3.0 %collective-permute-start = (s32[512]{0:T(512)S(1)}, s32[512]{0:T(512)S(1)}, u32[]{:S(2)}, u32[]{:S(2)}) collective-permute-start(s32[512]{0:T(512)S(1)} %slice.9), channel_id=1, source_target_pairs={{4,0},{8,4},{12,8},{16,12},{20,16},{24,20},{28,24},{5,1},{9,5},{13... | collective-permute-start | bytes 6152 | tf_op jit(solution)/shard_map/ppermute | solution.py:28
  11.5 2.3 %collective-permute-start.6 = (bf16[512,256]{1,0:T(8,128)(2,1)S(1)}, bf16[512,256]{1,0:T(8,128)(2,1)S(1)}, u32[]{:S(2)}, u32[]{:S(2)}) collective-permute-start(bf16[512,256]{1,0:T(8,128)(2,1)S(1)} %get-tuple-element.10), channel_id=1, source_target_pairs={{4,0},{8,4},{12,8},{16,12},{20,16},{24,20},{28,24},{5,1},{9,5},{13... | collective-permute-start | bytes 786440 | tf_op jit(solution)/shard_map/ppermute | solution.py:28
  13.7 0.3 collective-permute-done
  14.0 0.0 copy-start.2
  14.0 1.0 %collective-permute-start.3 = (bf16[512,256]{1,0:T(8,128)(2,1)S(1)}, bf16[512,256]{1,0:T(8,128)(2,1)S(1)}, u32[]{:S(2)}, u32[]{:S(2)}) collective-permute-start(bf16[512,256]{1,0:T(8,128)(2,1)S(1)} %get-tuple-element.9), channel_id=1, source_target_pairs={{0,2},{1,3},{2,0},{3,1},{4,6},{5,7},{6,4},{7,5},{8,10},{9,11},{10,... | collective-permute-start | bytes 786440 | tf_op jit(solution)/shard_map/ppermute | solution.py:24
  15.0 0.0 collective-permute-done.10.refs_11_
  15.0 3.7 %collective-permute-start.12 = (bf16[256,256]{1,0:T(8,128)(2,1)S(1)}, bf16[256,256]{1,0:T(8,128)(2,1)S(1)}, u32[]{:S(2)}, u32[]{:S(2)}) collective-permute-start(bf16[256,256]{1,0:T(8,128)(2,1)S(1)} %collective-permute-done.11.refs_12_), channel_id=1, source_target_pairs={{0,1},{1,0},{2,3},{3,2},{4,5},{5,4},{6,7},{7,6},{8,9},{9,8},{10,11... | collective-permute-start | bytes 393224 | tf_op jit(solution)/shard_map/ppermute | solution.py:24
  18.6 0.0 collective-permute-done.13.refs_14_
  18.7 0.0 copy-done
  18.7 0.1 collective-permute-start.1
  18.7 0.0 collective-permute-done.2.refs_2_
  18.7 2.1 %collective-permute-start.8 = (bf16[512,256]{1,0:T(8,128)(2,1)S(1)}, bf16[512,256]{1,0:T(8,128)(2,1)S(1)}, u32[]{:S(2)}, u32[]{:S(2)}) collective-permute-start(bf16[512,256]{1,0:T(8,128)(2,1)S(1)} %collective-permute-done.2.refs_2_), channel_id=1, source_target_pairs={{4,0},{8,4},{12,8},{16,12},{20,16},{24,20},{28,24},{5,1},{9,5},{13... | collective-permute-start | bytes 786440 | tf_op jit(solution)/shard_map/ppermute | solution.py:28
  20.9 0.0 collective-permute-done.12.refs_13_
  20.9 0.8 %collective-permute-start.14 = (bf16[256,256]{1,0:T(8,128)(2,1)S(1)}, bf16[256,256]{1,0:T(8,128)(2,1)S(1)}, u32[]{:S(2)}, u32[]{:S(2)}) collective-permute-start(bf16[256,256]{1,0:T(8,128)(2,1)S(1)} %collective-permute-done.13.refs_14_), channel_id=1, source_target_pairs={{0,1},{1,0},{2,3},{3,2},{4,5},{5,4},{6,7},{7,6},{8,9},{9,8},{10,11... | collective-permute-start | bytes 393224 | tf_op jit(solution)/shard_map/ppermute | solution.py:24
  21.7 0.0 collective-permute-done.3.refs_3_
  21.7 1.4 %collective-permute-start.5 = (bf16[512,256]{1,0:T(8,128)(2,1)S(1)}, bf16[512,256]{1,0:T(8,128)(2,1)S(1)}, u32[]{:S(2)}, u32[]{:S(2)}) collective-permute-start(bf16[512,256]{1,0:T(8,128)(2,1)S(1)} %collective-permute-done.3.refs_3_), channel_id=1, source_target_pairs={{0,1},{1,0},{2,3},{3,2},{4,5},{5,4},{6,7},{7,6},{8,9},{9,8},{10,11... | collective-permute-start | bytes 786440 | tf_op jit(solution)/shard_map/ppermute | solution.py:24
  23.0 0.0 collective-permute-done.6.refs_6_
  23.0 0.0 collective-permute-start.7
  23.0 0.0 collective-permute-done.14.refs_15_
  23.0 0.5 %collective-permute-start.4 = (bf16[512,256]{1,0:T(8,128)(2,1)S(1)}, bf16[512,256]{1,0:T(8,128)(2,1)S(1)}, u32[]{:S(2)}, u32[]{:S(2)}) collective-permute-start(bf16[512,256]{1,0:T(8,128)(2,1)S(1)} %collective-permute-done.2.refs_2_), channel_id=1, source_target_pairs={{0,1},{1,0},{2,3},{3,2},{4,5},{5,4},{6,7},{7,6},{8,9},{9,8},{10,11... | collective-permute-start | bytes 786440 | tf_op jit(solution)/shard_map/ppermute | solution.py:24
  23.5 5.4 %collective-permute-done.8.refs_8_ = bf16[512,256]{1,0:T(8,128)(2,1)S(1)} collective-permute-done((bf16[512,256]{1,0:T(8,128)(2,1)S(1)}, bf16[512,256]{1,0:T(8,128)(2,1)S(1)}, u32[]{:S(2)}, u32[]{:S(2)}) %collective-permute-start.8) | collective-permute-done | bytes 262176 | tf_op jit(solution)/shard_map/ppermute | solution.py:28
  29.0 1.3 %collective-permute-start.9 = (bf16[512,256]{1,0:T(8,128)(2,1)S(1)}, bf16[512,256]{1,0:T(8,128)(2,1)S(1)}, u32[]{:S(2)}, u32[]{:S(2)}) collective-permute-start(bf16[512,256]{1,0:T(8,128)(2,1)S(1)} %collective-permute-done.8.refs_8_), channel_id=1, source_target_pairs={{0,1},{1,0},{2,3},{3,2},{4,5},{5,4},{6,7},{7,6},{8,9},{9,8},{10,11... | collective-permute-start | bytes 786440 | tf_op jit(solution)/shard_map/ppermute | solution.py:24
  30.2 0.0 collective-permute-done.5.refs_5_
  30.2 0.0 collective-permute-done.7.refs_7_
  30.2 0.0 collective-permute-done.4.refs_4_
  30.3 0.0 collective-permute-done.1.refs_1_
  30.3 1.1 %collective-permute-done.9.refs_9_ = bf16[512,256]{1,0:T(8,128)(2,1)S(1)} collective-permute-done((bf16[512,256]{1,0:T(8,128)(2,1)S(1)}, bf16[512,256]{1,0:T(8,128)(2,1)S(1)}, u32[]{:S(2)}, u32[]{:S(2)}) %collective-permute-start.9) | collective-permute-done | bytes 262176 | tf_op jit(solution)/shard_map/ppermute | solution.py:24
  31.4 0.0 copy-start.3
  31.4 0.0 copy-done.2
  31.4 0.7 %copy-done.3 = s32[4]{0:T(128)S(1)} copy-done((s32[4]{0:T(128)S(1)}, s32[4]{0:T(128)}, u32[]{:S(2)}) %copy-start.3) | copy-done | bytes 40
  32.1 2.5 %affinity.1 = (bf16[256,256]{1,0:T(8,128)(2,1)S(1)}, bf16[6,256,256]{2,1,0:T(8,128)(2,1)S(1)}) custom-call(s32[4,4]{1,0:T(4,128)S(1)} %copy-done.2, s32[4]{0:T(128)S(1)} %copy-done.3, s32[1,1024]{1,0:T(1,128)S(1)} %bitcast.2, s32[1,512]{1,0:T(1,128)S(1)} %bitcast.3, bf16[1024,256]{1,0:T(8,128)(2,1)S(1)} %copy-done, ...), custom_call_target="tpu_custom_call" | custom-call | tf_op jit(solution)/shard_map/affinity/pallas_call | solution.py:218
  34.5 1.5 %collective-permute-start.20 = (bf16[256,256]{1,0:T(8,128)(2,1)S(1)}, bf16[256,256]{1,0:T(8,128)(2,1)S(1)}, u32[]{:S(2)}, u32[]{:S(2)}) collective-permute-start(bf16[256,256]{1,0:T(8,128)(2,1)S(1)} %get-tuple-element.8.refs_0_), channel_id=1, source_target_pairs={{4,2},{5,3},{8,6},{9,7},{12,10},{13,11},{16,14},{17,15},{20,18},{2... | collective-permute-start | bytes 393224 | tf_op jit(solution)/shard_map/ppermute | solution.py:38
  36.1 4.9 %collective-permute-start.18 = (bf16[256,256]{1,0:T(8,128)(2,1)S(1)}, bf16[256,256]{1,0:T(8,128)(2,1)S(1)}, u32[]{:S(2)}, u32[]{:S(2)}) collective-permute-start(bf16[256,256]{1,0:T(8,128)(2,1)S(1)} %get-tuple-element.8.refs_0_), channel_id=1, source_target_pairs={{4,0},{5,1},{8,4},{9,5},{12,8},{13,9},{16,12},{17,13},{20,16},{21,... | collective-permute-start | bytes 393224 | tf_op jit(solution)/shard_map/ppermute | solution.py:38
  41.0 0.1 collective-permute-start.16
  41.1 1.0 %collective-permute-start.15 = (bf16[256,256]{1,0:T(8,128)(2,1)S(1)}, bf16[256,256]{1,0:T(8,128)(2,1)S(1)}, u32[]{:S(2)}, u32[]{:S(2)}) collective-permute-start(bf16[256,256]{1,0:T(8,128)(2,1)S(1)} %get-tuple-element.8.refs_0_), channel_id=1, source_target_pairs={{0,1},{1,0},{2,3},{3,2},{4,5},{5,4},{6,7},{7,6},{8,9},{9,8},{10,11... | collective-permute-start | bytes 393224 | tf_op jit(solution)/shard_map/ppermute | solution.py:24
  42.1 0.0 collective-permute-done.20.refs_6_
  42.1 0.1 collective-permute-start.21
  42.2 3.7 %collective-permute-done.18.refs_4_ = bf16[256,256]{1,0:T(8,128)(2,1)S(1)} collective-permute-done((bf16[256,256]{1,0:T(8,128)(2,1)S(1)}, bf16[256,256]{1,0:T(8,128)(2,1)S(1)}, u32[]{:S(2)}, u32[]{:S(2)}) %collective-permute-start.18) | collective-permute-done | bytes 131104 | tf_op jit(solution)/shard_map/ppermute | solution.py:38
  45.9 0.7 %collective-permute-start.19 = (bf16[256,256]{1,0:T(8,128)(2,1)S(1)}, bf16[256,256]{1,0:T(8,128)(2,1)S(1)}, u32[]{:S(2)}, u32[]{:S(2)}) collective-permute-start(bf16[256,256]{1,0:T(8,128)(2,1)S(1)} %collective-permute-done.18.refs_4_), channel_id=1, source_target_pairs={{0,1},{1,0},{2,3},{3,2},{4,5},{5,4},{6,7},{7,6},{8,9},{9,8},{10,11... | collective-permute-start | bytes 393224 | tf_op jit(solution)/shard_map/ppermute | solution.py:24
  46.6 0.0 collective-permute-done.16.refs_2_
  46.6 0.4 collective-permute-start.17
  47.0 0.0 collective-permute-done.15.refs_1_
  47.0 0.0 collective-permute-done.21.refs_7_
  47.0 0.6 %collective-permute-done.19.refs_5_ = bf16[256,256]{1,0:T(8,128)(2,1)S(1)} collective-permute-done((bf16[256,256]{1,0:T(8,128)(2,1)S(1)}, bf16[256,256]{1,0:T(8,128)(2,1)S(1)}, u32[]{:S(2)}, u32[]{:S(2)}) %collective-permute-start.19) | collective-permute-done | bytes 131104 | tf_op jit(solution)/shard_map/ppermute | solution.py:24
  47.6 0.4 collective-permute-done.17.refs_3_
  48.0 1.0 %spread.1 = bf16[256,256]{1,0:T(8,128)(2,1)} custom-call(bf16[6,256,256]{2,1,0:T(8,128)(2,1)S(1)} %get-tuple-element.7.aff_ref, bf16[256,256]{1,0:T(8,128)(2,1)S(1)} %broadcast_multiply_fusion.refs_10_.seed_ref, bf16[256,256]{1,0:T(8,128)(2,1)S(1)} %get-tuple-element.8.refs_0_, bf16[256,256]{1,0:T(8,128)(2,1)S(1)} %collective-permute-done.15.refs_1_, ...), custom_call_target="tpu_custom_call" | custom-call | tf_op jit(solution)/shard_map/spread/pallas_call | solution.py:243
  (1 shorter events, 0.0 us)
Async XLA Ops:
  1.7 4.5 %copy-start.4 = (bf16[256,256]{1,0:T(8,128)(2,1)S(1)}, bf16[256,256]{1,0:T(8,128)(2,1)}, u32[]{:S(2)}) copy-start(bf16[256,256]{1,0:T(8,128)(2,1)} %param.11) | copy-start | bytes 393220
  1.7 17.0 %copy-start = (bf16[1024,256]{1,0:T(8,128)(2,1)S(1)}, bf16[1024,256]{1,0:T(8,128)(2,1)}, u32[]{:S(2)}) copy-start(bf16[1024,256]{1,0:T(8,128)(2,1)} %refs_0_.1) | copy-start | bytes 1572868
  1.7 4.4 %collective-permute-start.11 = (bf16[256,256]{1,0:T(8,128)(2,1)S(1)}, bf16[256,256]{1,0:T(8,128)(2,1)S(1)}, u32[]{:S(2)}, u32[]{:S(2)}) collective-permute-start(bf16[256,256]{1,0:T(8,128)(2,1)S(1)} %broadcast_multiply_fusion.refs_10_.seed_ref), channel_id=1, source_target_pairs={{0,2},{1,3},{2,0},{3,1},{4,6},{5,7},{6,4},{7,5},{8,10},{9,11},{10,... | collective-permute-start | bytes 393224 | tf_op jit(solution)/shard_map/ppermute | solution.py:24
  3.0 11.9 %collective-permute-start.10 = (bf16[256,256]{1,0:T(8,128)(2,1)S(1)}, bf16[256,256]{1,0:T(8,128)(2,1)S(1)}, u32[]{:S(2)}, u32[]{:S(2)}) collective-permute-start(bf16[256,256]{1,0:T(8,128)(2,1)S(1)} %broadcast_multiply_fusion.refs_10_.seed_ref), channel_id=1, source_target_pairs={{0,1},{1,0},{2,3},{3,2},{4,5},{5,4},{6,7},{7,6},{8,9},{9,8},{10,11... | collective-permute-start | bytes 393224 | tf_op jit(solution)/shard_map/ppermute | solution.py:24
  5.0 13.7 %collective-permute-start.2 = (bf16[512,256]{1,0:T(8,128)(2,1)S(1)}, bf16[512,256]{1,0:T(8,128)(2,1)S(1)}, u32[]{:S(2)}, u32[]{:S(2)}) collective-permute-start(bf16[512,256]{1,0:T(8,128)(2,1)S(1)} %get-tuple-element.10), channel_id=1, source_target_pairs={{0,2},{1,3},{2,0},{3,1},{4,6},{5,7},{6,4},{7,5},{8,10},{9,11},{10,... | collective-permute-start | bytes 786440 | tf_op jit(solution)/shard_map/ppermute | solution.py:24
  5.3 3.1 %copy-start.1 = (s32[1024]{0:T(1024)S(1)}, s32[1024]{0:T(1024)}, u32[]{:S(2)}) copy-start(s32[1024]{0:T(1024)} %param.7) | copy-start | bytes 12292
  6.3 12.4 %collective-permute-start.13 = (bf16[256,256]{1,0:T(8,128)(2,1)S(1)}, bf16[256,256]{1,0:T(8,128)(2,1)S(1)}, u32[]{:S(2)}, u32[]{:S(2)}) collective-permute-start(bf16[256,256]{1,0:T(8,128)(2,1)S(1)} %broadcast_select_fusion), channel_id=1, source_target_pairs={{4,0},{8,4},{12,8},{16,12},{20,16},{24,20},{28,24},{5,1},{9,5},{13... | collective-permute-start | bytes 393224 | tf_op jit(solution)/shard_map/ppermute | solution.py:28
  8.4 5.5 %collective-permute-start = (s32[512]{0:T(512)S(1)}, s32[512]{0:T(512)S(1)}, u32[]{:S(2)}, u32[]{:S(2)}) collective-permute-start(s32[512]{0:T(512)S(1)} %slice.9), channel_id=1, source_target_pairs={{4,0},{8,4},{12,8},{16,12},{20,16},{24,20},{28,24},{5,1},{9,5},{13... | collective-permute-start | bytes 6152 | tf_op jit(solution)/shard_map/ppermute | solution.py:28
  11.5 11.6 %collective-permute-start.6 = (bf16[512,256]{1,0:T(8,128)(2,1)S(1)}, bf16[512,256]{1,0:T(8,128)(2,1)S(1)}, u32[]{:S(2)}, u32[]{:S(2)}) collective-permute-start(bf16[512,256]{1,0:T(8,128)(2,1)S(1)} %get-tuple-element.10), channel_id=1, source_target_pairs={{4,0},{8,4},{12,8},{16,12},{20,16},{24,20},{28,24},{5,1},{9,5},{13... | collective-permute-start | bytes 786440 | tf_op jit(solution)/shard_map/ppermute | solution.py:28
  14.0 17.4 %copy-start.2 = (s32[4,4]{1,0:T(4,128)S(1)}, s32[4,4]{1,0:T(4,128)}, u32[]{:S(2)}) copy-start(s32[4,4]{1,0:T(4,128)} %blocks_ref.1) | copy-start | bytes 196
  14.0 7.7 %collective-permute-start.3 = (bf16[512,256]{1,0:T(8,128)(2,1)S(1)}, bf16[512,256]{1,0:T(8,128)(2,1)S(1)}, u32[]{:S(2)}, u32[]{:S(2)}) collective-permute-start(bf16[512,256]{1,0:T(8,128)(2,1)S(1)} %get-tuple-element.9), channel_id=1, source_target_pairs={{0,2},{1,3},{2,0},{3,1},{4,6},{5,7},{6,4},{7,5},{8,10},{9,11},{10,... | collective-permute-start | bytes 786440 | tf_op jit(solution)/shard_map/ppermute | solution.py:24
  15.0 5.9 %collective-permute-start.12 = (bf16[256,256]{1,0:T(8,128)(2,1)S(1)}, bf16[256,256]{1,0:T(8,128)(2,1)S(1)}, u32[]{:S(2)}, u32[]{:S(2)}) collective-permute-start(bf16[256,256]{1,0:T(8,128)(2,1)S(1)} %collective-permute-done.11.refs_12_), channel_id=1, source_target_pairs={{0,1},{1,0},{2,3},{3,2},{4,5},{5,4},{6,7},{7,6},{8,9},{9,8},{10,11... | collective-permute-start | bytes 393224 | tf_op jit(solution)/shard_map/ppermute | solution.py:24
  18.7 11.6 %collective-permute-start.1 = (bf16[1024,256]{1,0:T(8,128)(2,1)S(1)}, bf16[1024,256]{1,0:T(8,128)(2,1)S(1)}, u32[]{:S(2)}, u32[]{:S(2)}) collective-permute-start(bf16[1024,256]{1,0:T(8,128)(2,1)S(1)} %copy-done), channel_id=1, source_target_pairs={{0,1},{1,0},{2,3},{3,2},{4,5},{5,4},{6,7},{7,6},{8,9},{9,8},{10,11... | collective-permute-start | bytes 1572872 | tf_op jit(solution)/shard_map/ppermute | solution.py:24
  18.7 10.2 %collective-permute-start.8 = (bf16[512,256]{1,0:T(8,128)(2,1)S(1)}, bf16[512,256]{1,0:T(8,128)(2,1)S(1)}, u32[]{:S(2)}, u32[]{:S(2)}) collective-permute-start(bf16[512,256]{1,0:T(8,128)(2,1)S(1)} %collective-permute-done.2.refs_2_), channel_id=1, source_target_pairs={{4,0},{8,4},{12,8},{16,12},{20,16},{24,20},{28,24},{5,1},{9,5},{13... | collective-permute-start | bytes 786440 | tf_op jit(solution)/shard_map/ppermute | solution.py:28
  20.9 2.2 %collective-permute-start.14 = (bf16[256,256]{1,0:T(8,128)(2,1)S(1)}, bf16[256,256]{1,0:T(8,128)(2,1)S(1)}, u32[]{:S(2)}, u32[]{:S(2)}) collective-permute-start(bf16[256,256]{1,0:T(8,128)(2,1)S(1)} %collective-permute-done.13.refs_14_), channel_id=1, source_target_pairs={{0,1},{1,0},{2,3},{3,2},{4,5},{5,4},{6,7},{7,6},{8,9},{9,8},{10,11... | collective-permute-start | bytes 393224 | tf_op jit(solution)/shard_map/ppermute | solution.py:24
  21.7 8.6 %collective-permute-start.5 = (bf16[512,256]{1,0:T(8,128)(2,1)S(1)}, bf16[512,256]{1,0:T(8,128)(2,1)S(1)}, u32[]{:S(2)}, u32[]{:S(2)}) collective-permute-start(bf16[512,256]{1,0:T(8,128)(2,1)S(1)} %collective-permute-done.3.refs_3_), channel_id=1, source_target_pairs={{0,1},{1,0},{2,3},{3,2},{4,5},{5,4},{6,7},{7,6},{8,9},{9,8},{10,11... | collective-permute-start | bytes 786440 | tf_op jit(solution)/shard_map/ppermute | solution.py:24
  23.0 7.2 %collective-permute-start.7 = (bf16[512,256]{1,0:T(8,128)(2,1)S(1)}, bf16[512,256]{1,0:T(8,128)(2,1)S(1)}, u32[]{:S(2)}, u32[]{:S(2)}) collective-permute-start(bf16[512,256]{1,0:T(8,128)(2,1)S(1)} %collective-permute-done.6.refs_6_), channel_id=1, source_target_pairs={{0,1},{1,0},{2,3},{3,2},{4,5},{5,4},{6,7},{7,6},{8,9},{9,8},{10,11... | collective-permute-start | bytes 786440 | tf_op jit(solution)/shard_map/ppermute | solution.py:24
  23.0 7.2 %collective-permute-start.4 = (bf16[512,256]{1,0:T(8,128)(2,1)S(1)}, bf16[512,256]{1,0:T(8,128)(2,1)S(1)}, u32[]{:S(2)}, u32[]{:S(2)}) collective-permute-start(bf16[512,256]{1,0:T(8,128)(2,1)S(1)} %collective-permute-done.2.refs_2_), channel_id=1, source_target_pairs={{0,1},{1,0},{2,3},{3,2},{4,5},{5,4},{6,7},{7,6},{8,9},{9,8},{10,11... | collective-permute-start | bytes 786440 | tf_op jit(solution)/shard_map/ppermute | solution.py:24
  29.0 2.4 %collective-permute-start.9 = (bf16[512,256]{1,0:T(8,128)(2,1)S(1)}, bf16[512,256]{1,0:T(8,128)(2,1)S(1)}, u32[]{:S(2)}, u32[]{:S(2)}) collective-permute-start(bf16[512,256]{1,0:T(8,128)(2,1)S(1)} %collective-permute-done.8.refs_8_), channel_id=1, source_target_pairs={{0,1},{1,0},{2,3},{3,2},{4,5},{5,4},{6,7},{7,6},{8,9},{9,8},{10,11... | collective-permute-start | bytes 786440 | tf_op jit(solution)/shard_map/ppermute | solution.py:24
  31.4 0.7 %copy-start.3 = (s32[4]{0:T(128)S(1)}, s32[4]{0:T(128)}, u32[]{:S(2)}) copy-start(s32[4]{0:T(128)} %counts_ref.1) | copy-start | bytes 52
  34.5 7.6 %collective-permute-start.20 = (bf16[256,256]{1,0:T(8,128)(2,1)S(1)}, bf16[256,256]{1,0:T(8,128)(2,1)S(1)}, u32[]{:S(2)}, u32[]{:S(2)}) collective-permute-start(bf16[256,256]{1,0:T(8,128)(2,1)S(1)} %get-tuple-element.8.refs_0_), channel_id=1, source_target_pairs={{4,2},{5,3},{8,6},{9,7},{12,10},{13,11},{16,14},{17,15},{20,18},{2... | collective-permute-start | bytes 393224 | tf_op jit(solution)/shard_map/ppermute | solution.py:38
  36.1 9.8 %collective-permute-start.18 = (bf16[256,256]{1,0:T(8,128)(2,1)S(1)}, bf16[256,256]{1,0:T(8,128)(2,1)S(1)}, u32[]{:S(2)}, u32[]{:S(2)}) collective-permute-start(bf16[256,256]{1,0:T(8,128)(2,1)S(1)} %get-tuple-element.8.refs_0_), channel_id=1, source_target_pairs={{4,0},{5,1},{8,4},{9,5},{12,8},{13,9},{16,12},{17,13},{20,16},{21,... | collective-permute-start | bytes 393224 | tf_op jit(solution)/shard_map/ppermute | solution.py:38
  41.0 5.6 %collective-permute-start.16 = (bf16[256,256]{1,0:T(8,128)(2,1)S(1)}, bf16[256,256]{1,0:T(8,128)(2,1)S(1)}, u32[]{:S(2)}, u32[]{:S(2)}) collective-permute-start(bf16[256,256]{1,0:T(8,128)(2,1)S(1)} %get-tuple-element.8.refs_0_), channel_id=1, source_target_pairs={{0,2},{1,3},{2,0},{3,1},{4,6},{5,7},{6,4},{7,5},{8,10},{9,11},{10,... | collective-permute-start | bytes 393224 | tf_op jit(solution)/shard_map/ppermute | solution.py:24
  41.1 5.9 %collective-permute-start.15 = (bf16[256,256]{1,0:T(8,128)(2,1)S(1)}, bf16[256,256]{1,0:T(8,128)(2,1)S(1)}, u32[]{:S(2)}, u32[]{:S(2)}) collective-permute-start(bf16[256,256]{1,0:T(8,128)(2,1)S(1)} %get-tuple-element.8.refs_0_), channel_id=1, source_target_pairs={{0,1},{1,0},{2,3},{3,2},{4,5},{5,4},{6,7},{7,6},{8,9},{9,8},{10,11... | collective-permute-start | bytes 393224 | tf_op jit(solution)/shard_map/ppermute | solution.py:24
  42.1 4.9 %collective-permute-start.21 = (bf16[256,256]{1,0:T(8,128)(2,1)S(1)}, bf16[256,256]{1,0:T(8,128)(2,1)S(1)}, u32[]{:S(2)}, u32[]{:S(2)}) collective-permute-start(bf16[256,256]{1,0:T(8,128)(2,1)S(1)} %collective-permute-done.20.refs_6_), channel_id=1, source_target_pairs={{0,1},{1,0},{2,3},{3,2},{4,5},{5,4},{6,7},{7,6},{8,9},{9,8},{10,11... | collective-permute-start | bytes 393224 | tf_op jit(solution)/shard_map/ppermute | solution.py:24
  45.9 1.7 %collective-permute-start.19 = (bf16[256,256]{1,0:T(8,128)(2,1)S(1)}, bf16[256,256]{1,0:T(8,128)(2,1)S(1)}, u32[]{:S(2)}, u32[]{:S(2)}) collective-permute-start(bf16[256,256]{1,0:T(8,128)(2,1)S(1)} %collective-permute-done.18.refs_4_), channel_id=1, source_target_pairs={{0,1},{1,0},{2,3},{3,2},{4,5},{5,4},{6,7},{7,6},{8,9},{9,8},{10,11... | collective-permute-start | bytes 393224 | tf_op jit(solution)/shard_map/ppermute | solution.py:24
  46.6 1.4 %collective-permute-start.17 = (bf16[256,256]{1,0:T(8,128)(2,1)S(1)}, bf16[256,256]{1,0:T(8,128)(2,1)S(1)}, u32[]{:S(2)}, u32[]{:S(2)}) collective-permute-start(bf16[256,256]{1,0:T(8,128)(2,1)S(1)} %collective-permute-done.16.refs_2_), channel_id=1, source_target_pairs={{0,1},{1,0},{2,3},{3,2},{4,5},{5,4},{6,7},{7,6},{8,9},{9,8},{10,11... | collective-permute-start | bytes 393224 | tf_op jit(solution)/shard_map/ppermute | solution.py:24

commit v2 on v0

v2 whole, which is shorter than its diff:
```python
import functools

import jax
import jax.numpy as jnp
from jax import lax
from jax.experimental import pallas as pl
from jax.experimental.pallas import tpu as pltpu
from jax.sharding import PartitionSpec as P

TILE = 256
K = 4
SPILL = 2
ROWS = 32

kernel_width = 0.06
spread_weight = 0.6
MASKED = -1e30
LOG2E = 1.4426950408889634

NT = (((1,), (1,)), ((), ()))


def across(block, distance):
    groups = lax.axis_size("grp")
    return lax.ppermute(block, "grp", [(i, i ^ distance) for i in range(groups)])


def from_next(block, distance=0):
    groups = lax.axis_size("grp")
    shards = lax.axis_size("shard")
    if distance == 0:
        return lax.ppermute(block, "shard", [(i + 1, i) for i in range(shards - 1)])
    route = [
        ((i + 1) * groups + (g ^ distance), i * groups + g)
        for i in range(shards - 1)
        for g in range(groups)
    ]
    return lax.ppermute(block, ("shard", "grp"), route)


def after(block, done):
    return lax.optimization_barrier((block, done))[0]


def listed(blocks_ref, counts_ref, tile, groups):
    base = lax.axis_index("shard") * groups
    count = counts_ref[tile]
    ids = [blocks_ref[tile, k] - base for k in range(K)]
    return [
        sum(jnp.where((ids[k] == w) & (k < count), 1, 0) for k in range(K))
        for w in range(groups + SPILL)
    ]


def code_kernel(
    groups, blocks_ref, counts_ref, clusters_ref, spill_ref, code_ref, factor_ref, row_ref
):
    core = lax.rem(lax.axis_index("grp"), 2)
    eye = lax.broadcasted_iota(jnp.int32, (TILE, TILE), 0) == lax.broadcasted_iota(
        jnp.int32, (TILE, TILE), 1
    )
    packed = spill_ref[SPILL * TILE:, :].astype(jnp.float32)
    width = packed.shape[1]
    spilled = [
        jnp.concatenate(
            [packed[i // width:i // width + 1, :] for i in range(t * TILE, (t + 1) * TILE, width)],
            axis=1,
        )
        for t in range(SPILL)
    ]
    for m in range(groups // 2):
        tile = 2 * m + core
        mult = listed(blocks_ref, counts_ref, tile, groups)
        for w in range(groups + SPILL):
            if w < groups:
                row = clusters_ref[:, w * TILE:(w + 1) * TILE].astype(jnp.float32)
            else:
                row = spilled[w - groups]
            factor = jnp.full((1, TILE), mult[w].astype(jnp.float32))
            here = (slice(m * 8, m * 8 + 8), slice(w * TILE, (w + 1) * TILE))
            code_ref[here] = jnp.broadcast_to(jnp.where(factor > 0, row, -1.0), (8, TILE))
            factor_ref[here] = jnp.broadcast_to(factor, (8, TILE))
        own = clusters_ref[:, pl.ds(pl.multiple_of(tile * TILE, TILE), TILE)].astype(jnp.float32)
        column = jnp.sum(jnp.where(eye, own, jnp.zeros_like(own)), axis=1, keepdims=True)
        row_ref[m * TILE:(m + 1) * TILE, :] = jnp.broadcast_to(column, (TILE, 128))


def spread(aff_ref, parts, seed):
    total = jnp.zeros(seed.shape, jnp.float32)
    for w, ref in parts:
        total += jnp.dot(aff_ref[w], ref[...], preferred_element_type=jnp.float32)
    return (spread_weight * total + (1.0 - spread_weight) * seed.astype(jnp.float32)).astype(
        jnp.bfloat16
    )


def affinity_kernel(groups, m, windows, code_ref, factor_ref, row_ref, *refs):
    quarters = groups
    half = groups // 2
    wtiles = groups + SPILL
    ins, (aff_ref, labels_ref, logit_ref) = refs[:-3], refs[-3:]
    member = lax.axis_index("grp")
    core = lax.rem(member, 2)
    pair = member // 2
    tile = 2 * m + core
    scale = LOG2E / kernel_width

    def piece(at):
        ref, row = at
        return ins[ref].at[row:row + TILE, :]

    def columns(w, q):
        return piece(windows["x"][q][w])[...]

    def squares(tiles):
        return functools.reduce(
            jnp.add,
            [
                jnp.square(t[:, h * 128:(h + 1) * 128].astype(jnp.float32))
                for t in tiles
                for h in range(t.shape[1] // 128)
            ],
        )

    rows = [
        jnp.where(core == 0, columns(2 * m, q), columns(2 * m + 1, q)) for q in range(quarters)
    ]
    row_n = jnp.sum(squares(rows), axis=1, keepdims=True) * scale
    row_c = row_ref[m * TILE:(m + 1) * TILE, 0:1]
    eye = lax.broadcasted_iota(jnp.int32, (TILE, TILE), 0) == lax.broadcasted_iota(
        jnp.int32, (TILE, TILE), 1
    )
    for w in range(wtiles):
        tiles = [columns(w, q) for q in range(quarters)]
        column_n = jnp.sum(squares(tiles).T, axis=0, keepdims=True) * scale
        dots = functools.reduce(
            jnp.add,
            [
                lax.dot_general(rows[q], tiles[q], NT, preferred_element_type=jnp.float32)
                for q in range(quarters)
            ],
        )
        allowed = row_c == code_ref[m * 8:m * 8 + 1, w * TILE:(w + 1) * TILE]
        if w // 2 == m:
            allowed = allowed & jnp.logical_not(eye & (tile == w))
        logit_ref[w] = jnp.where(allowed, dots * (2.0 * scale) - column_n - row_n, MASKED)

    def softmax(step, carry):
        at = pl.ds(pl.multiple_of(step * ROWS, ROWS), ROWS)
        logits = [logit_ref[w, at, :] for w in range(wtiles)]
        top = jnp.max(functools.reduce(jnp.maximum, logits), axis=1, keepdims=True)
        weights = [
            jnp.exp2(logits[w] - top) * factor_ref[m * 8:m * 8 + 1, w * TILE:(w + 1) * TILE]
            for w in range(wtiles)
        ]
        total = jnp.sum(functools.reduce(jnp.add, weights), axis=1, keepdims=True)
        share = 1.0 / total
        for w in range(wtiles):
            aff_ref[w, at, :] = (weights[w] * share).astype(jnp.bfloat16)
        return carry

    lax.fori_loop(0, TILE // ROWS, softmax, 0, unroll=True)

    parts = []
    for r in range(half):
        parts.append((2 * (pair ^ r) + core, piece(windows["mine"][r])))
        parts.append((2 * (pair ^ r) + 1 - core, piece(windows["other"][r])))
    parts.append((groups + core, piece(windows["mine"][half])))
    parts.append((groups + 1 - core, piece(windows["other"][half])))
    seed = piece(windows["mine"][0])[...]
    for r in range(1, half):
        seed = jnp.where((pair ^ m) == r, piece(windows["mine"][r])[...], seed)
    labels_ref[...] = spread(aff_ref, parts, seed)


def last_kernel(groups, seed_ref, *refs):
    half = groups // 2
    core = lax.rem(lax.axis_index("grp"), 2)
    affs, mine, other = refs[:half], refs[half:2 * half + 1], refs[2 * half + 1:3 * half + 2]
    parts = []
    for m in range(half + 1):
        parts += [(2 * m + core, mine[m]), (2 * m + 1 - core, other[m])]
    for m in range(half):
        @pl.when(lax.axis_index("grp") // 2 == m)
        def _(m=m):
            refs[-1][...] = spread(affs[m], parts, seed_ref[...])


def local(embeddings, clusters, blocks, counts, seed_mask, prior):
    groups = lax.axis_size("grp")
    half = groups // 2
    apart = range(1, half)
    pair = lax.axis_index("grp") // 2
    width = embeddings.shape[1]
    concepts = prior.shape[1]
    wtiles = groups + SPILL
    head_rows = SPILL * TILE

    seeds = jnp.where(seed_mask[:, None] > 0, prior, jnp.zeros_like(prior))
    first = embeddings[:TILE]
    rest = embeddings[TILE:]
    head_c = clusters[:head_rows].astype(jnp.bfloat16).reshape(-1, width)
    head_c = jnp.pad(head_c, ((0, 16 - head_c.shape[0]), (0, 0)))
    packed = width == concepts
    if packed:
        first_out = jnp.concatenate([first, seeds])
        first_far = [across(first_out, 2 * m) for m in apart]
        seeds_far = [f[TILE:] for f in first_far]
    else:
        first_far = [across(first, 2 * m) for m in apart]
        seeds_far = [across(seeds, 2 * m) for m in apart]
    rest_far = [across(rest, 2 * m) for m in apart]
    near = from_next(jnp.concatenate([embeddings[:head_rows], head_c]))
    head_seeds = seeds
    for m in apart:
        head_seeds = jnp.where(pair == m, seeds_far[m - 1], head_seeds)
    if packed:
        first_on = [jnp.concatenate([first_far[0][:TILE], head_seeds])]
        first_on += [f[:TILE] for f in first_far[1:]]
        near_first = [from_next(f) for f in first_on]
    else:
        near_first = [from_next(f) for f in first_far]
        near_seeds = from_next(head_seeds)
    second = embeddings[TILE:head_rows]
    near_second = [from_next(second, 2 * m) for m in apart]

    own_other = across(embeddings, 1)
    near_other = across(near, 1)
    near_second_other = [across(f, 1) for f in near_second]
    near_first_other = [across(f, 1) for f in near_first]
    first_far_other = [across(f, 1) for f in first_far]
    rest_far_other = [(across(f[:TILE], 1), across(f[TILE:], 1)) for f in rest_far]
    seeds_other = across(after(seeds, (near_other, near_second_other)), 1)

    arrays = []
    windows = {"x": [], "mine": [], "other": []}

    def place(*blocks):
        out = []
        for block, tiles in blocks:
            at = [i for i, a in enumerate(arrays) if a is block]
            if not at:
                arrays.append(block)
                at = [len(arrays) - 1]
            out += [(at[0], t * TILE) for t in tiles]
        return out

    own, more = range(groups), range(groups - 1)
    windows["x"].append(place((embeddings, own), (near, range(SPILL))))
    windows["x"].append(place((own_other, own), (near_other, range(SPILL))))
    for m in range(half - 1):
        windows["x"].append(
            place((first_far[m], [0]), (rest_far[m], more), (near_first[m], [0]), (near_second[m], [0]))
        )
        one, others = rest_far_other[m]
        windows["x"].append(
            place(
                (first_far_other[m], [0]), (one, [0]), (others, range(groups - 2)),
                (near_first_other[m], [0]), (near_second_other[m], [0]),
            )
        )
    windows["mine"] += place((seeds, [0]))
    windows["other"] += place((seeds_other, [0]))
    for m in range(half - 1):
        if packed:
            windows["mine"] += place((first_far[m], [1]))
            windows["other"] += place((first_far_other[m], [1]))
        else:
            windows["mine"] += place((seeds_far[m], [0]))
            windows["other"] += place((across(seeds_far[m], 1), [0]))
    if packed:
        windows["mine"] += place((near_first[0], [1]))
        windows["other"] += place((near_first_other[0], [1]))
    else:
        windows["mine"] += place((near_seeds, [0]))
        windows["other"] += place((across(near_seeds, 1), [0]))

    smem = pl.BlockSpec(memory_space=pltpu.SMEM)
    vmem = pl.BlockSpec(memory_space=pltpu.VMEM)
    params = pltpu.CompilerParams(vmem_limit_bytes=40 * 1024 * 1024)
    little = pl.CostEstimate(flops=1, bytes_accessed=1, transcendentals=0)
    labels_shape = jax.ShapeDtypeStruct((TILE, concepts), jnp.bfloat16)
    codes = pl.pallas_call(
        functools.partial(code_kernel, groups),
        out_shape=(
            jax.ShapeDtypeStruct((half * 8, wtiles * TILE), jnp.float32),
            jax.ShapeDtypeStruct((half * 8, wtiles * TILE), jnp.float32),
            jax.ShapeDtypeStruct((half * TILE, 128), jnp.float32),
        ),
        in_specs=[smem, smem, vmem, vmem],
        out_specs=(vmem, vmem, vmem),
        compiler_params=params,
        cost_estimate=little,
        name="codes",
    )(blocks, counts, clusters.reshape(1, -1), near)

    def affinity_of(m):
        return pl.pallas_call(
            functools.partial(affinity_kernel, groups, m, windows),
            out_shape=(jax.ShapeDtypeStruct((wtiles, TILE, TILE), jnp.bfloat16), labels_shape),
            in_specs=[vmem] * (3 + len(arrays)),
            out_specs=(vmem, vmem),
            scratch_shapes=[pltpu.VMEM((wtiles, TILE, TILE), jnp.float32)],
            compiler_params=params,
            cost_estimate=little,
            name=f"affinity_{m}",
        )(*codes, *arrays)

    affinity, labels = zip(*[affinity_of(m) for m in range(half)])
    labels = list(labels) + [from_next(labels[0])]
    others = [across(l, 1) for l in labels]
    return pl.pallas_call(
        functools.partial(last_kernel, groups),
        out_shape=labels_shape,
        in_specs=[vmem] * (1 + half + 2 * len(labels)),
        out_specs=vmem,
        compiler_params=params,
        name="spread_last",
    )(seeds, *affinity, *labels, *others)


def solution(mesh):
    in_specs = (
        P("shard", "grp"),
        P("shard"),
        P("shard", None),
        P("shard"),
        P(("shard", "grp")),
        P(("shard", "grp"), None),
    )
    out_specs = P(("shard", "grp"), None)
    return jax.shard_map(local, mesh=mesh, in_specs=in_specs, out_specs=out_specs, check_vma=False)
```

time: 110 us -> 40.1 us (0.36)
  waiting for transfers between devices: 41.9 us -> 12.1 us
  local copies, waits for them, and re-layouts: 17.8 us -> 1.2 us
  blocking collectives: 15.9 us -> 0 us
  between operations: 13.7 us -> 0.23 us
  starting transfers between devices: 9.74 us -> 18 us
  Pallas kernels: 0 us -> 7.3 us
  other arithmetic: 5.96 us -> 0.96 us
  matrix products: 3.84 us -> 0 us
    reduce_scatter x1 -> x0, waiting for transfers between devices: 22.6 us -> none  [local(): lax.psum_scatter(term.reshape(TILE * lax.axis_size('grp'), K * TILE), 'gr...]
    all_gather x2 -> x0, blocking collectives: 15.9 us -> none  [local(): shard_labels = lax.all_gather(labels, 'grp', axis=0, tiled=True)]
    ppermute x4 -> x17, starting transfers between devices: 9.74 us -> 18 us  [the longest x13 8.4 us: across(): lax.ppermute(block, 'grp', [(i, i ^ distance) for i in range(groups)])]
    pallas_call x0 -> x4, Pallas kernels: none -> 7.3 us  [the longest x2 5.51 us: affinity_of(): pl.pallas_call(functools.partial(affinity_kernel, groups, m, windows), ou...]
    ppermute x4 -> x17, waiting for transfers between devices: 19.2 us -> 12.1 us  [the longest x3 8.77 us: from_next(): return lax.ppermute(block, 'shard', [(i + 1, i) for i in range(shards - 1)])]
    unnamed x13 -> x10, local copies, waits for them, and re-layouts: 6.92 us -> 0.09 us
    sub x1 -> x0, local copies, waits for them, and re-layouts: 5.22 us -> none  [local(): term = rows_n[:, :, None, None] + cols_n[:, None, :, :] - 2.0 * dots]
    dot_general x3 -> x0, matrix products: 3.84 us -> none  [the longest x1 2.48 us: local(): jnp.einsum('rif,rkjf->rikj', rows_x, cols_x, preferred_element_type=jnp.f...]
  transfers between devices with their start and end apart: 5 -> 17, of which waited for: 4 -> 6; matrix products, arithmetic and copies ran while one was open for 5% -> 1% of each run, Pallas kernels for 0% -> 9%
where the time goes in v2:
time: 40.1 us; the launch traced here: 39.8 us
  starting transfers between devices  18 us (45%)
  waiting for transfers between devices  12.1 us (30%)
  Pallas kernels  7.3 us (18%)
  local copies, waits for them, and re-layouts  1.2 us (3%)
  other arithmetic  0.96 us (2%)
    ppermute x3, waiting for transfers between devices, from_next(): return lax.ppermute(block, 'shard', [(i + 1, i) for i in range(shards - 1)])  8.77 us
    ppermute x13, starting transfers between devices, across(): lax.ppermute(block, 'grp', [(i, i ^ distance) for i in range(groups)])  8.4 us
    ppermute x3, starting transfers between devices, from_next(): return lax.ppermute(block, 'shard', [(i + 1, i) for i in range(shards - 1)])  7.09 us
    pallas_call x2, Pallas kernels, affinity_of(): pl.pallas_call(functools.partial(affinity_kernel, groups, m, windows), ou...  5.51 us
    ppermute x13, waiting for transfers between devices, across(): lax.ppermute(block, 'grp', [(i, i ^ distance) for i in range(groups)])  3.32 us
    ppermute x1, starting transfers between devices, from_next(): return lax.ppermute(block, ('shard', 'grp'), route)  2.55 us
    pallas_call x1, Pallas kernels, local(): pl.pallas_call(functools.partial(last_kernel, groups), out_shape=labels_s...  1.03 us
    slice x1, local copies, waits for them, and re-layouts, local(): second = embeddings[TILE:head_rows]  1.02 us
  transfers between devices with their start and end apart: 17, of which 6 were waited for; matrix products, arithmetic and copies ran while one was open for 1% of the time, Pallas kernels for 9%

profile of v2, /device:TPU:11, one launch (start us, length us, event | category | flops | bytes accessed | tf_op | source)
XLA Modules:
  0.0 39.8 jit_solution(6987232998771946775)
XLA Ops:
  0.0 0.7 %broadcast_compare_fusion = pred[256]{0:T(512)(128)(4,1)S(1)} fusion(s32[256]{0:T(256)} %param.10), kind=kLoop, calls=%fused_computation.7 | loop fusion | flops 256 | bytes 1280 | tf_op jit(solution)/shard_map/gt | solution.py:199
  0.7 0.0 copy-start.4
  0.7 1.0 %fusion.2 = (bf16[256,256]{1,0:T(8,128)(2,1)S(1)}, bf16[256,256]{1,0:T(8,128)(2,1)S(1)}) fusion(bf16[1024,256]{1,0:T(8,128)(2,1)} %refs_0_.3), kind=kLoop, calls=%fused_computation.8 | loop fusion | bytes 524288 | tf_op jit(solution)/shard_map/slice | solution.py:224
  1.7 0.0 copy-done.4
  1.7 0.0 copy-start
  1.7 0.1 broadcast_select_fusion.refs_13_.seed_ref
  1.9 1.3 %collective-permute-start.3 = (bf16[512,256]{1,0:T(8,128)(2,1)S(1)}, bf16[512,256]{1,0:T(8,128)(2,1)S(1)}, u32[]{:S(2)}, u32[]{:S(2)}) collective-permute-start(bf16[512,256]{1,0:T(8,128)(2,1)S(1)} %pad_maximum_fusion), channel_id=1, source_target_pairs={{0,2},{1,3},{2,0},{3,1},{4,6},{5,7},{6,4},{7,5},{8,10},{9,11},{10,... | collective-permute-start | bytes 786440 | tf_op jit(solution)/shard_map/ppermute | solution.py:25
  3.2 0.0 copy-done
  3.2 1.0 %collective-permute-start.1 = (bf16[1024,256]{1,0:T(8,128)(2,1)S(1)}, bf16[1024,256]{1,0:T(8,128)(2,1)S(1)}, u32[]{:S(2)}, u32[]{:S(2)}) collective-permute-start(bf16[1024,256]{1,0:T(8,128)(2,1)S(1)} %copy-done), channel_id=1, source_target_pairs={{0,1},{1,0},{2,3},{3,2},{4,5},{5,4},{6,7},{7,6},{8,9},{9,8},{10,11... | collective-permute-start | bytes 1572872 | tf_op jit(solution)/shard_map/ppermute | solution.py:25
  4.1 0.0 copy-start.1
  4.1 2.5 %collective-permute-start.6 = (bf16[256,256]{1,0:T(8,128)(2,1)S(1)}, bf16[256,256]{1,0:T(8,128)(2,1)S(1)}, u32[]{:S(2)}, u32[]{:S(2)}) collective-permute-start(bf16[256,256]{1,0:T(8,128)(2,1)S(1)} %get-tuple-element.21), channel_id=1, source_target_pairs={{6,0},{7,1},{4,2},{5,3},{10,4},{11,5},{8,6},{9,7},{14,8},{15,9},{1... | collective-permute-start | bytes 393224 | tf_op jit(solution)/shard_map/ppermute | solution.py:38
  6.7 0.0 copy-done.1
  6.8 3.0 %collective-permute-start = (bf16[528,256]{1,0:T(8,128)(2,1)S(1)}, bf16[528,256]{1,0:T(8,128)(2,1)S(1)}, u32[]{:S(2)}, u32[]{:S(2)}) collective-permute-start(bf16[528,256]{1,0:T(8,128)(2,1)S(1)} %fusion.1), channel_id=1, source_target_pairs={{4,0},{8,4},{12,8},{16,12},{20,16},{24,20},{28,24},{5,1},{9,5},{13... | collective-permute-start | bytes 811016 | tf_op jit(solution)/shard_map/ppermute | solution.py:32
  9.8 1.0 %collective-permute-start.4 = (bf16[768,256]{1,0:T(8,128)(2,1)S(1)}, bf16[768,256]{1,0:T(8,128)(2,1)S(1)}, u32[]{:S(2)}, u32[]{:S(2)}) collective-permute-start(bf16[768,256]{1,0:T(8,128)(2,1)S(1)} %slice.39), channel_id=1, source_target_pairs={{0,2},{1,3},{2,0},{3,1},{4,6},{5,7},{6,4},{7,5},{8,10},{9,11},{10,... | collective-permute-start | bytes 1179656 | tf_op jit(solution)/shard_map/ppermute | solution.py:25
  10.8 0.0 collective-permute-done.3.refs_4_
  10.8 0.1 fusion.3
  11.0 2.2 %collective-permute-start.5 = (bf16[512,256]{1,0:T(8,128)(2,1)S(1)}, bf16[512,256]{1,0:T(8,128)(2,1)S(1)}, u32[]{:S(2)}, u32[]{:S(2)}) collective-permute-start(bf16[512,256]{1,0:T(8,128)(2,1)S(1)} %pad_maximum_fusion.1), channel_id=1, source_target_pairs={{4,0},{8,4},{12,8},{16,12},{20,16},{24,20},{28,24},{5,1},{9,5},{13... | collective-permute-start | bytes 786440 | tf_op jit(solution)/shard_map/ppermute | solution.py:32
  13.1 5.1 %collective-permute-done.spill_ref.refs_1_ = bf16[528,256]{1,0:T(8,128)(2,1)S(1)} collective-permute-done((bf16[528,256]{1,0:T(8,128)(2,1)S(1)}, bf16[528,256]{1,0:T(8,128)(2,1)S(1)}, u32[]{:S(2)}, u32[]{:S(2)}) %collective-permute-start) | collective-permute-done | bytes 270368 | tf_op jit(solution)/shard_map/ppermute | solution.py:32
  18.2 1.2 %collective-permute-start.2 = (bf16[528,256]{1,0:T(8,128)(2,1)S(1)}, bf16[528,256]{1,0:T(8,128)(2,1)S(1)}, u32[]{:S(2)}, u32[]{:S(2)}) collective-permute-start(bf16[528,256]{1,0:T(8,128)(2,1)S(1)} %collective-permute-done.spill_ref.refs_1_), channel_id=1, source_target_pairs={{0,1},{1,0},{2,3},{3,2},{4,5},{5,4},{6,7},{7,6},{8,9},{9,8},{10,11... | collective-permute-start | bytes 811016 | tf_op jit(solution)/shard_map/ppermute | solution.py:25
  19.4 0.0 collective-permute-done.6.refs_7_
  19.4 0.0 collective-permute-start.11
  19.5 2.1 %collective-permute-done.4.refs_5_ = bf16[768,256]{1,0:T(8,128)(2,1)S(1)} collective-permute-done((bf16[768,256]{1,0:T(8,128)(2,1)S(1)}, bf16[768,256]{1,0:T(8,128)(2,1)S(1)}, u32[]{:S(2)}, u32[]{:S(2)}) %collective-permute-start.4) | collective-permute-done | bytes 393248 | tf_op jit(solution)/shard_map/ppermute | solution.py:25
  21.6 0.7 %collective-permute-start.7 = (bf16[512,256]{1,0:T(8,128)(2,1)S(1)}, bf16[512,256]{1,0:T(8,128)(2,1)S(1)}, u32[]{:S(2)}, u32[]{:S(2)}) collective-permute-start(bf16[512,256]{1,0:T(8,128)(2,1)S(1)} %collective-permute-done.3.refs_4_), channel_id=1, source_target_pairs={{0,1},{1,0},{2,3},{3,2},{4,5},{5,4},{6,7},{7,6},{8,9},{9,8},{10,11... | collective-permute-start | bytes 786440 | tf_op jit(solution)/shard_map/ppermute | solution.py:25
  22.3 0.0 collective-permute-done.11.refs_12_
  22.3 0.1 collective-permute-start.9
  22.4 1.5 %collective-permute-done.5.refs_6_ = bf16[512,256]{1,0:T(8,128)(2,1)S(1)} collective-permute-done((bf16[512,256]{1,0:T(8,128)(2,1)S(1)}, bf16[512,256]{1,0:T(8,128)(2,1)S(1)}, u32[]{:S(2)}, u32[]{:S(2)}) %collective-permute-start.5) | collective-permute-done | bytes 262176 | tf_op jit(solution)/shard_map/ppermute | solution.py:32
  23.9 0.8 %collective-permute-start.10 = (bf16[512,256]{1,0:T(8,128)(2,1)S(1)}, bf16[512,256]{1,0:T(8,128)(2,1)S(1)}, u32[]{:S(2)}, u32[]{:S(2)}) collective-permute-start(bf16[512,256]{1,0:T(8,128)(2,1)S(1)} %collective-permute-done.5.refs_6_), channel_id=1, source_target_pairs={{0,1},{1,0},{2,3},{3,2},{4,5},{5,4},{6,7},{7,6},{8,9},{9,8},{10,11... | collective-permute-start | bytes 786440 | tf_op jit(solution)/shard_map/ppermute | solution.py:25
  24.7 0.0 copy-start.2
  24.7 0.0 copy-start.3
  24.7 0.0 collective-permute-done.2.refs_3_
  24.7 0.1 collective-permute-start.8
  24.8 0.0 collective-permute-done.7.refs_8_
  24.8 0.5 %collective-permute-start.12 = (bf16[256,256]{1,0:T(8,128)(2,1)S(1)}, bf16[256,256]{1,0:T(8,128)(2,1)S(1)}, u32[]{:S(2)}, u32[]{:S(2)}) collective-permute-start(bf16[256,256]{1,0:T(8,128)(2,1)S(1)} %broadcast_select_fusion.refs_13_.seed_ref), channel_id=1, source_target_pairs={{0,1},{1,0},{2,3},{3,2},{4,5},{5,4},{6,7},{7,6},{8,9},{9,8},{10,11... | collective-permute-start | bytes 393224 | tf_op jit(solution)/shard_map/ppermute | solution.py:25
  25.3 0.1 copy-done.2
  25.4 0.0 copy-done.3
  25.4 0.8 %codes.1 = (f32[16,1536]{1,0:T(8,128)S(1)}, f32[16,1536]{1,0:T(8,128)S(1)}, f32[512,128]{1,0:T(8,128)S(1)}) custom-call(s32[4,4]{1,0:T(4,128)S(1)} %copy-done.2, s32[4]{0:T(128)S(1)} %copy-done.3, s32[1,1024]{1,0:T(1,128)S(1)} %bitcast.1, bf16[528,256]{1,0:T(8,128)(2,1)S(1)} %collective-permute-done.spill_ref.refs_1_), custom_call_target="tpu_custom_call" | custom-call | flops 1 | bytes 1 | tf_op jit(solution)/shard_map/codes/pallas_call | solution.py:283
  26.1 0.0 collective-permute-done.8.refs_9_
  26.1 0.0 collective-permute-done.1.refs_2_
  26.1 0.0 collective-permute-done.9.refs_10_
  26.2 0.2 collective-permute-done.12.refs_14_
  26.3 0.0 collective-permute-done.10.refs_11_
  26.3 2.8 %affinity_0.1 = (bf16[6,256,256]{2,1,0:T(8,128)(2,1)S(1)}, bf16[256,256]{1,0:T(8,128)(2,1)S(1)}) custom-call(f32[16,1536]{1,0:T(8,128)S(1)} %get-tuple-element.13.code_ref, f32[16,1536]{1,0:T(8,128)S(1)} %get-tuple-element.14.factor_ref, f32[512,128]{1,0:T(8,128)S(1)} %get-tuple-element.15.row_ref, bf16[1024,256]{1,0:T(8,128)(2,1)S(1)} %copy-done, ...), custom_call_target="tpu_custom_call" | custom-call | flops 1 | bytes 1 | tf_op jit(solution)/shard_map/affinity_0/pallas_call | solution.py:298
  29.1 1.9 %collective-permute-start.13 = (bf16[256,256]{1,0:T(8,128)(2,1)S(1)}, bf16[256,256]{1,0:T(8,128)(2,1)S(1)}, u32[]{:S(2)}, u32[]{:S(2)}) collective-permute-start(bf16[256,256]{1,0:T(8,128)(2,1)S(1)} %get-tuple-element.19.refs_2_), channel_id=1, source_target_pairs={{4,0},{8,4},{12,8},{16,12},{20,16},{24,20},{28,24},{5,1},{9,5},{13... | collective-permute-start | bytes 393224 | tf_op jit(solution)/shard_map/ppermute | solution.py:32
  31.0 0.4 collective-permute-start.14
  31.4 2.7 %affinity_1.1 = (bf16[6,256,256]{2,1,0:T(8,128)(2,1)S(1)}, bf16[256,256]{1,0:T(8,128)(2,1)S(1)}) custom-call(f32[16,1536]{1,0:T(8,128)S(1)} %get-tuple-element.13.code_ref, f32[16,1536]{1,0:T(8,128)S(1)} %get-tuple-element.14.factor_ref, f32[512,128]{1,0:T(8,128)S(1)} %get-tuple-element.15.row_ref, bf16[1024,256]{1,0:T(8,128)(2,1)S(1)} %copy-done, ...), custom_call_target="tpu_custom_call" | custom-call | flops 1 | bytes 1 | tf_op jit(solution)/shard_map/affinity_1/pallas_call | solution.py:298
  34.2 0.2 collective-permute-start.15
  34.4 2.2 %collective-permute-done.13.refs_4_ = bf16[256,256]{1,0:T(8,128)(2,1)S(1)} collective-permute-done((bf16[256,256]{1,0:T(8,128)(2,1)S(1)}, bf16[256,256]{1,0:T(8,128)(2,1)S(1)}, u32[]{:S(2)}, u32[]{:S(2)}) %collective-permute-start.13) | collective-permute-done | bytes 131104 | tf_op jit(solution)/shard_map/ppermute | solution.py:32
  36.6 1.2 %collective-permute-start.16 = (bf16[256,256]{1,0:T(8,128)(2,1)S(1)}, bf16[256,256]{1,0:T(8,128)(2,1)S(1)}, u32[]{:S(2)}, u32[]{:S(2)}) collective-permute-start(bf16[256,256]{1,0:T(8,128)(2,1)S(1)} %collective-permute-done.13.refs_4_), channel_id=1, source_target_pairs={{0,1},{1,0},{2,3},{3,2},{4,5},{5,4},{6,7},{7,6},{8,9},{9,8},{10,11... | collective-permute-start | bytes 393224 | tf_op jit(solution)/shard_map/ppermute | solution.py:25
  37.8 0.0 collective-permute-done.15.refs_6_
  37.8 0.0 collective-permute-done.14.refs_5_
  37.8 1.0 %collective-permute-done.16.refs_7_ = bf16[256,256]{1,0:T(8,128)(2,1)S(1)} collective-permute-done((bf16[256,256]{1,0:T(8,128)(2,1)S(1)}, bf16[256,256]{1,0:T(8,128)(2,1)S(1)}, u32[]{:S(2)}, u32[]{:S(2)}) %collective-permute-start.16) | collective-permute-done | bytes 131104 | tf_op jit(solution)/shard_map/ppermute | solution.py:25
  38.8 1.0 %spread_last.1 = bf16[256,256]{1,0:T(8,128)(2,1)} custom-call(bf16[256,256]{1,0:T(8,128)(2,1)S(1)} %broadcast_select_fusion.refs_13_.seed_ref, bf16[6,256,256]{2,1,0:T(8,128)(2,1)S(1)} %get-tuple-element.17.refs_0_, bf16[6,256,256]{2,1,0:T(8,128)(2,1)S(1)} %get-tuple-element.18.refs_1_, bf16[256,256]{1,0:T(8,128)(2,1)S(1)} %get-tuple-element.19.refs_2_, ...), custom_call_target="tpu_custom_call" | custom-call | tf_op jit(solution)/shard_map/spread_last/pallas_call | solution.py:312
  (10 shorter events, 0.2 us)
Async XLA Ops:
  0.7 1.0 %copy-start.4 = (bf16[256,256]{1,0:T(8,128)(2,1)S(1)}, bf16[256,256]{1,0:T(8,128)(2,1)}, u32[]{:S(2)}) copy-start(bf16[256,256]{1,0:T(8,128)(2,1)} %param.11) | copy-start | bytes 393220
  1.7 1.5 %copy-start = (bf16[1024,256]{1,0:T(8,128)(2,1)S(1)}, bf16[1024,256]{1,0:T(8,128)(2,1)}, u32[]{:S(2)}) copy-start(bf16[1024,256]{1,0:T(8,128)(2,1)} %refs_0_.3) | copy-start | bytes 1572868
  1.9 9.0 %collective-permute-start.3 = (bf16[512,256]{1,0:T(8,128)(2,1)S(1)}, bf16[512,256]{1,0:T(8,128)(2,1)S(1)}, u32[]{:S(2)}, u32[]{:S(2)}) collective-permute-start(bf16[512,256]{1,0:T(8,128)(2,1)S(1)} %pad_maximum_fusion), channel_id=1, source_target_pairs={{0,2},{1,3},{2,0},{3,1},{4,6},{5,7},{6,4},{7,5},{8,10},{9,11},{10,... | collective-permute-start | bytes 786440 | tf_op jit(solution)/shard_map/ppermute | solution.py:25
  3.2 23.0 %collective-permute-start.1 = (bf16[1024,256]{1,0:T(8,128)(2,1)S(1)}, bf16[1024,256]{1,0:T(8,128)(2,1)S(1)}, u32[]{:S(2)}, u32[]{:S(2)}) collective-permute-start(bf16[1024,256]{1,0:T(8,128)(2,1)S(1)} %copy-done), channel_id=1, source_target_pairs={{0,1},{1,0},{2,3},{3,2},{4,5},{5,4},{6,7},{7,6},{8,9},{9,8},{10,11... | collective-permute-start | bytes 1572872 | tf_op jit(solution)/shard_map/ppermute | solution.py:25
  4.1 2.6 %copy-start.1 = (s32[1024]{0:T(1024)S(1)}, s32[1024]{0:T(1024)}, u32[]{:S(2)}) copy-start(s32[1024]{0:T(1024)} %param.7) | copy-start | bytes 12292
  4.1 15.3 %collective-permute-start.6 = (bf16[256,256]{1,0:T(8,128)(2,1)S(1)}, bf16[256,256]{1,0:T(8,128)(2,1)S(1)}, u32[]{:S(2)}, u32[]{:S(2)}) collective-permute-start(bf16[256,256]{1,0:T(8,128)(2,1)S(1)} %get-tuple-element.21), channel_id=1, source_target_pairs={{6,0},{7,1},{4,2},{5,3},{10,4},{11,5},{8,6},{9,7},{14,8},{15,9},{1... | collective-permute-start | bytes 393224 | tf_op jit(solution)/shard_map/ppermute | solution.py:38
  6.8 11.4 %collective-permute-start = (bf16[528,256]{1,0:T(8,128)(2,1)S(1)}, bf16[528,256]{1,0:T(8,128)(2,1)S(1)}, u32[]{:S(2)}, u32[]{:S(2)}) collective-permute-start(bf16[528,256]{1,0:T(8,128)(2,1)S(1)} %fusion.1), channel_id=1, source_target_pairs={{4,0},{8,4},{12,8},{16,12},{20,16},{24,20},{28,24},{5,1},{9,5},{13... | collective-permute-start | bytes 811016 | tf_op jit(solution)/shard_map/ppermute | solution.py:32
  9.8 11.8 %collective-permute-start.4 = (bf16[768,256]{1,0:T(8,128)(2,1)S(1)}, bf16[768,256]{1,0:T(8,128)(2,1)S(1)}, u32[]{:S(2)}, u32[]{:S(2)}) collective-permute-start(bf16[768,256]{1,0:T(8,128)(2,1)S(1)} %slice.39), channel_id=1, source_target_pairs={{0,2},{1,3},{2,0},{3,1},{4,6},{5,7},{6,4},{7,5},{8,10},{9,11},{10,... | collective-permute-start | bytes 1179656 | tf_op jit(solution)/shard_map/ppermute | solution.py:25
  11.0 12.9 %collective-permute-start.5 = (bf16[512,256]{1,0:T(8,128)(2,1)S(1)}, bf16[512,256]{1,0:T(8,128)(2,1)S(1)}, u32[]{:S(2)}, u32[]{:S(2)}) collective-permute-start(bf16[512,256]{1,0:T(8,128)(2,1)S(1)} %pad_maximum_fusion.1), channel_id=1, source_target_pairs={{4,0},{8,4},{12,8},{16,12},{20,16},{24,20},{28,24},{5,1},{9,5},{13... | collective-permute-start | bytes 786440 | tf_op jit(solution)/shard_map/ppermute | solution.py:32
  18.2 6.5 %collective-permute-start.2 = (bf16[528,256]{1,0:T(8,128)(2,1)S(1)}, bf16[528,256]{1,0:T(8,128)(2,1)S(1)}, u32[]{:S(2)}, u32[]{:S(2)}) collective-permute-start(bf16[528,256]{1,0:T(8,128)(2,1)S(1)} %collective-permute-done.spill_ref.refs_1_), channel_id=1, source_target_pairs={{0,1},{1,0},{2,3},{3,2},{4,5},{5,4},{6,7},{7,6},{8,9},{9,8},{10,11... | collective-permute-start | bytes 811016 | tf_op jit(solution)/shard_map/ppermute | solution.py:25
  19.4 2.9 %collective-permute-start.11 = (bf16[256,256]{1,0:T(8,128)(2,1)S(1)}, bf16[256,256]{1,0:T(8,128)(2,1)S(1)}, u32[]{:S(2)}, u32[]{:S(2)}) collective-permute-start(bf16[256,256]{1,0:T(8,128)(2,1)S(1)} %collective-permute-done.6.refs_7_), channel_id=1, source_target_pairs={{0,1},{1,0},{2,3},{3,2},{4,5},{5,4},{6,7},{7,6},{8,9},{9,8},{10,11... | collective-permute-start | bytes 393224 | tf_op jit(solution)/shard_map/ppermute | solution.py:25
  21.6 3.2 %collective-permute-start.7 = (bf16[512,256]{1,0:T(8,128)(2,1)S(1)}, bf16[512,256]{1,0:T(8,128)(2,1)S(1)}, u32[]{:S(2)}, u32[]{:S(2)}) collective-permute-start(bf16[512,256]{1,0:T(8,128)(2,1)S(1)} %collective-permute-done.3.refs_4_), channel_id=1, source_target_pairs={{0,1},{1,0},{2,3},{3,2},{4,5},{5,4},{6,7},{7,6},{8,9},{9,8},{10,11... | collective-permute-start | bytes 786440 | tf_op jit(solution)/shard_map/ppermute | solution.py:25
  22.3 3.8 %collective-permute-start.9 = (bf16[512,256]{1,0:T(8,128)(2,1)S(1)}, bf16[512,256]{1,0:T(8,128)(2,1)S(1)}, u32[]{:S(2)}, u32[]{:S(2)}) collective-permute-start(bf16[512,256]{1,0:T(8,128)(2,1)S(1)} %slice.48), channel_id=1, source_target_pairs={{0,1},{1,0},{2,3},{3,2},{4,5},{5,4},{6,7},{7,6},{8,9},{9,8},{10,11... | collective-permute-start | bytes 786440 | tf_op jit(solution)/shard_map/ppermute | solution.py:25
  23.9 2.5 %collective-permute-start.10 = (bf16[512,256]{1,0:T(8,128)(2,1)S(1)}, bf16[512,256]{1,0:T(8,128)(2,1)S(1)}, u32[]{:S(2)}, u32[]{:S(2)}) collective-permute-start(bf16[512,256]{1,0:T(8,128)(2,1)S(1)} %collective-permute-done.5.refs_6_), channel_id=1, source_target_pairs={{0,1},{1,0},{2,3},{3,2},{4,5},{5,4},{6,7},{7,6},{8,9},{9,8},{10,11... | collective-permute-start | bytes 786440 | tf_op jit(solution)/shard_map/ppermute | solution.py:25
  24.7 0.7 %copy-start.2 = (s32[4,4]{1,0:T(4,128)S(1)}, s32[4,4]{1,0:T(4,128)}, u32[]{:S(2)}) copy-start(s32[4,4]{1,0:T(4,128)} %blocks_ref.1) | copy-start | bytes 196
  24.7 0.7 %copy-start.3 = (s32[4]{0:T(128)S(1)}, s32[4]{0:T(128)}, u32[]{:S(2)}) copy-start(s32[4]{0:T(128)} %counts_ref.1) | copy-start | bytes 52
  24.7 1.4 %collective-permute-start.8 = (bf16[256,256]{1,0:T(8,128)(2,1)S(1)}, bf16[256,256]{1,0:T(8,128)(2,1)S(1)}, u32[]{:S(2)}, u32[]{:S(2)}) collective-permute-start(bf16[256,256]{1,0:T(8,128)(2,1)S(1)} %slice.47), channel_id=1, source_target_pairs={{0,1},{1,0},{2,3},{3,2},{4,5},{5,4},{6,7},{7,6},{8,9},{9,8},{10,11... | collective-permute-start | bytes 393224 | tf_op jit(solution)/shard_map/ppermute | solution.py:25
  24.8 1.5 %collective-permute-start.12 = (bf16[256,256]{1,0:T(8,128)(2,1)S(1)}, bf16[256,256]{1,0:T(8,128)(2,1)S(1)}, u32[]{:S(2)}, u32[]{:S(2)}) collective-permute-start(bf16[256,256]{1,0:T(8,128)(2,1)S(1)} %broadcast_select_fusion.refs_13_.seed_ref), channel_id=1, source_target_pairs={{0,1},{1,0},{2,3},{3,2},{4,5},{5,4},{6,7},{7,6},{8,9},{9,8},{10,11... | collective-permute-start | bytes 393224 | tf_op jit(solution)/shard_map/ppermute | solution.py:25
  29.1 7.6 %collective-permute-start.13 = (bf16[256,256]{1,0:T(8,128)(2,1)S(1)}, bf16[256,256]{1,0:T(8,128)(2,1)S(1)}, u32[]{:S(2)}, u32[]{:S(2)}) collective-permute-start(bf16[256,256]{1,0:T(8,128)(2,1)S(1)} %get-tuple-element.19.refs_2_), channel_id=1, source_target_pairs={{4,0},{8,4},{12,8},{16,12},{20,16},{24,20},{28,24},{5,1},{9,5},{13... | collective-permute-start | bytes 393224 | tf_op jit(solution)/shard_map/ppermute | solution.py:32
  31.0 6.8 %collective-permute-start.14 = (bf16[256,256]{1,0:T(8,128)(2,1)S(1)}, bf16[256,256]{1,0:T(8,128)(2,1)S(1)}, u32[]{:S(2)}, u32[]{:S(2)}) collective-permute-start(bf16[256,256]{1,0:T(8,128)(2,1)S(1)} %get-tuple-element.19.refs_2_), channel_id=1, source_target_pairs={{0,1},{1,0},{2,3},{3,2},{4,5},{5,4},{6,7},{7,6},{8,9},{9,8},{10,11... | collective-permute-start | bytes 393224 | tf_op jit(solution)/shard_map/ppermute | solution.py:25
  34.2 3.6 %collective-permute-start.15 = (bf16[256,256]{1,0:T(8,128)(2,1)S(1)}, bf16[256,256]{1,0:T(8,128)(2,1)S(1)}, u32[]{:S(2)}, u32[]{:S(2)}) collective-permute-start(bf16[256,256]{1,0:T(8,128)(2,1)S(1)} %get-tuple-element.20.refs_3_), channel_id=1, source_target_pairs={{0,1},{1,0},{2,3},{3,2},{4,5},{5,4},{6,7},{7,6},{8,9},{9,8},{10,11... | collective-permute-start | bytes 393224 | tf_op jit(solution)/shard_map/ppermute | solution.py:25
  36.6 2.1 %collective-permute-start.16 = (bf16[256,256]{1,0:T(8,128)(2,1)S(1)}, bf16[256,256]{1,0:T(8,128)(2,1)S(1)}, u32[]{:S(2)}, u32[]{:S(2)}) collective-permute-start(bf16[256,256]{1,0:T(8,128)(2,1)S(1)} %collective-permute-done.13.refs_4_), channel_id=1, source_target_pairs={{0,1},{1,0},{2,3},{3,2},{4,5},{5,4},{6,7},{7,6},{8,9},{9,8},{10,11... | collective-permute-start | bytes 393224 | tf_op jit(solution)/shard_map/ppermute | solution.py:25

commit v3 on v2

v3 whole, which is shorter than its diff:
```python
import functools

import jax
import jax.numpy as jnp
from jax import lax
from jax.experimental import pallas as pl
from jax.experimental.pallas import tpu as pltpu
from jax.sharding import PartitionSpec as P

TILE = 256
K = 4
SPILL = 2
ROWS = 32

kernel_width = 0.06
spread_weight = 0.6
MASKED = -1e30
SCALE = 1.4426950408889634 / kernel_width

NT = (((1,), (1,)), ((), ()))


def across(block, distance):
    groups = lax.axis_size("grp")
    return lax.ppermute(block, "grp", [(i, i ^ distance) for i in range(groups)])


def from_next(block):
    shards = lax.axis_size("shard")
    return lax.ppermute(block, "shard", [(i + 1, i) for i in range(shards - 1)])


def bundle(*blocks):
    if len({b.shape[1] for b in blocks}) == 1:
        return (jnp.concatenate(blocks),)
    return blocks


def tile_in(blocks, t):
    return blocks[0][t * TILE:(t + 1) * TILE] if len(blocks) == 1 else blocks[t]


def masked(mask, labels):
    return jnp.where(mask[:, None] > 0, labels, jnp.zeros_like(labels))


def after(block, done):
    return lax.optimization_barrier((block, done))[0]


def listed(blocks_ref, counts_ref, tile, groups):
    base = lax.axis_index("shard") * groups
    count = counts_ref[tile]
    ids = [blocks_ref[tile, k] - base for k in range(K)]
    return [
        sum(jnp.where((ids[k] == w) & (k < count), 1, 0) for k in range(K))
        for w in range(groups + SPILL)
    ]


def squares(tiles):
    return functools.reduce(
        jnp.add,
        [
            jnp.square(t[:, h * 128:(h + 1) * 128].astype(jnp.float32))
            for t in tiles
            for h in range(t.shape[1] // 128)
        ],
    )


def row_norms(tiles):
    return jnp.sum(squares(tiles), axis=1, keepdims=True) * SCALE


def column_terms(rows, tiles):
    dots = functools.reduce(
        jnp.add,
        [
            lax.dot_general(r, t, NT, preferred_element_type=jnp.float32)
            for r, t in zip(rows, tiles)
        ],
    )
    return dots * (2.0 * SCALE) - jnp.sum(squares(tiles).T, axis=0, keepdims=True) * SCALE


def early_kernel(
    groups, m, blocks_ref, counts_ref, clusters_ref, own_ref, other_ref, part_ref, factor_ref,
    row_ref,
):
    core = lax.rem(lax.axis_index("grp"), 2)
    eye = lax.broadcasted_iota(jnp.int32, (TILE, TILE), 0) == lax.broadcasted_iota(
        jnp.int32, (TILE, TILE), 1
    )
    tile = 2 * m + core
    at = pl.ds(pl.multiple_of(tile * TILE, TILE), TILE)
    rows = [own_ref[at, :], other_ref[at, :]]
    norms = row_norms(rows)
    own = clusters_ref[:, at].astype(jnp.float32)
    own = jnp.sum(jnp.where(eye, own, jnp.zeros_like(own)), axis=1, keepdims=True)
    row_ref[:, :128] = jnp.broadcast_to(own, (TILE, 128))
    row_ref[:, 128:] = jnp.broadcast_to(norms, (TILE, 128))
    for w, mult in enumerate(listed(blocks_ref, counts_ref, tile, groups)):
        columns = slice(w * TILE, (w + 1) * TILE)
        factor = jnp.full((1, TILE), mult.astype(jnp.float32))
        factor_ref[:, columns] = jnp.broadcast_to(factor, (8, TILE))
        if w < groups:
            cluster = clusters_ref[:, columns].astype(jnp.float32)
            allowed = own == jnp.where(factor > 0, cluster, -1.0)
            if w // 2 == m:
                allowed = allowed & jnp.logical_not(eye & (tile == w))
            terms = column_terms(rows, [own_ref[columns, :], other_ref[columns, :]])
            part_ref[w] = jnp.where(allowed, terms - norms, MASKED)


def rows_of(columns, m, quarters):
    core = lax.rem(lax.axis_index("grp"), 2)
    return [jnp.where(core == 0, columns(2 * m, q), columns(2 * m + 1, q)) for q in quarters]


def logit_kernel(
    groups, m, windows, part_ref, factor_ref, row_ref, own_ref, other_ref, near_ref,
    near_other_ref, *refs,
):
    ins, logit_ref = refs[:-1], refs[-1]
    quarters = range(2, groups)
    core = lax.rem(lax.axis_index("grp"), 2)

    def columns(w, q):
        ref, row = windows[q][w]
        return ins[ref][row:row + TILE, :]

    rows = rows_of(columns, m, quarters)
    norms = row_norms(rows)
    for w in range(groups):
        logit_ref[w] = (
            part_ref[w] - norms + column_terms(rows, [columns(w, q) for q in quarters])
        )
    at = pl.ds(pl.multiple_of((2 * m + core) * TILE, TILE), TILE)
    rows = [own_ref[at, :], other_ref[at, :]] + rows
    norms = norms + row_ref[:, 128:129]
    packed = near_ref[SPILL * TILE:, :].astype(jnp.float32)
    width = packed.shape[1]
    for t in range(SPILL):
        w = groups + t
        cluster = jnp.concatenate(
            [packed[i // width:i // width + 1, :] for i in range(t * TILE, (t + 1) * TILE, width)],
            axis=1,
        )
        factor = factor_ref[0:1, w * TILE:(w + 1) * TILE]
        allowed = row_ref[:, 0:1] == jnp.where(factor > 0, cluster, -1.0)
        tiles = [ref[t * TILE:(t + 1) * TILE, :] for ref in (near_ref, near_other_ref)]
        if t:
            tiles += [columns(w, q) for q in quarters]
        logit_ref[w] = jnp.where(allowed, column_terms(rows, tiles) - norms, MASKED)


def spread(aff_ref, parts, seed):
    total = jnp.zeros(seed.shape, jnp.float32)
    for w, ref in parts:
        total += jnp.dot(aff_ref[w], ref[...], preferred_element_type=jnp.float32)
    return (spread_weight * total + (1.0 - spread_weight) * seed.astype(jnp.float32)).astype(
        jnp.bfloat16
    )


def affinity_kernel(groups, m, windows, logit_ref, factor_ref, *refs):
    half = groups // 2
    wtiles = groups + SPILL
    ins, (aff_ref, labels_ref, late_ref) = refs[:-3], refs[-3:]
    member = lax.axis_index("grp")
    core = lax.rem(member, 2)
    pair = member // 2
    quarters = range(2, groups)

    def piece(at):
        ref, row = at
        return ins[ref].at[row:row + TILE, :]

    def columns(w, q):
        return piece(windows["x"][q][w])[...]

    late_ref[...] = logit_ref[groups] + column_terms(
        rows_of(columns, m, quarters), [columns(groups, q) for q in quarters]
    )

    def softmax(step, carry):
        at = pl.ds(pl.multiple_of(step * ROWS, ROWS), ROWS)
        logits = [logit_ref[w, at, :] for w in range(wtiles)]
        logits[groups] = late_ref[at, :]
        top = jnp.max(functools.reduce(jnp.maximum, logits), axis=1, keepdims=True)
        weights = [
            jnp.exp2(logits[w] - top) * factor_ref[0:1, w * TILE:(w + 1) * TILE]
            for w in range(wtiles)
        ]
        total = jnp.sum(functools.reduce(jnp.add, weights), axis=1, keepdims=True)
        share = 1.0 / total
        for w in range(wtiles):
            aff_ref[w, at, :] = (weights[w] * share).astype(jnp.bfloat16)
        return carry

    lax.fori_loop(0, TILE // ROWS, softmax, 0, unroll=True)

    parts = []
    for r in range(half):
        parts.append((2 * (pair ^ r) + core, piece(windows["mine"][r])))
        parts.append((2 * (pair ^ r) + 1 - core, piece(windows["other"][r])))
    parts.append((groups + core, piece(windows["mine"][half])))
    parts.append((groups + 1 - core, piece(windows["other"][half])))
    seed = piece(windows["mine"][0])[...]
    for r in range(1, half):
        seed = jnp.where((pair ^ m) == r, piece(windows["mine"][r])[...], seed)
    labels_ref[...] = spread(aff_ref, parts, seed)


def own_kernel(groups, seed_ref, *refs):
    half = groups // 2
    core = lax.rem(lax.axis_index("grp"), 2)
    affs, mine, other, out_ref = refs[:half], refs[half:2 * half], refs[2 * half:3 * half], refs[-1]
    for p in range(half):
        @pl.when(lax.axis_index("grp") // 2 == p)
        def _(p=p):
            total = jnp.zeros(out_ref.shape, jnp.float32)
            for m in range(half):
                for w, ref in ((2 * m + core, mine[m]), (2 * m + 1 - core, other[m])):
                    total += jnp.dot(affs[p][w], ref[...], preferred_element_type=jnp.float32)
            out_ref[...] = spread_weight * total + (1.0 - spread_weight) * seed_ref[...].astype(
                jnp.float32
            )


def near_kernel(groups, distance, total_ref, labels_ref, *refs):
    affs, out_ref = refs[:-1], refs[-1]
    core = lax.rem(lax.axis_index("grp"), 2)
    for p in range(groups // 2):
        @pl.when(lax.axis_index("grp") // 2 == p)
        def _(p=p):
            out_ref[...] = (
                total_ref[...]
                + spread_weight
                * jnp.dot(
                    affs[p][groups + (core ^ distance)], labels_ref[...],
                    preferred_element_type=jnp.float32,
                )
            ).astype(out_ref.dtype)


def local(embeddings, clusters, blocks, counts, seed_mask, prior):
    groups = lax.axis_size("grp")
    half = groups // 2
    apart = range(1, half)
    pair = lax.axis_index("grp") // 2
    width = embeddings.shape[1]
    concepts = prior.shape[1]
    wtiles = groups + SPILL
    head_rows = SPILL * TILE
    smem = pl.BlockSpec(memory_space=pltpu.SMEM)
    vmem = pl.BlockSpec(memory_space=pltpu.VMEM)
    params = pltpu.CompilerParams(vmem_limit_bytes=40 * 1024 * 1024)
    little = pl.CostEstimate(flops=1, bytes_accessed=1, transcendentals=0)
    labels_shape = jax.ShapeDtypeStruct((TILE, concepts), jnp.bfloat16)

    first_far = [
        tuple(across(b, 2 * m) for b in bundle(embeddings[:TILE], prior)) for m in apart
    ]
    mask_far = [across(seed_mask, 2 * m) for m in apart]
    rest_far = [across(embeddings[TILE:], 2 * m) for m in apart]

    head_c = clusters[:head_rows].astype(jnp.bfloat16).reshape(-1, width)
    head_c = jnp.pad(head_c, ((0, 16 - head_c.shape[0]), (0, 0)))
    near = from_next(jnp.concatenate([embeddings[:head_rows], head_c]))

    own_other = across(embeddings, 1)
    near_other = across(near, 1)

    def early_of(m, done=()):
        own, other = after((embeddings, own_other), done) if m else (embeddings, own_other)
        return pl.pallas_call(
            functools.partial(early_kernel, groups, m),
            out_shape=(
                jax.ShapeDtypeStruct((groups, TILE, TILE), jnp.float32),
                jax.ShapeDtypeStruct((8, wtiles * TILE), jnp.float32),
                jax.ShapeDtypeStruct((TILE, 256), jnp.float32),
            ),
            in_specs=[smem, smem] + [vmem] * 3,
            out_specs=(vmem, vmem, vmem),
            compiler_params=params,
            cost_estimate=little,
            name=f"early_{m}",
        )(blocks, counts, clusters.reshape(1, -1), own, other)

    first_early = early_of(0)

    seeds = masked(seed_mask, prior)
    seeds_far = [masked(k, tile_in(f, 1)) for k, f in zip(mask_far, first_far)]
    head_seeds = seeds
    for m in apart:
        head_seeds = jnp.where(pair == m, seeds_far[m - 1], head_seeds)
    first_on = [bundle(tile_in(first_far[0], 0), head_seeds)]
    first_on += [(tile_in(f, 0),) for f in first_far[1:]]
    first_on = after(first_on, first_early)
    near_first = [tuple(from_next(b) for b in f) for f in first_on]

    near_second = [across(near[TILE:head_rows], 2 * m) for m in apart]

    near_second_other = [across(f, 1) for f in near_second]
    near_first_other = [tuple(across(b, 1) for b in f) for f in near_first]
    first_far_other = [across(tile_in(f, 0), 1) for f in first_far]
    rest_far_other = [(across(f[:TILE], 1), across(f[TILE:], 1)) for f in rest_far]
    seeds_other = across(seeds, 1)
    seeds_far_other = [across(f, 1) for f in seeds_far]

    arrays = []

    def place(*blocks):
        out = []
        for block, tiles in blocks:
            at = [i for i, a in enumerate(arrays) if a is block]
            if not at:
                arrays.append(block)
                at = [len(arrays) - 1]
            out += [(at[0], t * TILE) for t in tiles]
        return out

    def seeds_in(f):
        return (f[0], [1]) if len(f) == 1 else (f[1], [0])

    windows = {"x": [None, None], "mine": place((seeds, [0])), "other": place((seeds_other, [0]))}
    for m in range(half - 1):
        windows["x"].append(
            place(
                (first_far[m][0], [0]), (rest_far[m], range(groups - 1)),
                (near_first[m][0], [0]), (near_second[m], [0]),
            )
        )
        one, more = rest_far_other[m]
        windows["x"].append(
            place(
                (first_far_other[m], [0]), (one, [0]), (more, range(groups - 2)),
                (near_first_other[m][0], [0]), (near_second_other[m], [0]),
            )
        )
        windows["mine"] += place((seeds_far[m], [0]))
        windows["other"] += place((seeds_far_other[m], [0]))
    windows["mine"] += place(seeds_in(near_first[0]))
    windows["other"] += place(seeds_in(near_first_other[0]))

    early_arrays = []
    early_windows = [None, None]
    for q in range(2, groups):
        tiles = []
        for w, (ref, row) in enumerate(windows["x"][q]):
            if w == groups:
                tiles.append(None)
                continue
            at = [i for i, a in enumerate(early_arrays) if a is arrays[ref]]
            if not at:
                early_arrays.append(arrays[ref])
                at = [len(early_arrays) - 1]
            tiles.append((at[0], row))
        early_windows.append(tiles)

    def affinity_of(m, done):
        early = early_of(m, done) if m else first_early
        logits = pl.pallas_call(
            functools.partial(logit_kernel, groups, m, early_windows),
            out_shape=jax.ShapeDtypeStruct((wtiles, TILE, TILE), jnp.float32),
            in_specs=[vmem] * (7 + len(early_arrays)),
            out_specs=vmem,
            compiler_params=params,
            cost_estimate=little,
            name=f"logits_{m}",
        )(*early, embeddings, own_other, near, near_other, *early_arrays)
        return pl.pallas_call(
            functools.partial(affinity_kernel, groups, m, windows),
            out_shape=(jax.ShapeDtypeStruct((wtiles, TILE, TILE), jnp.bfloat16), labels_shape),
            in_specs=[vmem] * (2 + len(arrays)),
            out_specs=(vmem, vmem),
            scratch_shapes=[pltpu.VMEM((TILE, TILE), jnp.float32)],
            compiler_params=params,
            cost_estimate=little,
            name=f"affinity_{m}",
        )(logits, early[1], *arrays)

    affinity, labels = [], []
    for m in range(half):
        a, l = affinity_of(m, labels[-1:])
        affinity.append(a)
        labels.append(l)
    near_labels = from_next(labels[0])
    near_labels_other = across(near_labels, 1)
    others = [across(l, 1) for l in labels]
    total = pl.pallas_call(
        functools.partial(own_kernel, groups),
        out_shape=jax.ShapeDtypeStruct((TILE, concepts), jnp.float32),
        in_specs=[vmem] * (1 + 3 * half),
        out_specs=vmem,
        compiler_params=params,
        cost_estimate=little,
        name="spread_own",
    )(seeds, *affinity, *labels, *others)
    for distance, block in enumerate((near_labels, near_labels_other)):
        total = pl.pallas_call(
            functools.partial(near_kernel, groups, distance),
            out_shape=jax.ShapeDtypeStruct((TILE, concepts), jnp.bfloat16 if distance else jnp.float32),
            in_specs=[vmem] * (2 + half),
            out_specs=vmem,
            compiler_params=params,
            cost_estimate=little,
            name=f"spread_near_{distance}",
        )(total, block, *affinity)
    return total


def solution(mesh):
    in_specs = (
        P("shard", "grp"),
        P("shard"),
        P("shard", None),
        P("shard"),
        P(("shard", "grp")),
        P(("shard", "grp"), None),
    )
    out_specs = P(("shard", "grp"), None)
    return jax.shard_map(local, mesh=mesh, in_specs=in_specs, out_specs=out_specs, check_vma=False)
```

time: 40.1 us -> 37.1 us (0.925)
  waiting for transfers between devices: 12.1 us -> 3.51 us
  starting transfers between devices: 18 us -> 21.2 us
  other arithmetic: 0.96 us -> 1.81 us
  local copies, waits for them, and re-layouts: 1.2 us -> 2 us
  Pallas kernels: 7.3 us -> 8 us
    ppermute x3, waiting for transfers between devices: 8.77 us -> 1.46 us  [from_next(): return lax.ppermute(block, 'shard', [(i + 1, i) for i in range(shards - 1)])]
    ppermute x13 -> x16, starting transfers between devices: 8.4 us -> 14.1 us  [across(): lax.ppermute(block, 'grp', [(i, i ^ distance) for i in range(groups)])]
    pallas_call x2 -> x7, Pallas kernels: 1.79 us -> 5.86 us  [the longest x2 2.36 us: early_of(): pl.pallas_call(functools.partial(early_kernel, groups, m), out_shape=(jax...]
    pallas_call x2, Pallas kernels: 5.51 us -> 2.14 us  [affinity_of(): pl.pallas_call(functools.partial(affinity_kernel, groups, m, windows), ou...]
    ppermute x1 -> x0, starting transfers between devices: 2.55 us -> none  [from_next(): return lax.ppermute(block, ('shard', 'grp'), route)]
    ppermute x13 -> x16, waiting for transfers between devices: 3.32 us -> 2.05 us  [across(): lax.ppermute(block, 'grp', [(i, i ^ distance) for i in range(groups)])]
    slice x1, local copies, waits for them, and re-layouts: 0.02 us -> 0.97 us  [local(): near = from_next(jnp.concatenate([embeddings[:head_rows], head_c]))]
    concatenate x2, other arithmetic: 0.04 us -> 0.94 us  [bundle(): return (jnp.concatenate(blocks),)]
  transfers between devices with their start and end apart: 17 -> 19, of which waited for: 6 -> 6; matrix products, arithmetic and copies ran while one was open for 1% -> 10% of each run, Pallas kernels for 9% -> 17%
where the time goes in v3:
time: 37.1 us; the launch traced here: 36.8 us
  starting transfers between devices  21.2 us (57%)
  Pallas kernels  8 us (22%)
  waiting for transfers between devices  3.51 us (9%)
  local copies, waits for them, and re-layouts  2 us (5%)
  other arithmetic  1.81 us (5%)
    ppermute x16, starting transfers between devices, across(): lax.ppermute(block, 'grp', [(i, i ^ distance) for i in range(groups)])  14.1 us
    ppermute x3, starting transfers between devices, from_next(): return lax.ppermute(block, 'shard', [(i + 1, i) for i in range(shards - 1)])  7.13 us
    pallas_call x2, Pallas kernels, early_of(): pl.pallas_call(functools.partial(early_kernel, groups, m), out_shape=(jax...  2.36 us
    pallas_call x2, Pallas kernels, affinity_of(): pl.pallas_call(functools.partial(affinity_kernel, groups, m, windows), ou...  2.14 us
    pallas_call x2, Pallas kernels, affinity_of(): pl.pallas_call(functools.partial(logit_kernel, groups, m, early_windows),...  2.14 us
    ppermute x16, waiting for transfers between devices, across(): lax.ppermute(block, 'grp', [(i, i ^ distance) for i in range(groups)])  2.05 us
    ppermute x3, waiting for transfers between devices, from_next(): return lax.ppermute(block, 'shard', [(i + 1, i) for i in range(shards - 1)])  1.46 us
    pallas_call x2, Pallas kernels, local(): pl.pallas_call(functools.partial(near_kernel, groups, distance), out_shap...  1.06 us
  transfers between devices with their start and end apart: 19, of which 6 were waited for; matrix products, arithmetic and copies ran while one was open for 10% of the time, Pallas kernels for 17%

profile of v3, /device:TPU:11, one launch (start us, length us, event | category | flops | bytes accessed | tf_op | source)
XLA Modules:
  0.0 36.8 jit_solution(3714399794757261447)
XLA Ops:
  0.0 0.0 copy-start
  0.0 0.0 copy-start.4
  0.0 0.0 copy-start.5
  0.0 0.7 %collective-permute-start = (bf16[1024,256]{1,0:T(8,128)(2,1)}, bf16[1024,256]{1,0:T(8,128)(2,1)S(1)}, u32[]{:S(2)}, u32[]{:S(2)}) collective-permute-start(bf16[1024,256]{1,0:T(8,128)(2,1)} %own_ref.6), channel_id=1, source_target_pairs={{0,1},{1,0},{2,3},{3,2},{4,5},{5,4},{6,7},{7,6},{8,9},{9,8},{10,11... | collective-permute-start | bytes 1572872 | tf_op jit(solution)/shard_map/ppermute | solution.py:25
  0.8 0.9 %slice.39 = bf16[256,256]{1,0:T(8,128)(2,1)S(1)} slice(bf16[1024,256]{1,0:T(8,128)(2,1)} %own_ref.6), slice={[0:256], [0:256]} | slice | bytes 262144 | tf_op jit(solution)/shard_map/slice | solution.py:264
  1.7 0.9 %pad_maximum_fusion = bf16[512,256]{1,0:T(8,128)(2,1)S(1)} fusion(bf16[256,256]{1,0:T(8,128)(2,1)} %param.11, bf16[256,256]{1,0:T(8,128)(2,1)S(1)} %slice.39), kind=kLoop, calls=%fused_computation.3 | loop fusion | flops 524288 | bytes 524288 | tf_op jit(solution)/shard_map/concatenate | solution.py:35
  2.6 0.0 copy-start.1
  2.6 0.0 copy-start.2
  2.6 0.0 copy-start.3
  2.6 1.3 %collective-permute-start.3 = (bf16[512,256]{1,0:T(8,128)(2,1)S(1)}, bf16[512,256]{1,0:T(8,128)(2,1)S(1)}, u32[]{:S(2)}, u32[]{:S(2)}) collective-permute-start(bf16[512,256]{1,0:T(8,128)(2,1)S(1)} %pad_maximum_fusion), channel_id=1, source_target_pairs={{0,2},{1,3},{2,0},{3,1},{4,6},{5,7},{6,4},{7,5},{8,10},{9,11},{10,... | collective-permute-start | bytes 786440 | tf_op jit(solution)/shard_map/ppermute | solution.py:25
  4.0 0.2 collective-permute-start.11
  4.2 1.0 %slice.37 = bf16[512,256]{1,0:T(8,128)(2,1)S(1)} slice(bf16[1024,256]{1,0:T(8,128)(2,1)} %own_ref.6), slice={[0:512], [0:256]} | slice | bytes 524288 | tf_op jit(solution)/shard_map/slice | solution.py:271
  5.1 0.7 %convert.3 = bf16[1024]{0:T(1024)(128)(2,1)S(1)} convert(s32[1024]{0:T(1024)} %param.7) | non-fusion elementwise | flops 1024 | bytes 6144 | tf_op jit(solution)/shard_map/convert
  5.9 2.2 %collective-permute-start.1 = (bf16[528,256]{1,0:T(8,128)(2,1)S(1)}, bf16[528,256]{1,0:T(8,128)(2,1)S(1)}, u32[]{:S(2)}, u32[]{:S(2)}) collective-permute-start(bf16[528,256]{1,0:T(8,128)(2,1)S(1)} %fusion.1), channel_id=1, source_target_pairs={{4,0},{8,4},{12,8},{16,12},{20,16},{24,20},{28,24},{5,1},{9,5},{13... | collective-permute-start | bytes 811016 | tf_op jit(solution)/shard_map/ppermute | solution.py:30
  8.1 0.0 copy-done
  8.1 1.3 %collective-permute-start.4 = (bf16[768,256]{1,0:T(8,128)(2,1)S(1)}, bf16[768,256]{1,0:T(8,128)(2,1)S(1)}, u32[]{:S(2)}, u32[]{:S(2)}) collective-permute-start(bf16[768,256]{1,0:T(8,128)(2,1)S(1)} %slice.40), channel_id=1, source_target_pairs={{0,2},{1,3},{2,0},{3,1},{4,6},{5,7},{6,4},{7,5},{8,10},{9,11},{10,... | collective-permute-start | bytes 1179656 | tf_op jit(solution)/shard_map/ppermute | solution.py:25
  9.4 0.0 copy-done.5
  9.4 1.2 %collective-permute-done.11 = s32[256]{0:T(256)S(1)} collective-permute-done((s32[256]{0:T(256)}, s32[256]{0:T(256)S(1)}, u32[]{:S(2)}, u32[]{:S(2)}) %collective-permute-start.11) | collective-permute-done | bytes 1056 | tf_op jit(solution)/shard_map/ppermute | solution.py:25
  10.6 0.0 collective-permute-done.3.refs_0_.refs_2_
  10.6 0.0 copy-done.4
  10.6 0.1 broadcast_select_fusion.1
  10.8 0.0 collective-permute-done.other_ref
  10.8 0.0 copy-done.1
  10.8 0.0 copy-done.2
  10.8 0.0 copy-done.3
  10.8 1.2 %early_0.1 = (f32[4,256,256]{2,1,0:T(8,128)S(1)}, f32[8,1536]{1,0:T(8,128)S(1)}, f32[256,256]{1,0:T(8,128)S(1)}) custom-call(s32[4,4]{1,0:T(4,128)S(1)} %copy-done.2, s32[4]{0:T(128)S(1)} %copy-done.3, s32[1,1024]{1,0:T(1,128)S(1)} %bitcast.1, bf16[1024,256]{1,0:T(8,128)(2,1)S(1)} %copy-done, bf16[1024,256]{1,0:T(8,128)(2,1)S(1)} %collective-permute-done.other_ref), custom_call_target="tpu_custom_call" | custom-call | flops 1 | bytes 1 | tf_op jit(solution)/shard_map/early_0/pallas_call | solution.py:278
  12.0 2.2 %collective-permute-start.12 = (bf16[512,256]{1,0:T(8,128)(2,1)S(1)}, bf16[512,256]{1,0:T(8,128)(2,1)S(1)}, u32[]{:S(2)}, u32[]{:S(2)}) collective-permute-start(bf16[512,256]{1,0:T(8,128)(2,1)S(1)} %pad_maximum_fusion.1), channel_id=1, source_target_pairs={{4,0},{8,4},{12,8},{16,12},{20,16},{24,20},{28,24},{5,1},{9,5},{13... | collective-permute-start | bytes 786440 | tf_op jit(solution)/shard_map/ppermute | solution.py:30
  14.2 1.2 %collective-permute-start.6 = (bf16[256,256]{1,0:T(8,128)(2,1)S(1)}, bf16[256,256]{1,0:T(8,128)(2,1)S(1)}, u32[]{:S(2)}, u32[]{:S(2)}) collective-permute-start(bf16[256,256]{1,0:T(8,128)(2,1)S(1)} %get-tuple-element.34), channel_id=1, source_target_pairs={{0,1},{1,0},{2,3},{3,2},{4,5},{5,4},{6,7},{7,6},{8,9},{9,8},{10,11... | collective-permute-start | bytes 393224 | tf_op jit(solution)/shard_map/ppermute | solution.py:25
  15.4 0.7 %collective-permute-done.1.near_ref = bf16[528,256]{1,0:T(8,128)(2,1)S(1)} collective-permute-done((bf16[528,256]{1,0:T(8,128)(2,1)S(1)}, bf16[528,256]{1,0:T(8,128)(2,1)S(1)}, u32[]{:S(2)}, u32[]{:S(2)}) %collective-permute-start.1) | collective-permute-done | bytes 270368 | tf_op jit(solution)/shard_map/ppermute | solution.py:30
  16.1 1.3 %collective-permute-start.5 = (bf16[256,256]{1,0:T(8,128)(2,1)S(1)}, bf16[256,256]{1,0:T(8,128)(2,1)S(1)}, u32[]{:S(2)}, u32[]{:S(2)}) collective-permute-start(bf16[256,256]{1,0:T(8,128)(2,1)S(1)} %slice.46), channel_id=1, source_target_pairs={{0,2},{1,3},{2,0},{3,1},{4,6},{5,7},{6,4},{7,5},{8,10},{9,11},{10,... | collective-permute-start | bytes 393224 | tf_op jit(solution)/shard_map/ppermute | solution.py:25
  17.4 1.8 %collective-permute-start.2 = (bf16[528,256]{1,0:T(8,128)(2,1)S(1)}, bf16[528,256]{1,0:T(8,128)(2,1)S(1)}, u32[]{:S(2)}, u32[]{:S(2)}) collective-permute-start(bf16[528,256]{1,0:T(8,128)(2,1)S(1)} %collective-permute-done.1.near_ref), channel_id=1, source_target_pairs={{0,1},{1,0},{2,3},{3,2},{4,5},{5,4},{6,7},{7,6},{8,9},{9,8},{10,11... | collective-permute-start | bytes 811016 | tf_op jit(solution)/shard_map/ppermute | solution.py:25
  19.2 0.0 collective-permute-done.4.refs_1_.refs_3_
  19.2 1.3 %collective-permute-start.7 = (bf16[256,256]{1,0:T(8,128)(2,1)S(1)}, bf16[256,256]{1,0:T(8,128)(2,1)S(1)}, u32[]{:S(2)}, u32[]{:S(2)}) collective-permute-start(bf16[256,256]{1,0:T(8,128)(2,1)S(1)} %slice.48), channel_id=1, source_target_pairs={{0,1},{1,0},{2,3},{3,2},{4,5},{5,4},{6,7},{7,6},{8,9},{9,8},{10,11... | collective-permute-start | bytes 393224 | tf_op jit(solution)/shard_map/ppermute | solution.py:25
  20.5 0.0 collective-permute-done.6.refs_3_.refs_6_
  20.5 0.1 collective-permute-start.8
  20.6 0.3 collective-permute-done.5.refs_2_.refs_5_
  20.9 1.8 %collective-permute-start.9 = (bf16[256,256]{1,0:T(8,128)(2,1)S(1)}, bf16[256,256]{1,0:T(8,128)(2,1)S(1)}, u32[]{:S(2)}, u32[]{:S(2)}) collective-permute-start(bf16[256,256]{1,0:T(8,128)(2,1)S(1)} %collective-permute-done.5.refs_2_.refs_5_), channel_id=1, source_target_pairs={{0,1},{1,0},{2,3},{3,2},{4,5},{5,4},{6,7},{7,6},{8,9},{9,8},{10,11... | collective-permute-start | bytes 393224 | tf_op jit(solution)/shard_map/ppermute | solution.py:25
  22.7 0.0 collective-permute-done.12.refs_4_
  22.7 0.8 %collective-permute-start.13 = (bf16[512,256]{1,0:T(8,128)(2,1)S(1)}, bf16[512,256]{1,0:T(8,128)(2,1)S(1)}, u32[]{:S(2)}, u32[]{:S(2)}) collective-permute-start(bf16[512,256]{1,0:T(8,128)(2,1)S(1)} %collective-permute-done.12.refs_4_), channel_id=1, source_target_pairs={{0,1},{1,0},{2,3},{3,2},{4,5},{5,4},{6,7},{7,6},{8,9},{9,8},{10,11... | collective-permute-start | bytes 786440 | tf_op jit(solution)/shard_map/ppermute | solution.py:25
  23.5 0.0 collective-permute-done.7.refs_4_.refs_7_
  23.5 0.0 collective-permute-start.10
  23.5 0.1 collective-permute-done.9.refs_6_.refs_10_
  23.7 0.4 %collective-permute-start.14 = (bf16[256,256]{1,0:T(8,128)(2,1)S(1)}, bf16[256,256]{1,0:T(8,128)(2,1)S(1)}, u32[]{:S(2)}, u32[]{:S(2)}) collective-permute-start(bf16[256,256]{1,0:T(8,128)(2,1)S(1)} %get-tuple-element.32.refs_11_), channel_id=1, source_target_pairs={{0,1},{1,0},{2,3},{3,2},{4,5},{5,4},{6,7},{7,6},{8,9},{9,8},{10,11... | collective-permute-start | bytes 393224 | tf_op jit(solution)/shard_map/ppermute | solution.py:25
  24.1 0.0 collective-permute-done.2.near_other_ref
  24.1 0.0 collective-permute-done.8.refs_5_.refs_8_
  24.1 1.1 %logits_0.1.logit_ref = f32[6,256,256]{2,1,0:T(8,128)S(1)} custom-call(f32[4,256,256]{2,1,0:T(8,128)S(1)} %get-tuple-element.18.part_ref, f32[8,1536]{1,0:T(8,128)S(1)} %get-tuple-element.19.factor_ref, f32[256,256]{1,0:T(8,128)S(1)} %get-tuple-element.20.row_ref, bf16[1024,256]{1,0:T(8,128)(2,1)S(1)} %copy-done, ...), custom_call_target="tpu_custom_call" | custom-call | flops 1 | bytes 1 | tf_op jit(solution)/shard_map/logits_0/pallas_call | solution.py:365
  25.1 0.0 collective-permute-done.10.refs_1_
  25.2 0.0 collective-permute-done.14.refs_12_
  25.2 0.0 collective-permute-done.13.refs_9_
  25.2 1.1 %affinity_0.1 = (bf16[6,256,256]{2,1,0:T(8,128)(2,1)S(1)}, bf16[256,256]{1,0:T(8,128)(2,1)S(1)}) custom-call(f32[6,256,256]{2,1,0:T(8,128)S(1)} %logits_0.1.logit_ref, f32[8,1536]{1,0:T(8,128)S(1)} %get-tuple-element.19.factor_ref, bf16[256,256]{1,0:T(8,128)(2,1)S(1)} %get-tuple-element.33.refs_0_.seed_ref, ...), custom_call_target="tpu_custom_call" | custom-call | flops 1 | bytes 1 | tf_op jit(solution)/shard_map/affinity_0/pallas_call | solution.py:374
  26.3 2.8 %collective-permute-start.17 = (bf16[256,256]{1,0:T(8,128)(2,1)S(1)}, bf16[256,256]{1,0:T(8,128)(2,1)S(1)}, u32[]{:S(2)}, u32[]{:S(2)}) collective-permute-start(bf16[256,256]{1,0:T(8,128)(2,1)S(1)} %get-tuple-element.23.refs_2_), channel_id=1, source_target_pairs={{4,0},{8,4},{12,8},{16,12},{20,16},{24,20},{28,24},{5,1},{9,5},{13... | collective-permute-start | bytes 393224 | tf_op jit(solution)/shard_map/ppermute | solution.py:30
  29.1 1.2 %early_1.1 = (f32[4,256,256]{2,1,0:T(8,128)S(1)}, f32[8,1536]{1,0:T(8,128)S(1)}, f32[256,256]{1,0:T(8,128)S(1)}) custom-call(s32[4,4]{1,0:T(4,128)S(1)} %copy-done.2, s32[4]{0:T(128)S(1)} %copy-done.3, s32[1,1024]{1,0:T(1,128)S(1)} %bitcast.2, bf16[1024,256]{1,0:T(8,128)(2,1)S(1)} %copy-done, bf16[1024,256]{1,0:T(8,128)(2,1)S(1)} %collective-permute-done.other_ref), custom_call_target="tpu_custom_call" | custom-call | flops 1 | bytes 1 | tf_op jit(solution)/shard_map/early_1/pallas_call | solution.py:278
  30.3 1.1 %logits_1.1.logit_ref = f32[6,256,256]{2,1,0:T(8,128)S(1)} custom-call(f32[4,256,256]{2,1,0:T(8,128)S(1)} %get-tuple-element.26.part_ref, f32[8,1536]{1,0:T(8,128)S(1)} %get-tuple-element.27.factor_ref, f32[256,256]{1,0:T(8,128)S(1)} %get-tuple-element.28.row_ref, bf16[1024,256]{1,0:T(8,128)(2,1)S(1)} %copy-done, ...), custom_call_target="tpu_custom_call" | custom-call | flops 1 | bytes 1 | tf_op jit(solution)/shard_map/logits_1/pallas_call | solution.py:365
  31.3 0.6 %collective-permute-start.15 = (bf16[256,256]{1,0:T(8,128)(2,1)S(1)}, bf16[256,256]{1,0:T(8,128)(2,1)S(1)}, u32[]{:S(2)}, u32[]{:S(2)}) collective-permute-start(bf16[256,256]{1,0:T(8,128)(2,1)S(1)} %get-tuple-element.23.refs_2_), channel_id=1, source_target_pairs={{0,1},{1,0},{2,3},{3,2},{4,5},{5,4},{6,7},{7,6},{8,9},{9,8},{10,11... | collective-permute-start | bytes 393224 | tf_op jit(solution)/shard_map/ppermute | solution.py:25
  31.9 1.1 %affinity_1.1 = (bf16[6,256,256]{2,1,0:T(8,128)(2,1)S(1)}, bf16[256,256]{1,0:T(8,128)(2,1)S(1)}) custom-call(f32[6,256,256]{2,1,0:T(8,128)S(1)} %logits_1.1.logit_ref, f32[8,1536]{1,0:T(8,128)S(1)} %get-tuple-element.27.factor_ref, bf16[256,256]{1,0:T(8,128)(2,1)S(1)} %get-tuple-element.33.refs_0_.seed_ref, ...), custom_call_target="tpu_custom_call" | custom-call | flops 1 | bytes 1 | tf_op jit(solution)/shard_map/affinity_1/pallas_call | solution.py:374
  33.0 0.1 collective-permute-start.16
  33.1 0.8 %collective-permute-done.17.labels_ref = bf16[256,256]{1,0:T(8,128)(2,1)S(1)} collective-permute-done((bf16[256,256]{1,0:T(8,128)(2,1)S(1)}, bf16[256,256]{1,0:T(8,128)(2,1)S(1)}, u32[]{:S(2)}, u32[]{:S(2)}) %collective-permute-start.17) | collective-permute-done | bytes 131104 | tf_op jit(solution)/shard_map/ppermute | solution.py:30
  33.9 1.1 %collective-permute-start.18 = (bf16[256,256]{1,0:T(8,128)(2,1)S(1)}, bf16[256,256]{1,0:T(8,128)(2,1)S(1)}, u32[]{:S(2)}, u32[]{:S(2)}) collective-permute-start(bf16[256,256]{1,0:T(8,128)(2,1)S(1)} %collective-permute-done.17.labels_ref), channel_id=1, source_target_pairs={{0,1},{1,0},{2,3},{3,2},{4,5},{5,4},{6,7},{7,6},{8,9},{9,8},{10,11... | collective-permute-start | bytes 393224 | tf_op jit(solution)/shard_map/ppermute | solution.py:25
  35.0 0.0 collective-permute-done.15.refs_4_
  35.0 0.0 collective-permute-done.16.refs_5_
  35.0 0.3 spread_own.1.total_ref
  35.3 0.2 spread_near_0.1.total_ref
  35.5 0.4 %collective-permute-done.18.labels_ref = bf16[256,256]{1,0:T(8,128)(2,1)S(1)} collective-permute-done((bf16[256,256]{1,0:T(8,128)(2,1)S(1)}, bf16[256,256]{1,0:T(8,128)(2,1)S(1)}, u32[]{:S(2)}, u32[]{:S(2)}) %collective-permute-start.18) | collective-permute-done | bytes 131104 | tf_op jit(solution)/shard_map/ppermute | solution.py:25
  36.0 0.8 %spread_near_1.1 = bf16[256,256]{1,0:T(8,128)(2,1)} custom-call(f32[256,256]{1,0:T(8,128)S(1)} %spread_near_0.1.total_ref, bf16[256,256]{1,0:T(8,128)(2,1)S(1)} %collective-permute-done.18.labels_ref, bf16[6,256,256]{2,1,0:T(8,128)(2,1)S(1)} %get-tuple-element.22.refs_0_, bf16[6,256,256]{2,1,0:T(8,128)(2,1)S(1)} %get-tuple-element.29.refs_1_), custom_call_target="tpu_custom_call" | custom-call | flops 1 | bytes 1 | tf_op jit(solution)/shard_map/spread_near_1/pallas_call | solution.py:403
  (10 shorter events, 0.1 us)
Async XLA Ops:
  0.0 8.1 %copy-start = (bf16[1024,256]{1,0:T(8,128)(2,1)S(1)}, bf16[1024,256]{1,0:T(8,128)(2,1)}, u32[]{:S(2)}) copy-start(bf16[1024,256]{1,0:T(8,128)(2,1)} %own_ref.6) | copy-start | bytes 1572868
  0.0 10.6 %copy-start.4 = (bf16[256,256]{1,0:T(8,128)(2,1)S(1)}, bf16[256,256]{1,0:T(8,128)(2,1)}, u32[]{:S(2)}) copy-start(bf16[256,256]{1,0:T(8,128)(2,1)} %param.11) | copy-start | bytes 393220
  0.0 9.4 %copy-start.5 = (s32[256]{0:T(256)S(1)}, s32[256]{0:T(256)}, u32[]{:S(2)}) copy-start(s32[256]{0:T(256)} %param.10) | copy-start | bytes 3076
  0.0 10.8 %collective-permute-start = (bf16[1024,256]{1,0:T(8,128)(2,1)}, bf16[1024,256]{1,0:T(8,128)(2,1)S(1)}, u32[]{:S(2)}, u32[]{:S(2)}) collective-permute-start(bf16[1024,256]{1,0:T(8,128)(2,1)} %own_ref.6), channel_id=1, source_target_pairs={{0,1},{1,0},{2,3},{3,2},{4,5},{5,4},{6,7},{7,6},{8,9},{9,8},{10,11... | collective-permute-start | bytes 1572872 | tf_op jit(solution)/shard_map/ppermute | solution.py:25
  2.6 8.2 %copy-start.1 = (s32[1024]{0:T(1024)S(1)}, s32[1024]{0:T(1024)}, u32[]{:S(2)}) copy-start(s32[1024]{0:T(1024)} %param.7) | copy-start | bytes 12292
  2.6 8.2 %copy-start.2 = (s32[4,4]{1,0:T(4,128)S(1)}, s32[4,4]{1,0:T(4,128)}, u32[]{:S(2)}) copy-start(s32[4,4]{1,0:T(4,128)} %blocks_ref.3) | copy-start | bytes 196
  2.6 8.2 %copy-start.3 = (s32[4]{0:T(128)S(1)}, s32[4]{0:T(128)}, u32[]{:S(2)}) copy-start(s32[4]{0:T(128)} %counts_ref.3) | copy-start | bytes 52
  2.6 8.0 %collective-permute-start.3 = (bf16[512,256]{1,0:T(8,128)(2,1)S(1)}, bf16[512,256]{1,0:T(8,128)(2,1)S(1)}, u32[]{:S(2)}, u32[]{:S(2)}) collective-permute-start(bf16[512,256]{1,0:T(8,128)(2,1)S(1)} %pad_maximum_fusion), channel_id=1, source_target_pairs={{0,2},{1,3},{2,0},{3,1},{4,6},{5,7},{6,4},{7,5},{8,10},{9,11},{10,... | collective-permute-start | bytes 786440 | tf_op jit(solution)/shard_map/ppermute | solution.py:25
  4.0 6.6 %collective-permute-start.11 = (s32[256]{0:T(256)}, s32[256]{0:T(256)S(1)}, u32[]{:S(2)}, u32[]{:S(2)}) collective-permute-start(s32[256]{0:T(256)} %param.10), channel_id=1, source_target_pairs={{0,2},{1,3},{2,0},{3,1},{4,6},{5,7},{6,4},{7,5},{8,10},{9,11},{10,... | collective-permute-start | bytes 3080 | tf_op jit(solution)/shard_map/ppermute | solution.py:25
  5.9 10.2 %collective-permute-start.1 = (bf16[528,256]{1,0:T(8,128)(2,1)S(1)}, bf16[528,256]{1,0:T(8,128)(2,1)S(1)}, u32[]{:S(2)}, u32[]{:S(2)}) collective-permute-start(bf16[528,256]{1,0:T(8,128)(2,1)S(1)} %fusion.1), channel_id=1, source_target_pairs={{4,0},{8,4},{12,8},{16,12},{20,16},{24,20},{28,24},{5,1},{9,5},{13... | collective-permute-start | bytes 811016 | tf_op jit(solution)/shard_map/ppermute | solution.py:30
  8.1 11.1 %collective-permute-start.4 = (bf16[768,256]{1,0:T(8,128)(2,1)S(1)}, bf16[768,256]{1,0:T(8,128)(2,1)S(1)}, u32[]{:S(2)}, u32[]{:S(2)}) collective-permute-start(bf16[768,256]{1,0:T(8,128)(2,1)S(1)} %slice.40), channel_id=1, source_target_pairs={{0,2},{1,3},{2,0},{3,1},{4,6},{5,7},{6,4},{7,5},{8,10},{9,11},{10,... | collective-permute-start | bytes 1179656 | tf_op jit(solution)/shard_map/ppermute | solution.py:25
  12.0 10.7 %collective-permute-start.12 = (bf16[512,256]{1,0:T(8,128)(2,1)S(1)}, bf16[512,256]{1,0:T(8,128)(2,1)S(1)}, u32[]{:S(2)}, u32[]{:S(2)}) collective-permute-start(bf16[512,256]{1,0:T(8,128)(2,1)S(1)} %pad_maximum_fusion.1), channel_id=1, source_target_pairs={{4,0},{8,4},{12,8},{16,12},{20,16},{24,20},{28,24},{5,1},{9,5},{13... | collective-permute-start | bytes 786440 | tf_op jit(solution)/shard_map/ppermute | solution.py:30
  14.2 6.3 %collective-permute-start.6 = (bf16[256,256]{1,0:T(8,128)(2,1)S(1)}, bf16[256,256]{1,0:T(8,128)(2,1)S(1)}, u32[]{:S(2)}, u32[]{:S(2)}) collective-permute-start(bf16[256,256]{1,0:T(8,128)(2,1)S(1)} %get-tuple-element.34), channel_id=1, source_target_pairs={{0,1},{1,0},{2,3},{3,2},{4,5},{5,4},{6,7},{7,6},{8,9},{9,8},{10,11... | collective-permute-start | bytes 393224 | tf_op jit(solution)/shard_map/ppermute | solution.py:25
  16.1 4.8 %collective-permute-start.5 = (bf16[256,256]{1,0:T(8,128)(2,1)S(1)}, bf16[256,256]{1,0:T(8,128)(2,1)S(1)}, u32[]{:S(2)}, u32[]{:S(2)}) collective-permute-start(bf16[256,256]{1,0:T(8,128)(2,1)S(1)} %slice.46), channel_id=1, source_target_pairs={{0,2},{1,3},{2,0},{3,1},{4,6},{5,7},{6,4},{7,5},{8,10},{9,11},{10,... | collective-permute-start | bytes 393224 | tf_op jit(solution)/shard_map/ppermute | solution.py:25
  17.4 6.7 %collective-permute-start.2 = (bf16[528,256]{1,0:T(8,128)(2,1)S(1)}, bf16[528,256]{1,0:T(8,128)(2,1)S(1)}, u32[]{:S(2)}, u32[]{:S(2)}) collective-permute-start(bf16[528,256]{1,0:T(8,128)(2,1)S(1)} %collective-permute-done.1.near_ref), channel_id=1, source_target_pairs={{0,1},{1,0},{2,3},{3,2},{4,5},{5,4},{6,7},{7,6},{8,9},{9,8},{10,11... | collective-permute-start | bytes 811016 | tf_op jit(solution)/shard_map/ppermute | solution.py:25
  19.2 4.3 %collective-permute-start.7 = (bf16[256,256]{1,0:T(8,128)(2,1)S(1)}, bf16[256,256]{1,0:T(8,128)(2,1)S(1)}, u32[]{:S(2)}, u32[]{:S(2)}) collective-permute-start(bf16[256,256]{1,0:T(8,128)(2,1)S(1)} %slice.48), channel_id=1, source_target_pairs={{0,1},{1,0},{2,3},{3,2},{4,5},{5,4},{6,7},{7,6},{8,9},{9,8},{10,11... | collective-permute-start | bytes 393224 | tf_op jit(solution)/shard_map/ppermute | solution.py:25
  20.5 3.5 %collective-permute-start.8 = (bf16[512,256]{1,0:T(8,128)(2,1)S(1)}, bf16[512,256]{1,0:T(8,128)(2,1)S(1)}, u32[]{:S(2)}, u32[]{:S(2)}) collective-permute-start(bf16[512,256]{1,0:T(8,128)(2,1)S(1)} %slice.49), channel_id=1, source_target_pairs={{0,1},{1,0},{2,3},{3,2},{4,5},{5,4},{6,7},{7,6},{8,9},{9,8},{10,11... | collective-permute-start | bytes 786440 | tf_op jit(solution)/shard_map/ppermute | solution.py:25
  20.9 2.8 %collective-permute-start.9 = (bf16[256,256]{1,0:T(8,128)(2,1)S(1)}, bf16[256,256]{1,0:T(8,128)(2,1)S(1)}, u32[]{:S(2)}, u32[]{:S(2)}) collective-permute-start(bf16[256,256]{1,0:T(8,128)(2,1)S(1)} %collective-permute-done.5.refs_2_.refs_5_), channel_id=1, source_target_pairs={{0,1},{1,0},{2,3},{3,2},{4,5},{5,4},{6,7},{7,6},{8,9},{9,8},{10,11... | collective-permute-start | bytes 393224 | tf_op jit(solution)/shard_map/ppermute | solution.py:25
  22.7 2.5 %collective-permute-start.13 = (bf16[512,256]{1,0:T(8,128)(2,1)S(1)}, bf16[512,256]{1,0:T(8,128)(2,1)S(1)}, u32[]{:S(2)}, u32[]{:S(2)}) collective-permute-start(bf16[512,256]{1,0:T(8,128)(2,1)S(1)} %collective-permute-done.12.refs_4_), channel_id=1, source_target_pairs={{0,1},{1,0},{2,3},{3,2},{4,5},{5,4},{6,7},{7,6},{8,9},{9,8},{10,11... | collective-permute-start | bytes 786440 | tf_op jit(solution)/shard_map/ppermute | solution.py:25
  23.5 1.6 %collective-permute-start.10 = (bf16[256,256]{1,0:T(8,128)(2,1)S(1)}, bf16[256,256]{1,0:T(8,128)(2,1)S(1)}, u32[]{:S(2)}, u32[]{:S(2)}) collective-permute-start(bf16[256,256]{1,0:T(8,128)(2,1)S(1)} %get-tuple-element.33.refs_0_.seed_ref), channel_id=1, source_target_pairs={{0,1},{1,0},{2,3},{3,2},{4,5},{5,4},{6,7},{7,6},{8,9},{9,8},{10,11... | collective-permute-start | bytes 393224 | tf_op jit(solution)/shard_map/ppermute | solution.py:25
  23.7 1.5 %collective-permute-start.14 = (bf16[256,256]{1,0:T(8,128)(2,1)S(1)}, bf16[256,256]{1,0:T(8,128)(2,1)S(1)}, u32[]{:S(2)}, u32[]{:S(2)}) collective-permute-start(bf16[256,256]{1,0:T(8,128)(2,1)S(1)} %get-tuple-element.32.refs_11_), channel_id=1, source_target_pairs={{0,1},{1,0},{2,3},{3,2},{4,5},{5,4},{6,7},{7,6},{8,9},{9,8},{10,11... | collective-permute-start | bytes 393224 | tf_op jit(solution)/shard_map/ppermute | solution.py:25
  26.3 7.6 %collective-permute-start.17 = (bf16[256,256]{1,0:T(8,128)(2,1)S(1)}, bf16[256,256]{1,0:T(8,128)(2,1)S(1)}, u32[]{:S(2)}, u32[]{:S(2)}) collective-permute-start(bf16[256,256]{1,0:T(8,128)(2,1)S(1)} %get-tuple-element.23.refs_2_), channel_id=1, source_target_pairs={{4,0},{8,4},{12,8},{16,12},{20,16},{24,20},{28,24},{5,1},{9,5},{13... | collective-permute-start | bytes 393224 | tf_op jit(solution)/shard_map/ppermute | solution.py:30
  31.3 3.6 %collective-permute-start.15 = (bf16[256,256]{1,0:T(8,128)(2,1)S(1)}, bf16[256,256]{1,0:T(8,128)(2,1)S(1)}, u32[]{:S(2)}, u32[]{:S(2)}) collective-permute-start(bf16[256,256]{1,0:T(8,128)(2,1)S(1)} %get-tuple-element.23.refs_2_), channel_id=1, source_target_pairs={{0,1},{1,0},{2,3},{3,2},{4,5},{5,4},{6,7},{7,6},{8,9},{9,8},{10,11... | collective-permute-start | bytes 393224 | tf_op jit(solution)/shard_map/ppermute | solution.py:25
  33.0 2.0 %collective-permute-start.16 = (bf16[256,256]{1,0:T(8,128)(2,1)S(1)}, bf16[256,256]{1,0:T(8,128)(2,1)S(1)}, u32[]{:S(2)}, u32[]{:S(2)}) collective-permute-start(bf16[256,256]{1,0:T(8,128)(2,1)S(1)} %get-tuple-element.30.refs_3_), channel_id=1, source_target_pairs={{0,1},{1,0},{2,3},{3,2},{4,5},{5,4},{6,7},{7,6},{8,9},{9,8},{10,11... | collective-permute-start | bytes 393224 | tf_op jit(solution)/shard_map/ppermute | solution.py:25
  33.9 2.1 %collective-permute-start.18 = (bf16[256,256]{1,0:T(8,128)(2,1)S(1)}, bf16[256,256]{1,0:T(8,128)(2,1)S(1)}, u32[]{:S(2)}, u32[]{:S(2)}) collective-permute-start(bf16[256,256]{1,0:T(8,128)(2,1)S(1)} %collective-permute-done.17.labels_ref), channel_id=1, source_target_pairs={{0,1},{1,0},{2,3},{3,2},{4,5},{5,4},{6,7},{7,6},{8,9},{9,8},{10,11... | collective-permute-start | bytes 393224 | tf_op jit(solution)/shard_map/ppermute | solution.py:25

commit v4 on v3

--- a/solution.py
+++ b/solution.py
@@ -34,6 +34,13 @@
     if len({b.shape[1] for b in blocks}) == 1:
         return (jnp.concatenate(blocks),)
     return blocks
+
+
+def tile_and(tiles, block):
+    if tiles.shape[1] != block.shape[1]:
+        return tiles[:TILE], block
+    first = lax.broadcasted_iota(jnp.int32, tiles.shape, 0) < TILE
+    return (jnp.where(first, tiles, jnp.concatenate([block, block])),)
 
 
 def tile_in(blocks, t):
@@ -261,7 +268,7 @@
     labels_shape = jax.ShapeDtypeStruct((TILE, concepts), jnp.bfloat16)
 
     first_far = [
-        tuple(across(b, 2 * m) for b in bundle(embeddings[:TILE], prior)) for m in apart
+        tuple(across(b, 2 * m) for b in tile_and(embeddings[:2 * TILE], prior)) for m in apart
     ]
     mask_far = [across(seed_mask, 2 * m) for m in apart]
     rest_far = [across(embeddings[TILE:], 2 * m) for m in apart]

time: 37.1 us -> 36.3 us (0.978)
  waiting for transfers between devices: 3.51 us -> 6.22 us
  local copies, waits for them, and re-layouts: 2 us -> 0.12 us
  starting transfers between devices: 21.2 us -> 19.5 us
    ppermute x16, waiting for transfers between devices: 2.05 us -> 4.82 us  [across(): lax.ppermute(block, 'grp', [(i, i ^ distance) for i in range(groups)])]
    slice x2 -> x0, local copies, waits for them, and re-layouts: 1.88 us -> none  [the longest x1 0.97 us: local(): near = from_next(jnp.concatenate([embeddings[:head_rows], head_c]))]
    slice x0 -> x1, other arithmetic: none -> 1.18 us  [local(): near = from_next(jnp.concatenate([embeddings[:head_rows], head_c]))]
    ppermute x16, starting transfers between devices: 14.1 us -> 12.9 us  [across(): lax.ppermute(block, 'grp', [(i, i ^ distance) for i in range(groups)])]
    concatenate x2 -> x1, other arithmetic: 0.94 us -> 0.02 us  [bundle(): return (jnp.concatenate(blocks),)]
    ppermute x3, starting transfers between devices: 7.13 us -> 6.54 us  [from_next(): return lax.ppermute(block, 'shard', [(i + 1, i) for i in range(shards - 1)])]
  transfers between devices with their start and end apart: 19 -> 19, of which waited for: 6 -> 6; matrix products, arithmetic and copies ran while one was open for 10% -> 6% of each run, Pallas kernels for 17% -> 17%
where the time goes in v4:
time: 36.3 us; the launch traced here: 36.1 us
  starting transfers between devices  19.5 us (54%)
  Pallas kernels  8 us (22%)
  waiting for transfers between devices  6.22 us (17%)
  other arithmetic  2.06 us (6%)
    ppermute x16, starting transfers between devices, across(): lax.ppermute(block, 'grp', [(i, i ^ distance) for i in range(groups)])  12.9 us
    ppermute x3, starting transfers between devices, from_next(): return lax.ppermute(block, 'shard', [(i + 1, i) for i in range(shards - 1)])  6.54 us
    ppermute x16, waiting for transfers between devices, across(): lax.ppermute(block, 'grp', [(i, i ^ distance) for i in range(groups)])  4.82 us
    pallas_call x2, Pallas kernels, early_of(): pl.pallas_call(functools.partial(early_kernel, groups, m), out_shape=(jax...  2.36 us
    pallas_call x2, Pallas kernels, affinity_of(): pl.pallas_call(functools.partial(affinity_kernel, groups, m, windows), ou...  2.14 us
    pallas_call x2, Pallas kernels, affinity_of(): pl.pallas_call(functools.partial(logit_kernel, groups, m, early_windows),...  2.14 us
    ppermute x3, waiting for transfers between devices, from_next(): return lax.ppermute(block, 'shard', [(i + 1, i) for i in range(shards - 1)])  1.4 us
    slice x1, other arithmetic, local(): near = from_next(jnp.concatenate([embeddings[:head_rows], head_c]))  1.18 us
  transfers between devices with their start and end apart: 19, of which 6 were waited for; matrix products, arithmetic and copies ran while one was open for 6% of the time, Pallas kernels for 17%

profile of v4, /device:TPU:11, one launch (start us, length us, event | category | flops | bytes accessed | tf_op | source)
XLA Modules:
  0.0 36.1 jit_solution(6517220260591130847)
XLA Ops:
  0.0 0.0 copy-start
  0.0 0.0 copy-start.4
  0.0 0.0 copy-start.5
  0.0 0.7 %collective-permute-start = (bf16[1024,256]{1,0:T(8,128)(2,1)}, bf16[1024,256]{1,0:T(8,128)(2,1)S(1)}, u32[]{:S(2)}, u32[]{:S(2)}) collective-permute-start(bf16[1024,256]{1,0:T(8,128)(2,1)} %own_ref.6), channel_id=1, source_target_pairs={{0,1},{1,0},{2,3},{3,2},{4,5},{5,4},{6,7},{7,6},{8,9},{9,8},{10,11... | collective-permute-start | bytes 1572872 | tf_op jit(solution)/shard_map/ppermute | solution.py:25
  0.8 1.2 %fusion.2 = (bf16[512,256]{1,0:T(8,128)(2,1)S(1)}, bf16[512,256]{1,0:T(8,128)(2,1)S(1)}) fusion(bf16[1024,256]{1,0:T(8,128)(2,1)} %own_ref.6, bf16[256,256]{1,0:T(8,128)(2,1)} %param.11, pred[512]{0:T(512)(128)(4,1)S(1)} %iota_compare_fusion.1), kind=kLoop, calls=%fused_computation.11 | loop fusion | flops 655360 | bytes 918016 | tf_op jit(solution)/shard_map/slice | solution.py:278
  1.9 0.0 copy-start.1
  2.0 0.0 copy-start.2
  2.0 0.0 copy-start.3
  2.0 1.3 %collective-permute-start.3 = (bf16[512,256]{1,0:T(8,128)(2,1)S(1)}, bf16[512,256]{1,0:T(8,128)(2,1)S(1)}, u32[]{:S(2)}, u32[]{:S(2)}) collective-permute-start(bf16[512,256]{1,0:T(8,128)(2,1)S(1)} %get-tuple-element.35), channel_id=1, source_target_pairs={{0,2},{1,3},{2,0},{3,1},{4,6},{5,7},{6,4},{7,5},{8,10},{9,11},{10,... | collective-permute-start | bytes 786440 | tf_op jit(solution)/shard_map/ppermute | solution.py:25
  3.3 0.2 collective-permute-start.11
  3.5 0.7 %convert.3 = bf16[1024]{0:T(1024)(128)(2,1)S(1)} convert(s32[1024]{0:T(1024)} %param.7) | non-fusion elementwise | flops 1024 | bytes 6144 | tf_op jit(solution)/shard_map/convert
  4.3 2.2 %collective-permute-start.1 = (bf16[528,256]{1,0:T(8,128)(2,1)S(1)}, bf16[528,256]{1,0:T(8,128)(2,1)S(1)}, u32[]{:S(2)}, u32[]{:S(2)}) collective-permute-start(bf16[528,256]{1,0:T(8,128)(2,1)S(1)} %fusion.1), channel_id=1, source_target_pairs={{4,0},{8,4},{12,8},{16,12},{20,16},{24,20},{28,24},{5,1},{9,5},{13... | collective-permute-start | bytes 811016 | tf_op jit(solution)/shard_map/ppermute | solution.py:30
  6.4 0.0 copy-done
  6.5 1.3 %collective-permute-start.4 = (bf16[768,256]{1,0:T(8,128)(2,1)S(1)}, bf16[768,256]{1,0:T(8,128)(2,1)S(1)}, u32[]{:S(2)}, u32[]{:S(2)}) collective-permute-start(bf16[768,256]{1,0:T(8,128)(2,1)S(1)} %slice.37), channel_id=1, source_target_pairs={{0,2},{1,3},{2,0},{3,1},{4,6},{5,7},{6,4},{7,5},{8,10},{9,11},{10,... | collective-permute-start | bytes 1179656 | tf_op jit(solution)/shard_map/ppermute | solution.py:25
  7.8 0.0 copy-done.5
  7.8 2.1 %collective-permute-done.11 = s32[256]{0:T(256)S(1)} collective-permute-done((s32[256]{0:T(256)}, s32[256]{0:T(256)S(1)}, u32[]{:S(2)}, u32[]{:S(2)}) %collective-permute-start.11) | collective-permute-done | bytes 1056 | tf_op jit(solution)/shard_map/ppermute | solution.py:25
  9.9 0.0 collective-permute-done.3.refs_0_.refs_2_
  9.9 0.0 copy-done.4
  9.9 0.1 broadcast_select_fusion.1
  10.1 0.0 collective-permute-done.other_ref
  10.1 0.0 copy-done.1
  10.1 0.0 copy-done.2
  10.1 0.0 copy-done.3
  10.2 1.2 %early_0.1 = (f32[4,256,256]{2,1,0:T(8,128)S(1)}, f32[8,1536]{1,0:T(8,128)S(1)}, f32[256,256]{1,0:T(8,128)S(1)}) custom-call(s32[4,4]{1,0:T(4,128)S(1)} %copy-done.2, s32[4]{0:T(128)S(1)} %copy-done.3, s32[1,1024]{1,0:T(1,128)S(1)} %bitcast.1, bf16[1024,256]{1,0:T(8,128)(2,1)S(1)} %copy-done, bf16[1024,256]{1,0:T(8,128)(2,1)S(1)} %collective-permute-done.other_ref), custom_call_target="tpu_custom_call" | custom-call | flops 1 | bytes 1 | tf_op jit(solution)/shard_map/early_0/pallas_call | solution.py:285
  11.4 2.2 %collective-permute-start.12 = (bf16[512,256]{1,0:T(8,128)(2,1)S(1)}, bf16[512,256]{1,0:T(8,128)(2,1)S(1)}, u32[]{:S(2)}, u32[]{:S(2)}) collective-permute-start(bf16[512,256]{1,0:T(8,128)(2,1)S(1)} %pad_maximum_fusion), channel_id=1, source_target_pairs={{4,0},{8,4},{12,8},{16,12},{20,16},{24,20},{28,24},{5,1},{9,5},{13... | collective-permute-start | bytes 786440 | tf_op jit(solution)/shard_map/ppermute | solution.py:30
  13.5 1.5 %collective-permute-start.6 = (bf16[256,256]{1,0:T(8,128)(2,1)S(1)}, bf16[256,256]{1,0:T(8,128)(2,1)S(1)}, u32[]{:S(2)}, u32[]{:S(2)}) collective-permute-start(bf16[256,256]{1,0:T(8,128)(2,1)S(1)} %get-tuple-element.36), channel_id=1, source_target_pairs={{0,1},{1,0},{2,3},{3,2},{4,5},{5,4},{6,7},{7,6},{8,9},{9,8},{10,11... | collective-permute-start | bytes 393224 | tf_op jit(solution)/shard_map/ppermute | solution.py:25
  15.0 0.0 collective-permute-done.1.near_ref
  15.0 1.3 %collective-permute-start.5 = (bf16[256,256]{1,0:T(8,128)(2,1)S(1)}, bf16[256,256]{1,0:T(8,128)(2,1)S(1)}, u32[]{:S(2)}, u32[]{:S(2)}) collective-permute-start(bf16[256,256]{1,0:T(8,128)(2,1)S(1)} %slice.43), channel_id=1, source_target_pairs={{0,2},{1,3},{2,0},{3,1},{4,6},{5,7},{6,4},{7,5},{8,10},{9,11},{10,... | collective-permute-start | bytes 393224 | tf_op jit(solution)/shard_map/ppermute | solution.py:25
  16.3 1.2 %collective-permute-start.2 = (bf16[528,256]{1,0:T(8,128)(2,1)S(1)}, bf16[528,256]{1,0:T(8,128)(2,1)S(1)}, u32[]{:S(2)}, u32[]{:S(2)}) collective-permute-start(bf16[528,256]{1,0:T(8,128)(2,1)S(1)} %collective-permute-done.1.near_ref), channel_id=1, source_target_pairs={{0,1},{1,0},{2,3},{3,2},{4,5},{5,4},{6,7},{7,6},{8,9},{9,8},{10,11... | collective-permute-start | bytes 811016 | tf_op jit(solution)/shard_map/ppermute | solution.py:25
  17.6 0.8 %collective-permute-done.4.refs_1_.refs_3_ = bf16[768,256]{1,0:T(8,128)(2,1)S(1)} collective-permute-done((bf16[768,256]{1,0:T(8,128)(2,1)S(1)}, bf16[768,256]{1,0:T(8,128)(2,1)S(1)}, u32[]{:S(2)}, u32[]{:S(2)}) %collective-permute-start.4) | collective-permute-done | bytes 393248 | tf_op jit(solution)/shard_map/ppermute | solution.py:25
  18.4 1.4 %collective-permute-start.7 = (bf16[256,256]{1,0:T(8,128)(2,1)S(1)}, bf16[256,256]{1,0:T(8,128)(2,1)S(1)}, u32[]{:S(2)}, u32[]{:S(2)}) collective-permute-start(bf16[256,256]{1,0:T(8,128)(2,1)S(1)} %slice.45), channel_id=1, source_target_pairs={{0,1},{1,0},{2,3},{3,2},{4,5},{5,4},{6,7},{7,6},{8,9},{9,8},{10,11... | collective-permute-start | bytes 393224 | tf_op jit(solution)/shard_map/ppermute | solution.py:25
  19.8 0.0 collective-permute-done.6.refs_3_.refs_6_
  19.8 0.1 collective-permute-start.8
  19.9 1.3 %collective-permute-done.5.refs_2_.refs_5_ = bf16[256,256]{1,0:T(8,128)(2,1)S(1)} collective-permute-done((bf16[256,256]{1,0:T(8,128)(2,1)S(1)}, bf16[256,256]{1,0:T(8,128)(2,1)S(1)}, u32[]{:S(2)}, u32[]{:S(2)}) %collective-permute-start.5) | collective-permute-done | bytes 131104 | tf_op jit(solution)/shard_map/ppermute | solution.py:25
  21.2 0.9 %collective-permute-start.9 = (bf16[256,256]{1,0:T(8,128)(2,1)S(1)}, bf16[256,256]{1,0:T(8,128)(2,1)S(1)}, u32[]{:S(2)}, u32[]{:S(2)}) collective-permute-start(bf16[256,256]{1,0:T(8,128)(2,1)S(1)} %collective-permute-done.5.refs_2_.refs_5_), channel_id=1, source_target_pairs={{0,1},{1,0},{2,3},{3,2},{4,5},{5,4},{6,7},{7,6},{8,9},{9,8},{10,11... | collective-permute-start | bytes 393224 | tf_op jit(solution)/shard_map/ppermute | solution.py:25
  22.0 0.0 collective-permute-done.12.refs_4_
  22.0 0.8 %collective-permute-start.13 = (bf16[512,256]{1,0:T(8,128)(2,1)S(1)}, bf16[512,256]{1,0:T(8,128)(2,1)S(1)}, u32[]{:S(2)}, u32[]{:S(2)}) collective-permute-start(bf16[512,256]{1,0:T(8,128)(2,1)S(1)} %collective-permute-done.12.refs_4_), channel_id=1, source_target_pairs={{0,1},{1,0},{2,3},{3,2},{4,5},{5,4},{6,7},{7,6},{8,9},{9,8},{10,11... | collective-permute-start | bytes 786440 | tf_op jit(solution)/shard_map/ppermute | solution.py:25
  22.9 0.0 collective-permute-done.7.refs_4_.refs_7_
  22.9 0.0 collective-permute-start.10
  22.9 0.1 collective-permute-done.9.refs_6_.refs_10_
  23.0 0.4 %collective-permute-start.14 = (bf16[256,256]{1,0:T(8,128)(2,1)S(1)}, bf16[256,256]{1,0:T(8,128)(2,1)S(1)}, u32[]{:S(2)}, u32[]{:S(2)}) collective-permute-start(bf16[256,256]{1,0:T(8,128)(2,1)S(1)} %get-tuple-element.32.refs_11_), channel_id=1, source_target_pairs={{0,1},{1,0},{2,3},{3,2},{4,5},{5,4},{6,7},{7,6},{8,9},{9,8},{10,11... | collective-permute-start | bytes 393224 | tf_op jit(solution)/shard_map/ppermute | solution.py:25
  23.4 0.0 collective-permute-done.2.near_other_ref
  23.4 0.0 collective-permute-done.8.refs_5_.refs_8_
  23.4 1.1 %logits_0.1.logit_ref = f32[6,256,256]{2,1,0:T(8,128)S(1)} custom-call(f32[4,256,256]{2,1,0:T(8,128)S(1)} %get-tuple-element.18.part_ref, f32[8,1536]{1,0:T(8,128)S(1)} %get-tuple-element.19.factor_ref, f32[256,256]{1,0:T(8,128)S(1)} %get-tuple-element.20.row_ref, bf16[1024,256]{1,0:T(8,128)(2,1)S(1)} %copy-done, ...), custom_call_target="tpu_custom_call" | custom-call | flops 1 | bytes 1 | tf_op jit(solution)/shard_map/logits_0/pallas_call | solution.py:372
  24.5 0.0 collective-permute-done.10.refs_1_
  24.5 0.0 collective-permute-done.14.refs_12_
  24.5 0.0 collective-permute-done.13.refs_9_
  24.5 1.1 %affinity_0.1 = (bf16[6,256,256]{2,1,0:T(8,128)(2,1)S(1)}, bf16[256,256]{1,0:T(8,128)(2,1)S(1)}) custom-call(f32[6,256,256]{2,1,0:T(8,128)S(1)} %logits_0.1.logit_ref, f32[8,1536]{1,0:T(8,128)S(1)} %get-tuple-element.19.factor_ref, bf16[256,256]{1,0:T(8,128)(2,1)S(1)} %get-tuple-element.33.refs_0_.seed_ref, ...), custom_call_target="tpu_custom_call" | custom-call | flops 1 | bytes 1 | tf_op jit(solution)/shard_map/affinity_0/pallas_call | solution.py:381
  25.6 2.2 %collective-permute-start.17 = (bf16[256,256]{1,0:T(8,128)(2,1)S(1)}, bf16[256,256]{1,0:T(8,128)(2,1)S(1)}, u32[]{:S(2)}, u32[]{:S(2)}) collective-permute-start(bf16[256,256]{1,0:T(8,128)(2,1)S(1)} %get-tuple-element.23.refs_2_), channel_id=1, source_target_pairs={{4,0},{8,4},{12,8},{16,12},{20,16},{24,20},{28,24},{5,1},{9,5},{13... | collective-permute-start | bytes 393224 | tf_op jit(solution)/shard_map/ppermute | solution.py:30
  27.8 1.2 %early_1.1 = (f32[4,256,256]{2,1,0:T(8,128)S(1)}, f32[8,1536]{1,0:T(8,128)S(1)}, f32[256,256]{1,0:T(8,128)S(1)}) custom-call(s32[4,4]{1,0:T(4,128)S(1)} %copy-done.2, s32[4]{0:T(128)S(1)} %copy-done.3, s32[1,1024]{1,0:T(1,128)S(1)} %bitcast.2, bf16[1024,256]{1,0:T(8,128)(2,1)S(1)} %copy-done, bf16[1024,256]{1,0:T(8,128)(2,1)S(1)} %collective-permute-done.other_ref), custom_call_target="tpu_custom_call" | custom-call | flops 1 | bytes 1 | tf_op jit(solution)/shard_map/early_1/pallas_call | solution.py:285
  29.0 1.1 %logits_1.1.logit_ref = f32[6,256,256]{2,1,0:T(8,128)S(1)} custom-call(f32[4,256,256]{2,1,0:T(8,128)S(1)} %get-tuple-element.26.part_ref, f32[8,1536]{1,0:T(8,128)S(1)} %get-tuple-element.27.factor_ref, f32[256,256]{1,0:T(8,128)S(1)} %get-tuple-element.28.row_ref, bf16[1024,256]{1,0:T(8,128)(2,1)S(1)} %copy-done, ...), custom_call_target="tpu_custom_call" | custom-call | flops 1 | bytes 1 | tf_op jit(solution)/shard_map/logits_1/pallas_call | solution.py:372
  30.1 0.6 %collective-permute-start.15 = (bf16[256,256]{1,0:T(8,128)(2,1)S(1)}, bf16[256,256]{1,0:T(8,128)(2,1)S(1)}, u32[]{:S(2)}, u32[]{:S(2)}) collective-permute-start(bf16[256,256]{1,0:T(8,128)(2,1)S(1)} %get-tuple-element.23.refs_2_), channel_id=1, source_target_pairs={{0,1},{1,0},{2,3},{3,2},{4,5},{5,4},{6,7},{7,6},{8,9},{9,8},{10,11... | collective-permute-start | bytes 393224 | tf_op jit(solution)/shard_map/ppermute | solution.py:25
  30.6 1.1 %affinity_1.1 = (bf16[6,256,256]{2,1,0:T(8,128)(2,1)S(1)}, bf16[256,256]{1,0:T(8,128)(2,1)S(1)}) custom-call(f32[6,256,256]{2,1,0:T(8,128)S(1)} %logits_1.1.logit_ref, f32[8,1536]{1,0:T(8,128)S(1)} %get-tuple-element.27.factor_ref, bf16[256,256]{1,0:T(8,128)(2,1)S(1)} %get-tuple-element.33.refs_0_.seed_ref, ...), custom_call_target="tpu_custom_call" | custom-call | flops 1 | bytes 1 | tf_op jit(solution)/shard_map/affinity_1/pallas_call | solution.py:381
  31.7 0.1 collective-permute-start.16
  31.8 1.4 %collective-permute-done.17.labels_ref = bf16[256,256]{1,0:T(8,128)(2,1)S(1)} collective-permute-done((bf16[256,256]{1,0:T(8,128)(2,1)S(1)}, bf16[256,256]{1,0:T(8,128)(2,1)S(1)}, u32[]{:S(2)}, u32[]{:S(2)}) %collective-permute-start.17) | collective-permute-done | bytes 131104 | tf_op jit(solution)/shard_map/ppermute | solution.py:30
  33.2 1.1 %collective-permute-start.18 = (bf16[256,256]{1,0:T(8,128)(2,1)S(1)}, bf16[256,256]{1,0:T(8,128)(2,1)S(1)}, u32[]{:S(2)}, u32[]{:S(2)}) collective-permute-start(bf16[256,256]{1,0:T(8,128)(2,1)S(1)} %collective-permute-done.17.labels_ref), channel_id=1, source_target_pairs={{0,1},{1,0},{2,3},{3,2},{4,5},{5,4},{6,7},{7,6},{8,9},{9,8},{10,11... | collective-permute-start | bytes 393224 | tf_op jit(solution)/shard_map/ppermute | solution.py:25
  34.3 0.0 collective-permute-done.15.refs_4_
  34.3 0.0 collective-permute-done.16.refs_5_
  34.3 0.3 spread_own.1.total_ref
  34.6 0.2 spread_near_0.1.total_ref
  34.8 0.4 %collective-permute-done.18.labels_ref = bf16[256,256]{1,0:T(8,128)(2,1)S(1)} collective-permute-done((bf16[256,256]{1,0:T(8,128)(2,1)S(1)}, bf16[256,256]{1,0:T(8,128)(2,1)S(1)}, u32[]{:S(2)}, u32[]{:S(2)}) %collective-permute-start.18) | collective-permute-done | bytes 131104 | tf_op jit(solution)/shard_map/ppermute | solution.py:25
  35.3 0.8 %spread_near_1.1 = bf16[256,256]{1,0:T(8,128)(2,1)} custom-call(f32[256,256]{1,0:T(8,128)S(1)} %spread_near_0.1.total_ref, bf16[256,256]{1,0:T(8,128)(2,1)S(1)} %collective-permute-done.18.labels_ref, bf16[6,256,256]{2,1,0:T(8,128)(2,1)S(1)} %get-tuple-element.22.refs_0_, bf16[6,256,256]{2,1,0:T(8,128)(2,1)S(1)} %get-tuple-element.29.refs_1_), custom_call_target="tpu_custom_call" | custom-call | flops 1 | bytes 1 | tf_op jit(solution)/shard_map/spread_near_1/pallas_call | solution.py:410
  (11 shorter events, 0.1 us)
Async XLA Ops:
  0.0 6.4 %copy-start = (bf16[1024,256]{1,0:T(8,128)(2,1)S(1)}, bf16[1024,256]{1,0:T(8,128)(2,1)}, u32[]{:S(2)}) copy-start(bf16[1024,256]{1,0:T(8,128)(2,1)} %own_ref.6) | copy-start | bytes 1572868
  0.0 9.9 %copy-start.4 = (bf16[256,256]{1,0:T(8,128)(2,1)S(1)}, bf16[256,256]{1,0:T(8,128)(2,1)}, u32[]{:S(2)}) copy-start(bf16[256,256]{1,0:T(8,128)(2,1)} %param.11) | copy-start | bytes 393220
  0.0 7.8 %copy-start.5 = (s32[256]{0:T(256)S(1)}, s32[256]{0:T(256)}, u32[]{:S(2)}) copy-start(s32[256]{0:T(256)} %param.10) | copy-start | bytes 3076
  0.0 10.1 %collective-permute-start = (bf16[1024,256]{1,0:T(8,128)(2,1)}, bf16[1024,256]{1,0:T(8,128)(2,1)S(1)}, u32[]{:S(2)}, u32[]{:S(2)}) collective-permute-start(bf16[1024,256]{1,0:T(8,128)(2,1)} %own_ref.6), channel_id=1, source_target_pairs={{0,1},{1,0},{2,3},{3,2},{4,5},{5,4},{6,7},{7,6},{8,9},{9,8},{10,11... | collective-permute-start | bytes 1572872 | tf_op jit(solution)/shard_map/ppermute | solution.py:25
  1.9 8.2 %copy-start.1 = (s32[1024]{0:T(1024)S(1)}, s32[1024]{0:T(1024)}, u32[]{:S(2)}) copy-start(s32[1024]{0:T(1024)} %param.7) | copy-start | bytes 12292
  2.0 8.2 %copy-start.2 = (s32[4,4]{1,0:T(4,128)S(1)}, s32[4,4]{1,0:T(4,128)}, u32[]{:S(2)}) copy-start(s32[4,4]{1,0:T(4,128)} %blocks_ref.3) | copy-start | bytes 196
  2.0 8.2 %copy-start.3 = (s32[4]{0:T(128)S(1)}, s32[4]{0:T(128)}, u32[]{:S(2)}) copy-start(s32[4]{0:T(128)} %counts_ref.3) | copy-start | bytes 52
  2.0 8.0 %collective-permute-start.3 = (bf16[512,256]{1,0:T(8,128)(2,1)S(1)}, bf16[512,256]{1,0:T(8,128)(2,1)S(1)}, u32[]{:S(2)}, u32[]{:S(2)}) collective-permute-start(bf16[512,256]{1,0:T(8,128)(2,1)S(1)} %get-tuple-element.35), channel_id=1, source_target_pairs={{0,2},{1,3},{2,0},{3,1},{4,6},{5,7},{6,4},{7,5},{8,10},{9,11},{10,... | collective-permute-start | bytes 786440 | tf_op jit(solution)/shard_map/ppermute | solution.py:25
  3.3 6.6 %collective-permute-start.11 = (s32[256]{0:T(256)}, s32[256]{0:T(256)S(1)}, u32[]{:S(2)}, u32[]{:S(2)}) collective-permute-start(s32[256]{0:T(256)} %param.10), channel_id=1, source_target_pairs={{0,2},{1,3},{2,0},{3,1},{4,6},{5,7},{6,4},{7,5},{8,10},{9,11},{10,... | collective-permute-start | bytes 3080 | tf_op jit(solution)/shard_map/ppermute | solution.py:25
  4.3 10.8 %collective-permute-start.1 = (bf16[528,256]{1,0:T(8,128)(2,1)S(1)}, bf16[528,256]{1,0:T(8,128)(2,1)S(1)}, u32[]{:S(2)}, u32[]{:S(2)}) collective-permute-start(bf16[528,256]{1,0:T(8,128)(2,1)S(1)} %fusion.1), channel_id=1, source_target_pairs={{4,0},{8,4},{12,8},{16,12},{20,16},{24,20},{28,24},{5,1},{9,5},{13... | collective-permute-start | bytes 811016 | tf_op jit(solution)/shard_map/ppermute | solution.py:30
  6.5 11.9 %collective-permute-start.4 = (bf16[768,256]{1,0:T(8,128)(2,1)S(1)}, bf16[768,256]{1,0:T(8,128)(2,1)S(1)}, u32[]{:S(2)}, u32[]{:S(2)}) collective-permute-start(bf16[768,256]{1,0:T(8,128)(2,1)S(1)} %slice.37), channel_id=1, source_target_pairs={{0,2},{1,3},{2,0},{3,1},{4,6},{5,7},{6,4},{7,5},{8,10},{9,11},{10,... | collective-permute-start | bytes 1179656 | tf_op jit(solution)/shard_map/ppermute | solution.py:25
  11.4 10.7 %collective-permute-start.12 = (bf16[512,256]{1,0:T(8,128)(2,1)S(1)}, bf16[512,256]{1,0:T(8,128)(2,1)S(1)}, u32[]{:S(2)}, u32[]{:S(2)}) collective-permute-start(bf16[512,256]{1,0:T(8,128)(2,1)S(1)} %pad_maximum_fusion), channel_id=1, source_target_pairs={{4,0},{8,4},{12,8},{16,12},{20,16},{24,20},{28,24},{5,1},{9,5},{13... | collective-permute-start | bytes 786440 | tf_op jit(solution)/shard_map/ppermute | solution.py:30
  13.5 6.3 %collective-permute-start.6 = (bf16[256,256]{1,0:T(8,128)(2,1)S(1)}, bf16[256,256]{1,0:T(8,128)(2,1)S(1)}, u32[]{:S(2)}, u32[]{:S(2)}) collective-permute-start(bf16[256,256]{1,0:T(8,128)(2,1)S(1)} %get-tuple-element.36), channel_id=1, source_target_pairs={{0,1},{1,0},{2,3},{3,2},{4,5},{5,4},{6,7},{7,6},{8,9},{9,8},{10,11... | collective-permute-start | bytes 393224 | tf_op jit(solution)/shard_map/ppermute | solution.py:25
  15.0 6.1 %collective-permute-start.5 = (bf16[256,256]{1,0:T(8,128)(2,1)S(1)}, bf16[256,256]{1,0:T(8,128)(2,1)S(1)}, u32[]{:S(2)}, u32[]{:S(2)}) collective-permute-start(bf16[256,256]{1,0:T(8,128)(2,1)S(1)} %slice.43), channel_id=1, source_target_pairs={{0,2},{1,3},{2,0},{3,1},{4,6},{5,7},{6,4},{7,5},{8,10},{9,11},{10,... | collective-permute-start | bytes 393224 | tf_op jit(solution)/shard_map/ppermute | solution.py:25
  16.3 7.0 %collective-permute-start.2 = (bf16[528,256]{1,0:T(8,128)(2,1)S(1)}, bf16[528,256]{1,0:T(8,128)(2,1)S(1)}, u32[]{:S(2)}, u32[]{:S(2)}) collective-permute-start(bf16[528,256]{1,0:T(8,128)(2,1)S(1)} %collective-permute-done.1.near_ref), channel_id=1, source_target_pairs={{0,1},{1,0},{2,3},{3,2},{4,5},{5,4},{6,7},{7,6},{8,9},{9,8},{10,11... | collective-permute-start | bytes 811016 | tf_op jit(solution)/shard_map/ppermute | solution.py:25
  18.4 4.5 %collective-permute-start.7 = (bf16[256,256]{1,0:T(8,128)(2,1)S(1)}, bf16[256,256]{1,0:T(8,128)(2,1)S(1)}, u32[]{:S(2)}, u32[]{:S(2)}) collective-permute-start(bf16[256,256]{1,0:T(8,128)(2,1)S(1)} %slice.45), channel_id=1, source_target_pairs={{0,1},{1,0},{2,3},{3,2},{4,5},{5,4},{6,7},{7,6},{8,9},{9,8},{10,11... | collective-permute-start | bytes 393224 | tf_op jit(solution)/shard_map/ppermute | solution.py:25
  19.8 3.6 %collective-permute-start.8 = (bf16[512,256]{1,0:T(8,128)(2,1)S(1)}, bf16[512,256]{1,0:T(8,128)(2,1)S(1)}, u32[]{:S(2)}, u32[]{:S(2)}) collective-permute-start(bf16[512,256]{1,0:T(8,128)(2,1)S(1)} %slice.46), channel_id=1, source_target_pairs={{0,1},{1,0},{2,3},{3,2},{4,5},{5,4},{6,7},{7,6},{8,9},{9,8},{10,11... | collective-permute-start | bytes 786440 | tf_op jit(solution)/shard_map/ppermute | solution.py:25
  21.2 1.9 %collective-permute-start.9 = (bf16[256,256]{1,0:T(8,128)(2,1)S(1)}, bf16[256,256]{1,0:T(8,128)(2,1)S(1)}, u32[]{:S(2)}, u32[]{:S(2)}) collective-permute-start(bf16[256,256]{1,0:T(8,128)(2,1)S(1)} %collective-permute-done.5.refs_2_.refs_5_), channel_id=1, source_target_pairs={{0,1},{1,0},{2,3},{3,2},{4,5},{5,4},{6,7},{7,6},{8,9},{9,8},{10,11... | collective-permute-start | bytes 393224 | tf_op jit(solution)/shard_map/ppermute | solution.py:25
  22.0 2.5 %collective-permute-start.13 = (bf16[512,256]{1,0:T(8,128)(2,1)S(1)}, bf16[512,256]{1,0:T(8,128)(2,1)S(1)}, u32[]{:S(2)}, u32[]{:S(2)}) collective-permute-start(bf16[512,256]{1,0:T(8,128)(2,1)S(1)} %collective-permute-done.12.refs_4_), channel_id=1, source_target_pairs={{0,1},{1,0},{2,3},{3,2},{4,5},{5,4},{6,7},{7,6},{8,9},{9,8},{10,11... | collective-permute-start | bytes 786440 | tf_op jit(solution)/shard_map/ppermute | solution.py:25
  22.9 1.6 %collective-permute-start.10 = (bf16[256,256]{1,0:T(8,128)(2,1)S(1)}, bf16[256,256]{1,0:T(8,128)(2,1)S(1)}, u32[]{:S(2)}, u32[]{:S(2)}) collective-permute-start(bf16[256,256]{1,0:T(8,128)(2,1)S(1)} %get-tuple-element.33.refs_0_.seed_ref), channel_id=1, source_target_pairs={{0,1},{1,0},{2,3},{3,2},{4,5},{5,4},{6,7},{7,6},{8,9},{9,8},{10,11... | collective-permute-start | bytes 393224 | tf_op jit(solution)/shard_map/ppermute | solution.py:25
  23.0 1.5 %collective-permute-start.14 = (bf16[256,256]{1,0:T(8,128)(2,1)S(1)}, bf16[256,256]{1,0:T(8,128)(2,1)S(1)}, u32[]{:S(2)}, u32[]{:S(2)}) collective-permute-start(bf16[256,256]{1,0:T(8,128)(2,1)S(1)} %get-tuple-element.32.refs_11_), channel_id=1, source_target_pairs={{0,1},{1,0},{2,3},{3,2},{4,5},{5,4},{6,7},{7,6},{8,9},{9,8},{10,11... | collective-permute-start | bytes 393224 | tf_op jit(solution)/shard_map/ppermute | solution.py:25
  25.6 7.6 %collective-permute-start.17 = (bf16[256,256]{1,0:T(8,128)(2,1)S(1)}, bf16[256,256]{1,0:T(8,128)(2,1)S(1)}, u32[]{:S(2)}, u32[]{:S(2)}) collective-permute-start(bf16[256,256]{1,0:T(8,128)(2,1)S(1)} %get-tuple-element.23.refs_2_), channel_id=1, source_target_pairs={{4,0},{8,4},{12,8},{16,12},{20,16},{24,20},{28,24},{5,1},{9,5},{13... | collective-permute-start | bytes 393224 | tf_op jit(solution)/shard_map/ppermute | solution.py:30
  30.1 4.2 %collective-permute-start.15 = (bf16[256,256]{1,0:T(8,128)(2,1)S(1)}, bf16[256,256]{1,0:T(8,128)(2,1)S(1)}, u32[]{:S(2)}, u32[]{:S(2)}) collective-permute-start(bf16[256,256]{1,0:T(8,128)(2,1)S(1)} %get-tuple-element.23.refs_2_), channel_id=1, source_target_pairs={{0,1},{1,0},{2,3},{3,2},{4,5},{5,4},{6,7},{7,6},{8,9},{9,8},{10,11... | collective-permute-start | bytes 393224 | tf_op jit(solution)/shard_map/ppermute | solution.py:25
  31.7 2.6 %collective-permute-start.16 = (bf16[256,256]{1,0:T(8,128)(2,1)S(1)}, bf16[256,256]{1,0:T(8,128)(2,1)S(1)}, u32[]{:S(2)}, u32[]{:S(2)}) collective-permute-start(bf16[256,256]{1,0:T(8,128)(2,1)S(1)} %get-tuple-element.30.refs_3_), channel_id=1, source_target_pairs={{0,1},{1,0},{2,3},{3,2},{4,5},{5,4},{6,7},{7,6},{8,9},{9,8},{10,11... | collective-permute-start | bytes 393224 | tf_op jit(solution)/shard_map/ppermute | solution.py:25
  33.2 2.1 %collective-permute-start.18 = (bf16[256,256]{1,0:T(8,128)(2,1)S(1)}, bf16[256,256]{1,0:T(8,128)(2,1)S(1)}, u32[]{:S(2)}, u32[]{:S(2)}) collective-permute-start(bf16[256,256]{1,0:T(8,128)(2,1)S(1)} %collective-permute-done.17.labels_ref), channel_id=1, source_target_pairs={{0,1},{1,0},{2,3},{3,2},{4,5},{5,4},{6,7},{7,6},{8,9},{9,8},{10,11... | collective-permute-start | bytes 393224 | tf_op jit(solution)/shard_map/ppermute | solution.py:25

commit v5 on v4

--- a/solution.py
+++ b/solution.py
@@ -144,7 +144,7 @@
             part_ref[w] - norms + column_terms(rows, [columns(w, q) for q in quarters])
         )
     at = pl.ds(pl.multiple_of((2 * m + core) * TILE, TILE), TILE)
-    rows = [own_ref[at, :], other_ref[at, :]] + rows
+    rows = [own_ref[at, :], other_ref[at, :]]
     norms = norms + row_ref[:, 128:129]
     packed = near_ref[SPILL * TILE:, :].astype(jnp.float32)
     width = packed.shape[1]
@@ -157,8 +157,6 @@
         factor = factor_ref[0:1, w * TILE:(w + 1) * TILE]
         allowed = row_ref[:, 0:1] == jnp.where(factor > 0, cluster, -1.0)
         tiles = [ref[t * TILE:(t + 1) * TILE, :] for ref in (near_ref, near_other_ref)]
-        if t:
-            tiles += [columns(w, q) for q in quarters]
         logit_ref[w] = jnp.where(allowed, column_terms(rows, tiles) - norms, MASKED)
 
 
@@ -187,14 +185,16 @@
     def columns(w, q):
         return piece(windows["x"][q][w])[...]
 
-    late_ref[...] = logit_ref[groups] + column_terms(
-        rows_of(columns, m, quarters), [columns(groups, q) for q in quarters]
-    )
+    rows = rows_of(columns, m, quarters)
+    for t in range(SPILL):
+        late_ref[t] = logit_ref[groups + t] + column_terms(
+            rows, [columns(groups + t, q) for q in quarters]
+        )
 
     def softmax(step, carry):
         at = pl.ds(pl.multiple_of(step * ROWS, ROWS), ROWS)
-        logits = [logit_ref[w, at, :] for w in range(wtiles)]
-        logits[groups] = late_ref[at, :]
+        logits = [logit_ref[w, at, :] for w in range(groups)]
+        logits += [late_ref[t, at, :] for t in range(SPILL)]
         top = jnp.max(functools.reduce(jnp.maximum, logits), axis=1, keepdims=True)
         weights = [
             jnp.exp2(logits[w] - top) * factor_ref[0:1, w * TILE:(w + 1) * TILE]
@@ -275,9 +275,10 @@
 
     head_c = clusters[:head_rows].astype(jnp.bfloat16).reshape(-1, width)
     head_c = jnp.pad(head_c, ((0, 16 - head_c.shape[0]), (0, 0)))
-    near = from_next(jnp.concatenate([embeddings[:head_rows], head_c]))
-
-    own_other = across(embeddings, 1)
+    head = jnp.concatenate([embeddings[:head_rows], head_c])
+    near = from_next(head)
+
+    own_other = across(after(embeddings, head), 1)
     near_other = across(near, 1)
 
     def early_of(m, done=()):
@@ -300,22 +301,43 @@
 
     seeds = masked(seed_mask, prior)
     seeds_far = [masked(k, tile_in(f, 1)) for k, f in zip(mask_far, first_far)]
+    seeds_far = after(seeds_far, first_early)
     head_seeds = seeds
     for m in apart:
         head_seeds = jnp.where(pair == m, seeds_far[m - 1], head_seeds)
     first_on = [bundle(tile_in(first_far[0], 0), head_seeds)]
     first_on += [(tile_in(f, 0),) for f in first_far[1:]]
-    first_on = after(first_on, first_early)
     near_first = [tuple(from_next(b) for b in f) for f in first_on]
 
     near_second = [across(near[TILE:head_rows], 2 * m) for m in apart]
 
+    first_far_other = [across(tile_in(f, 0), 1) for f in first_far]
+    rest_far_other = [(across(f[:TILE], 1), across(f[TILE:], 1)) for f in rest_far]
+    seeds_other = across(after(seeds, first_far_other), 1)
+    seeds_far_other = [across(f, 1) for f in seeds_far]
+
+    own_arrays = []
+    own_windows = [None, None]
+    for m in range(half - 1):
+        at = len(own_arrays)
+        own_arrays += [first_far[m][0], rest_far[m], first_far_other[m], *rest_far_other[m]]
+        own_windows.append([(at, 0)] + [(at + 1, t * TILE) for t in range(groups - 1)])
+        own_windows.append([(at + 2, 0), (at + 3, 0)] + [(at + 4, t * TILE) for t in range(groups - 2)])
+
+    def logits_of(m, early):
+        return pl.pallas_call(
+            functools.partial(logit_kernel, groups, m, own_windows),
+            out_shape=jax.ShapeDtypeStruct((wtiles, TILE, TILE), jnp.float32),
+            in_specs=[vmem] * (7 + len(own_arrays)),
+            out_specs=vmem,
+            compiler_params=params,
+            cost_estimate=little,
+            name=f"logits_{m}",
+        )(*early, embeddings, own_other, near, near_other, *own_arrays)
+
+    first_logits = logits_of(0, first_early)
     near_second_other = [across(f, 1) for f in near_second]
     near_first_other = [tuple(across(b, 1) for b in f) for f in near_first]
-    first_far_other = [across(tile_in(f, 0), 1) for f in first_far]
-    rest_far_other = [(across(f[:TILE], 1), across(f[TILE:], 1)) for f in rest_far]
-    seeds_other = across(seeds, 1)
-    seeds_far_other = [across(f, 1) for f in seeds_far]
 
     arrays = []
 
@@ -352,38 +374,15 @@
     windows["mine"] += place(seeds_in(near_first[0]))
     windows["other"] += place(seeds_in(near_first_other[0]))
 
-    early_arrays = []
-    early_windows = [None, None]
-    for q in range(2, groups):
-        tiles = []
-        for w, (ref, row) in enumerate(windows["x"][q]):
-            if w == groups:
-                tiles.append(None)
-                continue
-            at = [i for i, a in enumerate(early_arrays) if a is arrays[ref]]
-            if not at:
-                early_arrays.append(arrays[ref])
-                at = [len(early_arrays) - 1]
-            tiles.append((at[0], row))
-        early_windows.append(tiles)
-
     def affinity_of(m, done):
         early = early_of(m, done) if m else first_early
-        logits = pl.pallas_call(
-            functools.partial(logit_kernel, groups, m, early_windows),
-            out_shape=jax.ShapeDtypeStruct((wtiles, TILE, TILE), jnp.float32),
-            in_specs=[vmem] * (7 + len(early_arrays)),
-            out_specs=vmem,
-            compiler_params=params,
-            cost_estimate=little,
-            name=f"logits_{m}",
-        )(*early, embeddings, own_other, near, near_other, *early_arrays)
+        logits = logits_of(m, early) if m else first_logits
         return pl.pallas_call(
             functools.partial(affinity_kernel, groups, m, windows),
             out_shape=(jax.ShapeDtypeStruct((wtiles, TILE, TILE), jnp.bfloat16), labels_shape),
             in_specs=[vmem] * (2 + len(arrays)),
             out_specs=(vmem, vmem),
-            scratch_shapes=[pltpu.VMEM((TILE, TILE), jnp.float32)],
+            scratch_shapes=[pltpu.VMEM((SPILL, TILE, TILE), jnp.float32)],
             compiler_params=params,
             cost_estimate=little,
             name=f"affinity_{m}",

time: 36.3 us -> 35.9 us (0.989)
  waiting for transfers between devices: 6.22 us -> 3.9 us
  starting transfers between devices: 19.5 us -> 21.1 us
    ppermute x16, waiting for transfers between devices: 4.82 us -> 2.67 us  [across(): lax.ppermute(block, 'grp', [(i, i ^ distance) for i in range(groups)])]
    ppermute x3, starting transfers between devices: 6.54 us -> 7.67 us  [from_next(): return lax.ppermute(block, 'shard', [(i + 1, i) for i in range(shards - 1)])]
    ppermute x16, starting transfers between devices: 12.9 us -> 13.4 us  [across(): lax.ppermute(block, 'grp', [(i, i ^ distance) for i in range(groups)])]
    pallas_call x2, Pallas kernels: 2.14 us -> 2.58 us  [affinity_of(): pl.pallas_call(functools.partial(affinity_kernel, groups, m, windows), ou...]
    slice x1 -> x2, other arithmetic: 1.18 us -> 1.33 us  [the longest x1 1.23 us: local(): head = jnp.concatenate([embeddings[:head_rows], head_c])]
  transfers between devices with their start and end apart: 19 -> 19, of which waited for: 6 -> 6; matrix products, arithmetic and copies ran while one was open for 6% -> 3% of each run, Pallas kernels for 17% -> 17%
where the time goes in v5:
time: 35.9 us; the launch traced here: 35.6 us
  starting transfers between devices  21.1 us (59%)
  Pallas kernels  8.1 us (23%)
  waiting for transfers between devices  3.9 us (11%)
  other arithmetic  2.19 us (6%)
    ppermute x16, starting transfers between devices, across(): lax.ppermute(block, 'grp', [(i, i ^ distance) for i in range(groups)])  13.4 us
    ppermute x3, starting transfers between devices, from_next(): return lax.ppermute(block, 'shard', [(i + 1, i) for i in range(shards - 1)])  7.67 us
    ppermute x16, waiting for transfers between devices, across(): lax.ppermute(block, 'grp', [(i, i ^ distance) for i in range(groups)])  2.67 us
    pallas_call x2, Pallas kernels, affinity_of(): pl.pallas_call(functools.partial(affinity_kernel, groups, m, windows), ou...  2.58 us
    pallas_call x2, Pallas kernels, early_of(): pl.pallas_call(functools.partial(early_kernel, groups, m), out_shape=(jax...  2.36 us
    pallas_call x2, Pallas kernels, logits_of(): pl.pallas_call(functools.partial(logit_kernel, groups, m, own_windows), o...  1.79 us
    ppermute x3, waiting for transfers between devices, from_next(): return lax.ppermute(block, 'shard', [(i + 1, i) for i in range(shards - 1)])  1.23 us
    slice x1, other arithmetic, local(): head = jnp.concatenate([embeddings[:head_rows], head_c])  1.23 us
  transfers between devices with their start and end apart: 19, of which 6 were waited for; matrix products, arithmetic and copies ran while one was open for 3% of the time, Pallas kernels for 17%

profile of v5, /device:TPU:11, one launch (start us, length us, event | category | flops | bytes accessed | tf_op | source)
XLA Modules:
  0.0 35.6 jit_solution(10193122147064965178)
XLA Ops:
  0.0 0.0 copy-start
  0.0 0.0 copy-start.5
  0.0 0.0 copy-start.1
  0.0 0.0 copy-start.2
  0.0 0.0 copy-start.3
  0.0 1.2 %fusion.2 = (bf16[512,256]{1,0:T(8,128)(2,1)S(1)}, bf16[512,256]{1,0:T(8,128)(2,1)S(1)}) fusion(bf16[1024,256]{1,0:T(8,128)(2,1)} %own_ref.6, bf16[256,256]{1,0:T(8,128)(2,1)} %param.11, pred[512]{0:T(512)(128)(4,1)S(1)} %iota_compare_fusion.1), kind=kLoop, calls=%fused_computation.11 | loop fusion | flops 655360 | bytes 918016 | tf_op jit(solution)/shard_map/slice | solution.py:278
  1.3 0.0 copy-start.4
  1.3 1.3 %collective-permute-start.3 = (bf16[512,256]{1,0:T(8,128)(2,1)S(1)}, bf16[512,256]{1,0:T(8,128)(2,1)S(1)}, u32[]{:S(2)}, u32[]{:S(2)}) collective-permute-start(bf16[512,256]{1,0:T(8,128)(2,1)S(1)} %get-tuple-element.38), channel_id=1, source_target_pairs={{0,2},{1,3},{2,0},{3,1},{4,6},{5,7},{6,4},{7,5},{8,10},{9,11},{10,... | collective-permute-start | bytes 786440 | tf_op jit(solution)/shard_map/ppermute | solution.py:25
  2.6 0.2 collective-permute-start.9
  2.8 0.7 %convert.3 = bf16[1024]{0:T(1024)(128)(2,1)S(1)} convert(s32[1024]{0:T(1024)} %param.7) | non-fusion elementwise | flops 1024 | bytes 6144 | tf_op jit(solution)/shard_map/convert
  3.6 2.2 %collective-permute-start.1 = (bf16[528,256]{1,0:T(8,128)(2,1)S(1)}, bf16[528,256]{1,0:T(8,128)(2,1)S(1)}, u32[]{:S(2)}, u32[]{:S(2)}) collective-permute-start(bf16[528,256]{1,0:T(8,128)(2,1)S(1)} %fusion.1), channel_id=1, source_target_pairs={{4,0},{8,4},{12,8},{16,12},{20,16},{24,20},{28,24},{5,1},{9,5},{13... | collective-permute-start | bytes 811016 | tf_op jit(solution)/shard_map/ppermute | solution.py:30
  5.7 1.6 %collective-permute-start = (bf16[1024,256]{1,0:T(8,128)(2,1)}, bf16[1024,256]{1,0:T(8,128)(2,1)S(1)}, u32[]{:S(2)}, u32[]{:S(2)}) collective-permute-start(bf16[1024,256]{1,0:T(8,128)(2,1)} %own_ref.6), channel_id=1, source_target_pairs={{0,1},{1,0},{2,3},{3,2},{4,5},{5,4},{6,7},{7,6},{8,9},{9,8},{10,11... | collective-permute-start | bytes 1572872 | tf_op jit(solution)/shard_map/ppermute | solution.py:25
  7.3 0.0 copy-done
  7.3 1.3 %collective-permute-start.4 = (bf16[768,256]{1,0:T(8,128)(2,1)S(1)}, bf16[768,256]{1,0:T(8,128)(2,1)S(1)}, u32[]{:S(2)}, u32[]{:S(2)}) collective-permute-start(bf16[768,256]{1,0:T(8,128)(2,1)S(1)} %slice.37), channel_id=1, source_target_pairs={{0,2},{1,3},{2,0},{3,1},{4,6},{5,7},{6,4},{7,5},{8,10},{9,11},{10,... | collective-permute-start | bytes 1179656 | tf_op jit(solution)/shard_map/ppermute | solution.py:25
  8.7 0.0 copy-done.5
  8.7 0.0 collective-permute-done.9
  8.7 0.0 collective-permute-done.3.refs_0_.refs_2_
  8.7 0.1 fusion.3
  8.8 0.3 collective-permute-done.other_ref
  9.1 0.0 copy-done.1
  9.1 0.0 copy-done.2
  9.1 0.0 copy-done.3
  9.1 1.2 %early_0.1 = (f32[4,256,256]{2,1,0:T(8,128)S(1)}, f32[8,1536]{1,0:T(8,128)S(1)}, f32[256,256]{1,0:T(8,128)S(1)}) custom-call(s32[4,4]{1,0:T(4,128)S(1)} %copy-done.2, s32[4]{0:T(128)S(1)} %copy-done.3, s32[1,1024]{1,0:T(1,128)S(1)} %bitcast.1, bf16[1024,256]{1,0:T(8,128)(2,1)S(1)} %copy-done, bf16[1024,256]{1,0:T(8,128)(2,1)S(1)} %collective-permute-done.other_ref), custom_call_target="tpu_custom_call" | custom-call | flops 1 | bytes 1 | tf_op jit(solution)/shard_map/early_0/pallas_call | solution.py:286
  10.3 0.0 copy-done.4
  10.3 0.1 broadcast_select_fusion.1
  10.4 3.0 %collective-permute-start.10 = (bf16[512,256]{1,0:T(8,128)(2,1)S(1)}, bf16[512,256]{1,0:T(8,128)(2,1)S(1)}, u32[]{:S(2)}, u32[]{:S(2)}) collective-permute-start(bf16[512,256]{1,0:T(8,128)(2,1)S(1)} %pad_maximum_fusion), channel_id=1, source_target_pairs={{4,0},{8,4},{12,8},{16,12},{20,16},{24,20},{28,24},{5,1},{9,5},{13... | collective-permute-start | bytes 786440 | tf_op jit(solution)/shard_map/ppermute | solution.py:30
  13.4 0.0 collective-permute-done.1.near_ref
  13.4 1.8 %collective-permute-start.2 = (bf16[528,256]{1,0:T(8,128)(2,1)S(1)}, bf16[528,256]{1,0:T(8,128)(2,1)S(1)}, u32[]{:S(2)}, u32[]{:S(2)}) collective-permute-start(bf16[528,256]{1,0:T(8,128)(2,1)S(1)} %collective-permute-done.1.near_ref), channel_id=1, source_target_pairs={{0,1},{1,0},{2,3},{3,2},{4,5},{5,4},{6,7},{7,6},{8,9},{9,8},{10,11... | collective-permute-start | bytes 811016 | tf_op jit(solution)/shard_map/ppermute | solution.py:25
  15.3 0.0 collective-permute-start.5
  15.3 1.3 %collective-permute-start.11 = (bf16[256,256]{1,0:T(8,128)(2,1)S(1)}, bf16[256,256]{1,0:T(8,128)(2,1)S(1)}, u32[]{:S(2)}, u32[]{:S(2)}) collective-permute-start(bf16[256,256]{1,0:T(8,128)(2,1)S(1)} %slice.47), channel_id=1, source_target_pairs={{0,2},{1,3},{2,0},{3,1},{4,6},{5,7},{6,4},{7,5},{8,10},{9,11},{10,... | collective-permute-start | bytes 393224 | tf_op jit(solution)/shard_map/ppermute | solution.py:25
  16.6 1.6 %collective-permute-done.4.refs_1_.refs_3_ = bf16[768,256]{1,0:T(8,128)(2,1)S(1)} collective-permute-done((bf16[768,256]{1,0:T(8,128)(2,1)S(1)}, bf16[768,256]{1,0:T(8,128)(2,1)S(1)}, u32[]{:S(2)}, u32[]{:S(2)}) %collective-permute-start.4) | collective-permute-done | bytes 393248 | tf_op jit(solution)/shard_map/ppermute | solution.py:25
  18.1 1.3 %collective-permute-start.6 = (bf16[256,256]{1,0:T(8,128)(2,1)S(1)}, bf16[256,256]{1,0:T(8,128)(2,1)S(1)}, u32[]{:S(2)}, u32[]{:S(2)}) collective-permute-start(bf16[256,256]{1,0:T(8,128)(2,1)S(1)} %slice.44), channel_id=1, source_target_pairs={{0,1},{1,0},{2,3},{3,2},{4,5},{5,4},{6,7},{7,6},{8,9},{9,8},{10,11... | collective-permute-start | bytes 393224 | tf_op jit(solution)/shard_map/ppermute | solution.py:25
  19.5 0.0 collective-permute-done.5.refs_2_.refs_6_
  19.5 0.1 collective-permute-start.7
  19.6 0.2 collective-permute-done.10.refs_4_
  19.8 2.1 %collective-permute-start.12 = (bf16[512,256]{1,0:T(8,128)(2,1)S(1)}, bf16[512,256]{1,0:T(8,128)(2,1)S(1)}, u32[]{:S(2)}, u32[]{:S(2)}) collective-permute-start(bf16[512,256]{1,0:T(8,128)(2,1)S(1)} %collective-permute-done.10.refs_4_), channel_id=1, source_target_pairs={{0,1},{1,0},{2,3},{3,2},{4,5},{5,4},{6,7},{7,6},{8,9},{9,8},{10,11... | collective-permute-start | bytes 786440 | tf_op jit(solution)/shard_map/ppermute | solution.py:25
  21.9 0.0 collective-permute-done.11.refs_5_
  21.9 0.0 collective-permute-start.13
  21.9 0.0 collective-permute-done.6.refs_3_.refs_7_
  21.9 0.5 %collective-permute-start.8 = (bf16[256,256]{1,0:T(8,128)(2,1)S(1)}, bf16[256,256]{1,0:T(8,128)(2,1)S(1)}, u32[]{:S(2)}, u32[]{:S(2)}) collective-permute-start(bf16[256,256]{1,0:T(8,128)(2,1)S(1)} %get-tuple-element.24.refs_0_.seed_ref), channel_id=1, source_target_pairs={{0,1},{1,0},{2,3},{3,2},{4,5},{5,4},{6,7},{7,6},{8,9},{9,8},{10,11... | collective-permute-start | bytes 393224 | tf_op jit(solution)/shard_map/ppermute | solution.py:25
  22.5 0.0 collective-permute-done.2.near_other_ref
  22.5 0.1 collective-permute-start.14
  22.5 0.0 collective-permute-done.7.refs_4_.refs_8_
  22.5 0.9 %logits_0.1.logit_ref = f32[6,256,256]{2,1,0:T(8,128)S(1)} custom-call(f32[4,256,256]{2,1,0:T(8,128)S(1)} %get-tuple-element.21.part_ref, f32[8,1536]{1,0:T(8,128)S(1)} %get-tuple-element.22.factor_ref, f32[256,256]{1,0:T(8,128)S(1)} %get-tuple-element.23.row_ref, bf16[1024,256]{1,0:T(8,128)(2,1)S(1)} %copy-done, ...), custom_call_target="tpu_custom_call" | custom-call | flops 1 | bytes 1 | tf_op jit(solution)/shard_map/logits_0/pallas_call | solution.py:328
  23.4 0.0 collective-permute-done.13.refs_10_
  23.4 0.0 collective-permute-done.8.refs_1_
  23.5 0.3 collective-permute-done.14.refs_12_
  23.8 0.0 collective-permute-done.12.refs_9_
  23.8 1.3 %affinity_0.1 = (bf16[6,256,256]{2,1,0:T(8,128)(2,1)S(1)}, bf16[256,256]{1,0:T(8,128)(2,1)S(1)}) custom-call(f32[6,256,256]{2,1,0:T(8,128)S(1)} %logits_0.1.logit_ref, f32[8,1536]{1,0:T(8,128)S(1)} %get-tuple-element.22.factor_ref, bf16[256,256]{1,0:T(8,128)(2,1)S(1)} %get-tuple-element.24.refs_0_.seed_ref, ...), custom_call_target="tpu_custom_call" | custom-call | flops 1 | bytes 1 | tf_op jit(solution)/shard_map/affinity_0/pallas_call | solution.py:380
  25.1 2.5 %collective-permute-start.17 = (bf16[256,256]{1,0:T(8,128)(2,1)S(1)}, bf16[256,256]{1,0:T(8,128)(2,1)S(1)}, u32[]{:S(2)}, u32[]{:S(2)}) collective-permute-start(bf16[256,256]{1,0:T(8,128)(2,1)S(1)} %get-tuple-element.27.refs_2_), channel_id=1, source_target_pairs={{4,0},{8,4},{12,8},{16,12},{20,16},{24,20},{28,24},{5,1},{9,5},{13... | collective-permute-start | bytes 393224 | tf_op jit(solution)/shard_map/ppermute | solution.py:30
  27.6 1.2 %early_1.1 = (f32[4,256,256]{2,1,0:T(8,128)S(1)}, f32[8,1536]{1,0:T(8,128)S(1)}, f32[256,256]{1,0:T(8,128)S(1)}) custom-call(s32[4,4]{1,0:T(4,128)S(1)} %copy-done.2, s32[4]{0:T(128)S(1)} %copy-done.3, s32[1,1024]{1,0:T(1,128)S(1)} %bitcast.2, bf16[1024,256]{1,0:T(8,128)(2,1)S(1)} %copy-done, bf16[1024,256]{1,0:T(8,128)(2,1)S(1)} %collective-permute-done.other_ref), custom_call_target="tpu_custom_call" | custom-call | flops 1 | bytes 1 | tf_op jit(solution)/shard_map/early_1/pallas_call | solution.py:286
  28.8 0.9 %logits_1.1.logit_ref = f32[6,256,256]{2,1,0:T(8,128)S(1)} custom-call(f32[4,256,256]{2,1,0:T(8,128)S(1)} %get-tuple-element.30.part_ref, f32[8,1536]{1,0:T(8,128)S(1)} %get-tuple-element.31.factor_ref, f32[256,256]{1,0:T(8,128)S(1)} %get-tuple-element.32.row_ref, bf16[1024,256]{1,0:T(8,128)(2,1)S(1)} %copy-done, ...), custom_call_target="tpu_custom_call" | custom-call | flops 1 | bytes 1 | tf_op jit(solution)/shard_map/logits_1/pallas_call | solution.py:328
  29.7 0.7 %collective-permute-start.15 = (bf16[256,256]{1,0:T(8,128)(2,1)S(1)}, bf16[256,256]{1,0:T(8,128)(2,1)S(1)}, u32[]{:S(2)}, u32[]{:S(2)}) collective-permute-start(bf16[256,256]{1,0:T(8,128)(2,1)S(1)} %get-tuple-element.27.refs_2_), channel_id=1, source_target_pairs={{0,1},{1,0},{2,3},{3,2},{4,5},{5,4},{6,7},{7,6},{8,9},{9,8},{10,11... | collective-permute-start | bytes 393224 | tf_op jit(solution)/shard_map/ppermute | solution.py:25
  30.4 1.3 %affinity_1.1 = (bf16[6,256,256]{2,1,0:T(8,128)(2,1)S(1)}, bf16[256,256]{1,0:T(8,128)(2,1)S(1)}) custom-call(f32[6,256,256]{2,1,0:T(8,128)S(1)} %logits_1.1.logit_ref, f32[8,1536]{1,0:T(8,128)S(1)} %get-tuple-element.31.factor_ref, bf16[256,256]{1,0:T(8,128)(2,1)S(1)} %get-tuple-element.24.refs_0_.seed_ref, ...), custom_call_target="tpu_custom_call" | custom-call | flops 1 | bytes 1 | tf_op jit(solution)/shard_map/affinity_1/pallas_call | solution.py:380
  31.7 0.1 collective-permute-start.16
  31.8 1.0 %collective-permute-done.17.labels_ref = bf16[256,256]{1,0:T(8,128)(2,1)S(1)} collective-permute-done((bf16[256,256]{1,0:T(8,128)(2,1)S(1)}, bf16[256,256]{1,0:T(8,128)(2,1)S(1)}, u32[]{:S(2)}, u32[]{:S(2)}) %collective-permute-start.17) | collective-permute-done | bytes 131104 | tf_op jit(solution)/shard_map/ppermute | solution.py:30
  32.8 1.0 %collective-permute-start.18 = (bf16[256,256]{1,0:T(8,128)(2,1)S(1)}, bf16[256,256]{1,0:T(8,128)(2,1)S(1)}, u32[]{:S(2)}, u32[]{:S(2)}) collective-permute-start(bf16[256,256]{1,0:T(8,128)(2,1)S(1)} %collective-permute-done.17.labels_ref), channel_id=1, source_target_pairs={{0,1},{1,0},{2,3},{3,2},{4,5},{5,4},{6,7},{7,6},{8,9},{9,8},{10,11... | collective-permute-start | bytes 393224 | tf_op jit(solution)/shard_map/ppermute | solution.py:25
  33.8 0.0 collective-permute-done.15.refs_4_
  33.8 0.0 collective-permute-done.16.refs_5_
  33.8 0.3 spread_own.1.total_ref
  34.1 0.2 spread_near_0.1.total_ref
  34.3 0.5 %collective-permute-done.18.labels_ref = bf16[256,256]{1,0:T(8,128)(2,1)S(1)} collective-permute-done((bf16[256,256]{1,0:T(8,128)(2,1)S(1)}, bf16[256,256]{1,0:T(8,128)(2,1)S(1)}, u32[]{:S(2)}, u32[]{:S(2)}) %collective-permute-start.18) | collective-permute-done | bytes 131104 | tf_op jit(solution)/shard_map/ppermute | solution.py:25
  34.8 0.8 %spread_near_1.1 = bf16[256,256]{1,0:T(8,128)(2,1)} custom-call(f32[256,256]{1,0:T(8,128)S(1)} %spread_near_0.1.total_ref, bf16[256,256]{1,0:T(8,128)(2,1)S(1)} %collective-permute-done.18.labels_ref, bf16[6,256,256]{2,1,0:T(8,128)(2,1)S(1)} %get-tuple-element.26.refs_0_, bf16[6,256,256]{2,1,0:T(8,128)(2,1)S(1)} %get-tuple-element.33.refs_1_), custom_call_target="tpu_custom_call" | custom-call | flops 1 | bytes 1 | tf_op jit(solution)/shard_map/spread_near_1/pallas_call | solution.py:409
  (11 shorter events, 0.1 us)
Async XLA Ops:
  0.0 7.3 %copy-start = (bf16[1024,256]{1,0:T(8,128)(2,1)S(1)}, bf16[1024,256]{1,0:T(8,128)(2,1)}, u32[]{:S(2)}) copy-start(bf16[1024,256]{1,0:T(8,128)(2,1)} %own_ref.6) | copy-start | bytes 1572868
  0.0 8.7 %copy-start.5 = (s32[256]{0:T(256)S(1)}, s32[256]{0:T(256)}, u32[]{:S(2)}) copy-start(s32[256]{0:T(256)} %param.10) | copy-start | bytes 3076
  0.0 9.1 %copy-start.1 = (s32[1024]{0:T(1024)S(1)}, s32[1024]{0:T(1024)}, u32[]{:S(2)}) copy-start(s32[1024]{0:T(1024)} %param.7) | copy-start | bytes 12292
  0.0 9.1 %copy-start.2 = (s32[4,4]{1,0:T(4,128)S(1)}, s32[4,4]{1,0:T(4,128)}, u32[]{:S(2)}) copy-start(s32[4,4]{1,0:T(4,128)} %blocks_ref.3) | copy-start | bytes 196
  0.0 9.1 %copy-start.3 = (s32[4]{0:T(128)S(1)}, s32[4]{0:T(128)}, u32[]{:S(2)}) copy-start(s32[4]{0:T(128)} %counts_ref.3) | copy-start | bytes 52
  1.3 9.0 %copy-start.4 = (bf16[256,256]{1,0:T(8,128)(2,1)S(1)}, bf16[256,256]{1,0:T(8,128)(2,1)}, u32[]{:S(2)}) copy-start(bf16[256,256]{1,0:T(8,128)(2,1)} %param.11) | copy-start | bytes 393220
  1.3 7.4 %collective-permute-start.3 = (bf16[512,256]{1,0:T(8,128)(2,1)S(1)}, bf16[512,256]{1,0:T(8,128)(2,1)S(1)}, u32[]{:S(2)}, u32[]{:S(2)}) collective-permute-start(bf16[512,256]{1,0:T(8,128)(2,1)S(1)} %get-tuple-element.38), channel_id=1, source_target_pairs={{0,2},{1,3},{2,0},{3,1},{4,6},{5,7},{6,4},{7,5},{8,10},{9,11},{10,... | collective-permute-start | bytes 786440 | tf_op jit(solution)/shard_map/ppermute | solution.py:25
  2.6 6.1 %collective-permute-start.9 = (s32[256]{0:T(256)}, s32[256]{0:T(256)S(1)}, u32[]{:S(2)}, u32[]{:S(2)}) collective-permute-start(s32[256]{0:T(256)} %param.10), channel_id=1, source_target_pairs={{0,2},{1,3},{2,0},{3,1},{4,6},{5,7},{6,4},{7,5},{8,10},{9,11},{10,... | collective-permute-start | bytes 3080 | tf_op jit(solution)/shard_map/ppermute | solution.py:25
  3.6 9.9 %collective-permute-start.1 = (bf16[528,256]{1,0:T(8,128)(2,1)S(1)}, bf16[528,256]{1,0:T(8,128)(2,1)S(1)}, u32[]{:S(2)}, u32[]{:S(2)}) collective-permute-start(bf16[528,256]{1,0:T(8,128)(2,1)S(1)} %fusion.1), channel_id=1, source_target_pairs={{4,0},{8,4},{12,8},{16,12},{20,16},{24,20},{28,24},{5,1},{9,5},{13... | collective-permute-start | bytes 811016 | tf_op jit(solution)/shard_map/ppermute | solution.py:30
  5.7 3.3 %collective-permute-start = (bf16[1024,256]{1,0:T(8,128)(2,1)}, bf16[1024,256]{1,0:T(8,128)(2,1)S(1)}, u32[]{:S(2)}, u32[]{:S(2)}) collective-permute-start(bf16[1024,256]{1,0:T(8,128)(2,1)} %own_ref.6), channel_id=1, source_target_pairs={{0,1},{1,0},{2,3},{3,2},{4,5},{5,4},{6,7},{7,6},{8,9},{9,8},{10,11... | collective-permute-start | bytes 1572872 | tf_op jit(solution)/shard_map/ppermute | solution.py:25
  7.3 10.8 %collective-permute-start.4 = (bf16[768,256]{1,0:T(8,128)(2,1)S(1)}, bf16[768,256]{1,0:T(8,128)(2,1)S(1)}, u32[]{:S(2)}, u32[]{:S(2)}) collective-permute-start(bf16[768,256]{1,0:T(8,128)(2,1)S(1)} %slice.37), channel_id=1, source_target_pairs={{0,2},{1,3},{2,0},{3,1},{4,6},{5,7},{6,4},{7,5},{8,10},{9,11},{10,... | collective-permute-start | bytes 1179656 | tf_op jit(solution)/shard_map/ppermute | solution.py:25
  10.4 9.4 %collective-permute-start.10 = (bf16[512,256]{1,0:T(8,128)(2,1)S(1)}, bf16[512,256]{1,0:T(8,128)(2,1)S(1)}, u32[]{:S(2)}, u32[]{:S(2)}) collective-permute-start(bf16[512,256]{1,0:T(8,128)(2,1)S(1)} %pad_maximum_fusion), channel_id=1, source_target_pairs={{4,0},{8,4},{12,8},{16,12},{20,16},{24,20},{28,24},{5,1},{9,5},{13... | collective-permute-start | bytes 786440 | tf_op jit(solution)/shard_map/ppermute | solution.py:30
  13.4 9.0 %collective-permute-start.2 = (bf16[528,256]{1,0:T(8,128)(2,1)S(1)}, bf16[528,256]{1,0:T(8,128)(2,1)S(1)}, u32[]{:S(2)}, u32[]{:S(2)}) collective-permute-start(bf16[528,256]{1,0:T(8,128)(2,1)S(1)} %collective-permute-done.1.near_ref), channel_id=1, source_target_pairs={{0,1},{1,0},{2,3},{3,2},{4,5},{5,4},{6,7},{7,6},{8,9},{9,8},{10,11... | collective-permute-start | bytes 811016 | tf_op jit(solution)/shard_map/ppermute | solution.py:25
  15.3 4.2 %collective-permute-start.5 = (bf16[256,256]{1,0:T(8,128)(2,1)S(1)}, bf16[256,256]{1,0:T(8,128)(2,1)S(1)}, u32[]{:S(2)}, u32[]{:S(2)}) collective-permute-start(bf16[256,256]{1,0:T(8,128)(2,1)S(1)} %get-tuple-element.39), channel_id=1, source_target_pairs={{0,1},{1,0},{2,3},{3,2},{4,5},{5,4},{6,7},{7,6},{8,9},{9,8},{10,11... | collective-permute-start | bytes 393224 | tf_op jit(solution)/shard_map/ppermute | solution.py:25
  15.3 6.7 %collective-permute-start.11 = (bf16[256,256]{1,0:T(8,128)(2,1)S(1)}, bf16[256,256]{1,0:T(8,128)(2,1)S(1)}, u32[]{:S(2)}, u32[]{:S(2)}) collective-permute-start(bf16[256,256]{1,0:T(8,128)(2,1)S(1)} %slice.47), channel_id=1, source_target_pairs={{0,2},{1,3},{2,0},{3,1},{4,6},{5,7},{6,4},{7,5},{8,10},{9,11},{10,... | collective-permute-start | bytes 393224 | tf_op jit(solution)/shard_map/ppermute | solution.py:25
  18.1 3.8 %collective-permute-start.6 = (bf16[256,256]{1,0:T(8,128)(2,1)S(1)}, bf16[256,256]{1,0:T(8,128)(2,1)S(1)}, u32[]{:S(2)}, u32[]{:S(2)}) collective-permute-start(bf16[256,256]{1,0:T(8,128)(2,1)S(1)} %slice.44), channel_id=1, source_target_pairs={{0,1},{1,0},{2,3},{3,2},{4,5},{5,4},{6,7},{7,6},{8,9},{9,8},{10,11... | collective-permute-start | bytes 393224 | tf_op jit(solution)/shard_map/ppermute | solution.py:25
  19.5 3.1 %collective-permute-start.7 = (bf16[512,256]{1,0:T(8,128)(2,1)S(1)}, bf16[512,256]{1,0:T(8,128)(2,1)S(1)}, u32[]{:S(2)}, u32[]{:S(2)}) collective-permute-start(bf16[512,256]{1,0:T(8,128)(2,1)S(1)} %slice.45), channel_id=1, source_target_pairs={{0,1},{1,0},{2,3},{3,2},{4,5},{5,4},{6,7},{7,6},{8,9},{9,8},{10,11... | collective-permute-start | bytes 786440 | tf_op jit(solution)/shard_map/ppermute | solution.py:25
  19.8 4.0 %collective-permute-start.12 = (bf16[512,256]{1,0:T(8,128)(2,1)S(1)}, bf16[512,256]{1,0:T(8,128)(2,1)S(1)}, u32[]{:S(2)}, u32[]{:S(2)}) collective-permute-start(bf16[512,256]{1,0:T(8,128)(2,1)S(1)} %collective-permute-done.10.refs_4_), channel_id=1, source_target_pairs={{0,1},{1,0},{2,3},{3,2},{4,5},{5,4},{6,7},{7,6},{8,9},{9,8},{10,11... | collective-permute-start | bytes 786440 | tf_op jit(solution)/shard_map/ppermute | solution.py:25
  21.9 1.5 %collective-permute-start.13 = (bf16[256,256]{1,0:T(8,128)(2,1)S(1)}, bf16[256,256]{1,0:T(8,128)(2,1)S(1)}, u32[]{:S(2)}, u32[]{:S(2)}) collective-permute-start(bf16[256,256]{1,0:T(8,128)(2,1)S(1)} %collective-permute-done.11.refs_5_), channel_id=1, source_target_pairs={{0,1},{1,0},{2,3},{3,2},{4,5},{5,4},{6,7},{7,6},{8,9},{9,8},{10,11... | collective-permute-start | bytes 393224 | tf_op jit(solution)/shard_map/ppermute | solution.py:25
  21.9 1.5 %collective-permute-start.8 = (bf16[256,256]{1,0:T(8,128)(2,1)S(1)}, bf16[256,256]{1,0:T(8,128)(2,1)S(1)}, u32[]{:S(2)}, u32[]{:S(2)}) collective-permute-start(bf16[256,256]{1,0:T(8,128)(2,1)S(1)} %get-tuple-element.24.refs_0_.seed_ref), channel_id=1, source_target_pairs={{0,1},{1,0},{2,3},{3,2},{4,5},{5,4},{6,7},{7,6},{8,9},{9,8},{10,11... | collective-permute-start | bytes 393224 | tf_op jit(solution)/shard_map/ppermute | solution.py:25
  22.5 1.3 %collective-permute-start.14 = (bf16[256,256]{1,0:T(8,128)(2,1)S(1)}, bf16[256,256]{1,0:T(8,128)(2,1)S(1)}, u32[]{:S(2)}, u32[]{:S(2)}) collective-permute-start(bf16[256,256]{1,0:T(8,128)(2,1)S(1)} %get-tuple-element.25.refs_11_), channel_id=1, source_target_pairs={{0,1},{1,0},{2,3},{3,2},{4,5},{5,4},{6,7},{7,6},{8,9},{9,8},{10,11... | collective-permute-start | bytes 393224 | tf_op jit(solution)/shard_map/ppermute | solution.py:25
  25.1 7.7 %collective-permute-start.17 = (bf16[256,256]{1,0:T(8,128)(2,1)S(1)}, bf16[256,256]{1,0:T(8,128)(2,1)S(1)}, u32[]{:S(2)}, u32[]{:S(2)}) collective-permute-start(bf16[256,256]{1,0:T(8,128)(2,1)S(1)} %get-tuple-element.27.refs_2_), channel_id=1, source_target_pairs={{4,0},{8,4},{12,8},{16,12},{20,16},{24,20},{28,24},{5,1},{9,5},{13... | collective-permute-start | bytes 393224 | tf_op jit(solution)/shard_map/ppermute | solution.py:30
  29.7 4.1 %collective-permute-start.15 = (bf16[256,256]{1,0:T(8,128)(2,1)S(1)}, bf16[256,256]{1,0:T(8,128)(2,1)S(1)}, u32[]{:S(2)}, u32[]{:S(2)}) collective-permute-start(bf16[256,256]{1,0:T(8,128)(2,1)S(1)} %get-tuple-element.27.refs_2_), channel_id=1, source_target_pairs={{0,1},{1,0},{2,3},{3,2},{4,5},{5,4},{6,7},{7,6},{8,9},{9,8},{10,11... | collective-permute-start | bytes 393224 | tf_op jit(solution)/shard_map/ppermute | solution.py:25
  31.7 2.1 %collective-permute-start.16 = (bf16[256,256]{1,0:T(8,128)(2,1)S(1)}, bf16[256,256]{1,0:T(8,128)(2,1)S(1)}, u32[]{:S(2)}, u32[]{:S(2)}) collective-permute-start(bf16[256,256]{1,0:T(8,128)(2,1)S(1)} %get-tuple-element.34.refs_3_), channel_id=1, source_target_pairs={{0,1},{1,0},{2,3},{3,2},{4,5},{5,4},{6,7},{7,6},{8,9},{9,8},{10,11... | collective-permute-start | bytes 393224 | tf_op jit(solution)/shard_map/ppermute | solution.py:25
  32.8 2.0 %collective-permute-start.18 = (bf16[256,256]{1,0:T(8,128)(2,1)S(1)}, bf16[256,256]{1,0:T(8,128)(2,1)S(1)}, u32[]{:S(2)}, u32[]{:S(2)}) collective-permute-start(bf16[256,256]{1,0:T(8,128)(2,1)S(1)} %collective-permute-done.17.labels_ref), channel_id=1, source_target_pairs={{0,1},{1,0},{2,3},{3,2},{4,5},{5,4},{6,7},{7,6},{8,9},{9,8},{10,11... | collective-permute-start | bytes 393224 | tf_op jit(solution)/shard_map/ppermute | solution.py:25

commit v6 on v5

--- a/solution.py
+++ b/solution.py
@@ -313,7 +313,7 @@
 
     first_far_other = [across(tile_in(f, 0), 1) for f in first_far]
     rest_far_other = [(across(f[:TILE], 1), across(f[TILE:], 1)) for f in rest_far]
-    seeds_other = across(after(seeds, first_far_other), 1)
+    seeds_other = across(seeds, 1)
     seeds_far_other = [across(f, 1) for f in seeds_far]
 
     own_arrays = []

time: 35.9 us -> 35.9 us (level)
  no operation moved by 1% of the time
where the time goes in v6:
time: 35.9 us; the launch traced here: 35.6 us
  starting transfers between devices  21.1 us (59%)
  Pallas kernels  8.1 us (23%)
  waiting for transfers between devices  3.9 us (11%)
  other arithmetic  2.19 us (6%)
    ppermute x16, starting transfers between devices, across(): lax.ppermute(block, 'grp', [(i, i ^ distance) for i in range(groups)])  13.4 us
    ppermute x3, starting transfers between devices, from_next(): return lax.ppermute(block, 'shard', [(i + 1, i) for i in range(shards - 1)])  7.67 us
    ppermute x16, waiting for transfers between devices, across(): lax.ppermute(block, 'grp', [(i, i ^ distance) for i in range(groups)])  2.67 us
    pallas_call x2, Pallas kernels, affinity_of(): pl.pallas_call(functools.partial(affinity_kernel, groups, m, windows), ou...  2.58 us
    pallas_call x2, Pallas kernels, early_of(): pl.pallas_call(functools.partial(early_kernel, groups, m), out_shape=(jax...  2.36 us
    pallas_call x2, Pallas kernels, logits_of(): pl.pallas_call(functools.partial(logit_kernel, groups, m, own_windows), o...  1.79 us
    ppermute x3, waiting for transfers between devices, from_next(): return lax.ppermute(block, 'shard', [(i + 1, i) for i in range(shards - 1)])  1.23 us
    slice x1, other arithmetic, local(): head = jnp.concatenate([embeddings[:head_rows], head_c])  1.23 us
  transfers between devices with their start and end apart: 19, of which 6 were waited for; matrix products, arithmetic and copies ran while one was open for 3% of the time, Pallas kernels for 17%

profile of v6, /device:TPU:11, one launch (start us, length us, event | category | flops | bytes accessed | tf_op | source)
XLA Modules:
  0.0 35.6 jit_solution(10193122147064965178)
XLA Ops:
  0.0 0.0 copy-start
  0.0 0.0 copy-start.5
  0.0 0.0 copy-start.1
  0.0 0.0 copy-start.2
  0.0 0.0 copy-start.3
  0.0 1.2 %fusion.2 = (bf16[512,256]{1,0:T(8,128)(2,1)S(1)}, bf16[512,256]{1,0:T(8,128)(2,1)S(1)}) fusion(bf16[1024,256]{1,0:T(8,128)(2,1)} %own_ref.6, bf16[256,256]{1,0:T(8,128)(2,1)} %param.11, pred[512]{0:T(512)(128)(4,1)S(1)} %iota_compare_fusion.1), kind=kLoop, calls=%fused_computation.11 | loop fusion | flops 655360 | bytes 918016 | tf_op jit(solution)/shard_map/slice | solution.py:278
  1.3 0.0 copy-start.4
  1.3 1.3 %collective-permute-start.3 = (bf16[512,256]{1,0:T(8,128)(2,1)S(1)}, bf16[512,256]{1,0:T(8,128)(2,1)S(1)}, u32[]{:S(2)}, u32[]{:S(2)}) collective-permute-start(bf16[512,256]{1,0:T(8,128)(2,1)S(1)} %get-tuple-element.36), channel_id=1, source_target_pairs={{0,2},{1,3},{2,0},{3,1},{4,6},{5,7},{6,4},{7,5},{8,10},{9,11},{10,... | collective-permute-start | bytes 786440 | tf_op jit(solution)/shard_map/ppermute | solution.py:25
  2.6 0.2 collective-permute-start.9
  2.8 0.7 %convert.3 = bf16[1024]{0:T(1024)(128)(2,1)S(1)} convert(s32[1024]{0:T(1024)} %param.7) | non-fusion elementwise | flops 1024 | bytes 6144 | tf_op jit(solution)/shard_map/convert
  3.6 2.2 %collective-permute-start.1 = (bf16[528,256]{1,0:T(8,128)(2,1)S(1)}, bf16[528,256]{1,0:T(8,128)(2,1)S(1)}, u32[]{:S(2)}, u32[]{:S(2)}) collective-permute-start(bf16[528,256]{1,0:T(8,128)(2,1)S(1)} %fusion.1), channel_id=1, source_target_pairs={{4,0},{8,4},{12,8},{16,12},{20,16},{24,20},{28,24},{5,1},{9,5},{13... | collective-permute-start | bytes 811016 | tf_op jit(solution)/shard_map/ppermute | solution.py:30
  5.7 1.6 %collective-permute-start = (bf16[1024,256]{1,0:T(8,128)(2,1)}, bf16[1024,256]{1,0:T(8,128)(2,1)S(1)}, u32[]{:S(2)}, u32[]{:S(2)}) collective-permute-start(bf16[1024,256]{1,0:T(8,128)(2,1)} %own_ref.6), channel_id=1, source_target_pairs={{0,1},{1,0},{2,3},{3,2},{4,5},{5,4},{6,7},{7,6},{8,9},{9,8},{10,11... | collective-permute-start | bytes 1572872 | tf_op jit(solution)/shard_map/ppermute | solution.py:25
  7.3 0.0 copy-done
  7.3 1.3 %collective-permute-start.4 = (bf16[768,256]{1,0:T(8,128)(2,1)S(1)}, bf16[768,256]{1,0:T(8,128)(2,1)S(1)}, u32[]{:S(2)}, u32[]{:S(2)}) collective-permute-start(bf16[768,256]{1,0:T(8,128)(2,1)S(1)} %slice.37), channel_id=1, source_target_pairs={{0,2},{1,3},{2,0},{3,1},{4,6},{5,7},{6,4},{7,5},{8,10},{9,11},{10,... | collective-permute-start | bytes 1179656 | tf_op jit(solution)/shard_map/ppermute | solution.py:25
  8.7 0.0 copy-done.5
  8.7 0.0 collective-permute-done.9
  8.7 0.0 collective-permute-done.3.refs_0_.refs_2_
  8.7 0.1 fusion.3
  8.8 0.3 collective-permute-done.other_ref
  9.1 0.0 copy-done.1
  9.1 0.0 copy-done.2
  9.1 0.0 copy-done.3
  9.1 1.2 %early_0.1 = (f32[4,256,256]{2,1,0:T(8,128)S(1)}, f32[8,1536]{1,0:T(8,128)S(1)}, f32[256,256]{1,0:T(8,128)S(1)}) custom-call(s32[4,4]{1,0:T(4,128)S(1)} %copy-done.2, s32[4]{0:T(128)S(1)} %copy-done.3, s32[1,1024]{1,0:T(1,128)S(1)} %bitcast.1, bf16[1024,256]{1,0:T(8,128)(2,1)S(1)} %copy-done, bf16[1024,256]{1,0:T(8,128)(2,1)S(1)} %collective-permute-done.other_ref), custom_call_target="tpu_custom_call" | custom-call | flops 1 | bytes 1 | tf_op jit(solution)/shard_map/early_0/pallas_call | solution.py:286
  10.3 0.0 copy-done.4
  10.3 0.1 broadcast_select_fusion.1
  10.4 3.0 %collective-permute-start.10 = (bf16[512,256]{1,0:T(8,128)(2,1)S(1)}, bf16[512,256]{1,0:T(8,128)(2,1)S(1)}, u32[]{:S(2)}, u32[]{:S(2)}) collective-permute-start(bf16[512,256]{1,0:T(8,128)(2,1)S(1)} %pad_maximum_fusion), channel_id=1, source_target_pairs={{4,0},{8,4},{12,8},{16,12},{20,16},{24,20},{28,24},{5,1},{9,5},{13... | collective-permute-start | bytes 786440 | tf_op jit(solution)/shard_map/ppermute | solution.py:30
  13.4 0.0 collective-permute-done.1.near_ref
  13.4 1.8 %collective-permute-start.2 = (bf16[528,256]{1,0:T(8,128)(2,1)S(1)}, bf16[528,256]{1,0:T(8,128)(2,1)S(1)}, u32[]{:S(2)}, u32[]{:S(2)}) collective-permute-start(bf16[528,256]{1,0:T(8,128)(2,1)S(1)} %collective-permute-done.1.near_ref), channel_id=1, source_target_pairs={{0,1},{1,0},{2,3},{3,2},{4,5},{5,4},{6,7},{7,6},{8,9},{9,8},{10,11... | collective-permute-start | bytes 811016 | tf_op jit(solution)/shard_map/ppermute | solution.py:25
  15.3 0.0 collective-permute-start.5
  15.3 1.3 %collective-permute-start.11 = (bf16[256,256]{1,0:T(8,128)(2,1)S(1)}, bf16[256,256]{1,0:T(8,128)(2,1)S(1)}, u32[]{:S(2)}, u32[]{:S(2)}) collective-permute-start(bf16[256,256]{1,0:T(8,128)(2,1)S(1)} %slice.47), channel_id=1, source_target_pairs={{0,2},{1,3},{2,0},{3,1},{4,6},{5,7},{6,4},{7,5},{8,10},{9,11},{10,... | collective-permute-start | bytes 393224 | tf_op jit(solution)/shard_map/ppermute | solution.py:25
  16.6 1.6 %collective-permute-done.4.refs_1_.refs_3_ = bf16[768,256]{1,0:T(8,128)(2,1)S(1)} collective-permute-done((bf16[768,256]{1,0:T(8,128)(2,1)S(1)}, bf16[768,256]{1,0:T(8,128)(2,1)S(1)}, u32[]{:S(2)}, u32[]{:S(2)}) %collective-permute-start.4) | collective-permute-done | bytes 393248 | tf_op jit(solution)/shard_map/ppermute | solution.py:25
  18.1 1.3 %collective-permute-start.6 = (bf16[256,256]{1,0:T(8,128)(2,1)S(1)}, bf16[256,256]{1,0:T(8,128)(2,1)S(1)}, u32[]{:S(2)}, u32[]{:S(2)}) collective-permute-start(bf16[256,256]{1,0:T(8,128)(2,1)S(1)} %slice.44), channel_id=1, source_target_pairs={{0,1},{1,0},{2,3},{3,2},{4,5},{5,4},{6,7},{7,6},{8,9},{9,8},{10,11... | collective-permute-start | bytes 393224 | tf_op jit(solution)/shard_map/ppermute | solution.py:25
  19.5 0.0 collective-permute-done.5.refs_2_.refs_6_
  19.5 0.1 collective-permute-start.7
  19.6 0.2 collective-permute-done.10.refs_4_
  19.8 2.1 %collective-permute-start.12 = (bf16[512,256]{1,0:T(8,128)(2,1)S(1)}, bf16[512,256]{1,0:T(8,128)(2,1)S(1)}, u32[]{:S(2)}, u32[]{:S(2)}) collective-permute-start(bf16[512,256]{1,0:T(8,128)(2,1)S(1)} %collective-permute-done.10.refs_4_), channel_id=1, source_target_pairs={{0,1},{1,0},{2,3},{3,2},{4,5},{5,4},{6,7},{7,6},{8,9},{9,8},{10,11... | collective-permute-start | bytes 786440 | tf_op jit(solution)/shard_map/ppermute | solution.py:25
  21.9 0.0 collective-permute-done.11.refs_5_
  21.9 0.0 collective-permute-start.13
  21.9 0.0 collective-permute-done.6.refs_3_.refs_7_
  21.9 0.5 %collective-permute-start.8 = (bf16[256,256]{1,0:T(8,128)(2,1)S(1)}, bf16[256,256]{1,0:T(8,128)(2,1)S(1)}, u32[]{:S(2)}, u32[]{:S(2)}) collective-permute-start(bf16[256,256]{1,0:T(8,128)(2,1)S(1)} %get-tuple-element.34.refs_0_.seed_ref), channel_id=1, source_target_pairs={{0,1},{1,0},{2,3},{3,2},{4,5},{5,4},{6,7},{7,6},{8,9},{9,8},{10,11... | collective-permute-start | bytes 393224 | tf_op jit(solution)/shard_map/ppermute | solution.py:25
  22.5 0.0 collective-permute-done.2.near_other_ref
  22.5 0.1 collective-permute-start.14
  22.5 0.0 collective-permute-done.7.refs_4_.refs_8_
  22.5 0.9 %logits_0.1.logit_ref = f32[6,256,256]{2,1,0:T(8,128)S(1)} custom-call(f32[4,256,256]{2,1,0:T(8,128)S(1)} %get-tuple-element.20.part_ref, f32[8,1536]{1,0:T(8,128)S(1)} %get-tuple-element.21.factor_ref, f32[256,256]{1,0:T(8,128)S(1)} %get-tuple-element.22.row_ref, bf16[1024,256]{1,0:T(8,128)(2,1)S(1)} %copy-done, ...), custom_call_target="tpu_custom_call" | custom-call | flops 1 | bytes 1 | tf_op jit(solution)/shard_map/logits_0/pallas_call | solution.py:328
  23.4 0.0 collective-permute-done.13.refs_10_
  23.4 0.0 collective-permute-done.8.refs_1_
  23.5 0.3 collective-permute-done.14.refs_12_
  23.8 0.0 collective-permute-done.12.refs_9_
  23.8 1.3 %affinity_0.1 = (bf16[6,256,256]{2,1,0:T(8,128)(2,1)S(1)}, bf16[256,256]{1,0:T(8,128)(2,1)S(1)}) custom-call(f32[6,256,256]{2,1,0:T(8,128)S(1)} %logits_0.1.logit_ref, f32[8,1536]{1,0:T(8,128)S(1)} %get-tuple-element.21.factor_ref, bf16[256,256]{1,0:T(8,128)(2,1)S(1)} %get-tuple-element.34.refs_0_.seed_ref, ...), custom_call_target="tpu_custom_call" | custom-call | flops 1 | bytes 1 | tf_op jit(solution)/shard_map/affinity_0/pallas_call | solution.py:380
  25.1 2.5 %collective-permute-start.17 = (bf16[256,256]{1,0:T(8,128)(2,1)S(1)}, bf16[256,256]{1,0:T(8,128)(2,1)S(1)}, u32[]{:S(2)}, u32[]{:S(2)}) collective-permute-start(bf16[256,256]{1,0:T(8,128)(2,1)S(1)} %get-tuple-element.25.refs_2_), channel_id=1, source_target_pairs={{4,0},{8,4},{12,8},{16,12},{20,16},{24,20},{28,24},{5,1},{9,5},{13... | collective-permute-start | bytes 393224 | tf_op jit(solution)/shard_map/ppermute | solution.py:30
  27.6 1.2 %early_1.1 = (f32[4,256,256]{2,1,0:T(8,128)S(1)}, f32[8,1536]{1,0:T(8,128)S(1)}, f32[256,256]{1,0:T(8,128)S(1)}) custom-call(s32[4,4]{1,0:T(4,128)S(1)} %copy-done.2, s32[4]{0:T(128)S(1)} %copy-done.3, s32[1,1024]{1,0:T(1,128)S(1)} %bitcast.2, bf16[1024,256]{1,0:T(8,128)(2,1)S(1)} %copy-done, bf16[1024,256]{1,0:T(8,128)(2,1)S(1)} %collective-permute-done.other_ref), custom_call_target="tpu_custom_call" | custom-call | flops 1 | bytes 1 | tf_op jit(solution)/shard_map/early_1/pallas_call | solution.py:286
  28.8 0.9 %logits_1.1.logit_ref = f32[6,256,256]{2,1,0:T(8,128)S(1)} custom-call(f32[4,256,256]{2,1,0:T(8,128)S(1)} %get-tuple-element.28.part_ref, f32[8,1536]{1,0:T(8,128)S(1)} %get-tuple-element.29.factor_ref, f32[256,256]{1,0:T(8,128)S(1)} %get-tuple-element.30.row_ref, bf16[1024,256]{1,0:T(8,128)(2,1)S(1)} %copy-done, ...), custom_call_target="tpu_custom_call" | custom-call | flops 1 | bytes 1 | tf_op jit(solution)/shard_map/logits_1/pallas_call | solution.py:328
  29.7 0.7 %collective-permute-start.15 = (bf16[256,256]{1,0:T(8,128)(2,1)S(1)}, bf16[256,256]{1,0:T(8,128)(2,1)S(1)}, u32[]{:S(2)}, u32[]{:S(2)}) collective-permute-start(bf16[256,256]{1,0:T(8,128)(2,1)S(1)} %get-tuple-element.25.refs_2_), channel_id=1, source_target_pairs={{0,1},{1,0},{2,3},{3,2},{4,5},{5,4},{6,7},{7,6},{8,9},{9,8},{10,11... | collective-permute-start | bytes 393224 | tf_op jit(solution)/shard_map/ppermute | solution.py:25
  30.4 1.3 %affinity_1.1 = (bf16[6,256,256]{2,1,0:T(8,128)(2,1)S(1)}, bf16[256,256]{1,0:T(8,128)(2,1)S(1)}) custom-call(f32[6,256,256]{2,1,0:T(8,128)S(1)} %logits_1.1.logit_ref, f32[8,1536]{1,0:T(8,128)S(1)} %get-tuple-element.29.factor_ref, bf16[256,256]{1,0:T(8,128)(2,1)S(1)} %get-tuple-element.34.refs_0_.seed_ref, ...), custom_call_target="tpu_custom_call" | custom-call | flops 1 | bytes 1 | tf_op jit(solution)/shard_map/affinity_1/pallas_call | solution.py:380
  31.7 0.1 collective-permute-start.16
  31.8 1.0 %collective-permute-done.17.labels_ref = bf16[256,256]{1,0:T(8,128)(2,1)S(1)} collective-permute-done((bf16[256,256]{1,0:T(8,128)(2,1)S(1)}, bf16[256,256]{1,0:T(8,128)(2,1)S(1)}, u32[]{:S(2)}, u32[]{:S(2)}) %collective-permute-start.17) | collective-permute-done | bytes 131104 | tf_op jit(solution)/shard_map/ppermute | solution.py:30
  32.8 1.0 %collective-permute-start.18 = (bf16[256,256]{1,0:T(8,128)(2,1)S(1)}, bf16[256,256]{1,0:T(8,128)(2,1)S(1)}, u32[]{:S(2)}, u32[]{:S(2)}) collective-permute-start(bf16[256,256]{1,0:T(8,128)(2,1)S(1)} %collective-permute-done.17.labels_ref), channel_id=1, source_target_pairs={{0,1},{1,0},{2,3},{3,2},{4,5},{5,4},{6,7},{7,6},{8,9},{9,8},{10,11... | collective-permute-start | bytes 393224 | tf_op jit(solution)/shard_map/ppermute | solution.py:25
  33.8 0.0 collective-permute-done.15.refs_4_
  33.8 0.0 collective-permute-done.16.refs_5_
  33.8 0.3 spread_own.1.total_ref
  34.1 0.2 spread_near_0.1.total_ref
  34.3 0.5 %collective-permute-done.18.labels_ref = bf16[256,256]{1,0:T(8,128)(2,1)S(1)} collective-permute-done((bf16[256,256]{1,0:T(8,128)(2,1)S(1)}, bf16[256,256]{1,0:T(8,128)(2,1)S(1)}, u32[]{:S(2)}, u32[]{:S(2)}) %collective-permute-start.18) | collective-permute-done | bytes 131104 | tf_op jit(solution)/shard_map/ppermute | solution.py:25
  34.8 0.8 %spread_near_1.1 = bf16[256,256]{1,0:T(8,128)(2,1)} custom-call(f32[256,256]{1,0:T(8,128)S(1)} %spread_near_0.1.total_ref, bf16[256,256]{1,0:T(8,128)(2,1)S(1)} %collective-permute-done.18.labels_ref, bf16[6,256,256]{2,1,0:T(8,128)(2,1)S(1)} %get-tuple-element.24.refs_0_, bf16[6,256,256]{2,1,0:T(8,128)(2,1)S(1)} %get-tuple-element.31.refs_1_), custom_call_target="tpu_custom_call" | custom-call | flops 1 | bytes 1 | tf_op jit(solution)/shard_map/spread_near_1/pallas_call | solution.py:409
  (11 shorter events, 0.1 us)
Async XLA Ops:
  0.0 7.3 %copy-start = (bf16[1024,256]{1,0:T(8,128)(2,1)S(1)}, bf16[1024,256]{1,0:T(8,128)(2,1)}, u32[]{:S(2)}) copy-start(bf16[1024,256]{1,0:T(8,128)(2,1)} %own_ref.6) | copy-start | bytes 1572868
  0.0 8.7 %copy-start.5 = (s32[256]{0:T(256)S(1)}, s32[256]{0:T(256)}, u32[]{:S(2)}) copy-start(s32[256]{0:T(256)} %param.10) | copy-start | bytes 3076
  0.0 9.1 %copy-start.1 = (s32[1024]{0:T(1024)S(1)}, s32[1024]{0:T(1024)}, u32[]{:S(2)}) copy-start(s32[1024]{0:T(1024)} %param.7) | copy-start | bytes 12292
  0.0 9.1 %copy-start.2 = (s32[4,4]{1,0:T(4,128)S(1)}, s32[4,4]{1,0:T(4,128)}, u32[]{:S(2)}) copy-start(s32[4,4]{1,0:T(4,128)} %blocks_ref.3) | copy-start | bytes 196
  0.0 9.1 %copy-start.3 = (s32[4]{0:T(128)S(1)}, s32[4]{0:T(128)}, u32[]{:S(2)}) copy-start(s32[4]{0:T(128)} %counts_ref.3) | copy-start | bytes 52
  1.3 9.0 %copy-start.4 = (bf16[256,256]{1,0:T(8,128)(2,1)S(1)}, bf16[256,256]{1,0:T(8,128)(2,1)}, u32[]{:S(2)}) copy-start(bf16[256,256]{1,0:T(8,128)(2,1)} %param.11) | copy-start | bytes 393220
  1.3 7.4 %collective-permute-start.3 = (bf16[512,256]{1,0:T(8,128)(2,1)S(1)}, bf16[512,256]{1,0:T(8,128)(2,1)S(1)}, u32[]{:S(2)}, u32[]{:S(2)}) collective-permute-start(bf16[512,256]{1,0:T(8,128)(2,1)S(1)} %get-tuple-element.36), channel_id=1, source_target_pairs={{0,2},{1,3},{2,0},{3,1},{4,6},{5,7},{6,4},{7,5},{8,10},{9,11},{10,... | collective-permute-start | bytes 786440 | tf_op jit(solution)/shard_map/ppermute | solution.py:25
  2.6 6.1 %collective-permute-start.9 = (s32[256]{0:T(256)}, s32[256]{0:T(256)S(1)}, u32[]{:S(2)}, u32[]{:S(2)}) collective-permute-start(s32[256]{0:T(256)} %param.10), channel_id=1, source_target_pairs={{0,2},{1,3},{2,0},{3,1},{4,6},{5,7},{6,4},{7,5},{8,10},{9,11},{10,... | collective-permute-start | bytes 3080 | tf_op jit(solution)/shard_map/ppermute | solution.py:25
  3.6 9.9 %collective-permute-start.1 = (bf16[528,256]{1,0:T(8,128)(2,1)S(1)}, bf16[528,256]{1,0:T(8,128)(2,1)S(1)}, u32[]{:S(2)}, u32[]{:S(2)}) collective-permute-start(bf16[528,256]{1,0:T(8,128)(2,1)S(1)} %fusion.1), channel_id=1, source_target_pairs={{4,0},{8,4},{12,8},{16,12},{20,16},{24,20},{28,24},{5,1},{9,5},{13... | collective-permute-start | bytes 811016 | tf_op jit(solution)/shard_map/ppermute | solution.py:30
  5.7 3.3 %collective-permute-start = (bf16[1024,256]{1,0:T(8,128)(2,1)}, bf16[1024,256]{1,0:T(8,128)(2,1)S(1)}, u32[]{:S(2)}, u32[]{:S(2)}) collective-permute-start(bf16[1024,256]{1,0:T(8,128)(2,1)} %own_ref.6), channel_id=1, source_target_pairs={{0,1},{1,0},{2,3},{3,2},{4,5},{5,4},{6,7},{7,6},{8,9},{9,8},{10,11... | collective-permute-start | bytes 1572872 | tf_op jit(solution)/shard_map/ppermute | solution.py:25
  7.3 10.8 %collective-permute-start.4 = (bf16[768,256]{1,0:T(8,128)(2,1)S(1)}, bf16[768,256]{1,0:T(8,128)(2,1)S(1)}, u32[]{:S(2)}, u32[]{:S(2)}) collective-permute-start(bf16[768,256]{1,0:T(8,128)(2,1)S(1)} %slice.37), channel_id=1, source_target_pairs={{0,2},{1,3},{2,0},{3,1},{4,6},{5,7},{6,4},{7,5},{8,10},{9,11},{10,... | collective-permute-start | bytes 1179656 | tf_op jit(solution)/shard_map/ppermute | solution.py:25
  10.4 9.4 %collective-permute-start.10 = (bf16[512,256]{1,0:T(8,128)(2,1)S(1)}, bf16[512,256]{1,0:T(8,128)(2,1)S(1)}, u32[]{:S(2)}, u32[]{:S(2)}) collective-permute-start(bf16[512,256]{1,0:T(8,128)(2,1)S(1)} %pad_maximum_fusion), channel_id=1, source_target_pairs={{4,0},{8,4},{12,8},{16,12},{20,16},{24,20},{28,24},{5,1},{9,5},{13... | collective-permute-start | bytes 786440 | tf_op jit(solution)/shard_map/ppermute | solution.py:30
  13.4 9.0 %collective-permute-start.2 = (bf16[528,256]{1,0:T(8,128)(2,1)S(1)}, bf16[528,256]{1,0:T(8,128)(2,1)S(1)}, u32[]{:S(2)}, u32[]{:S(2)}) collective-permute-start(bf16[528,256]{1,0:T(8,128)(2,1)S(1)} %collective-permute-done.1.near_ref), channel_id=1, source_target_pairs={{0,1},{1,0},{2,3},{3,2},{4,5},{5,4},{6,7},{7,6},{8,9},{9,8},{10,11... | collective-permute-start | bytes 811016 | tf_op jit(solution)/shard_map/ppermute | solution.py:25
  15.3 4.2 %collective-permute-start.5 = (bf16[256,256]{1,0:T(8,128)(2,1)S(1)}, bf16[256,256]{1,0:T(8,128)(2,1)S(1)}, u32[]{:S(2)}, u32[]{:S(2)}) collective-permute-start(bf16[256,256]{1,0:T(8,128)(2,1)S(1)} %get-tuple-element.37), channel_id=1, source_target_pairs={{0,1},{1,0},{2,3},{3,2},{4,5},{5,4},{6,7},{7,6},{8,9},{9,8},{10,11... | collective-permute-start | bytes 393224 | tf_op jit(solution)/shard_map/ppermute | solution.py:25
  15.3 6.7 %collective-permute-start.11 = (bf16[256,256]{1,0:T(8,128)(2,1)S(1)}, bf16[256,256]{1,0:T(8,128)(2,1)S(1)}, u32[]{:S(2)}, u32[]{:S(2)}) collective-permute-start(bf16[256,256]{1,0:T(8,128)(2,1)S(1)} %slice.47), channel_id=1, source_target_pairs={{0,2},{1,3},{2,0},{3,1},{4,6},{5,7},{6,4},{7,5},{8,10},{9,11},{10,... | collective-permute-start | bytes 393224 | tf_op jit(solution)/shard_map/ppermute | solution.py:25
  18.1 3.8 %collective-permute-start.6 = (bf16[256,256]{1,0:T(8,128)(2,1)S(1)}, bf16[256,256]{1,0:T(8,128)(2,1)S(1)}, u32[]{:S(2)}, u32[]{:S(2)}) collective-permute-start(bf16[256,256]{1,0:T(8,128)(2,1)S(1)} %slice.44), channel_id=1, source_target_pairs={{0,1},{1,0},{2,3},{3,2},{4,5},{5,4},{6,7},{7,6},{8,9},{9,8},{10,11... | collective-permute-start | bytes 393224 | tf_op jit(solution)/shard_map/ppermute | solution.py:25
  19.5 3.1 %collective-permute-start.7 = (bf16[512,256]{1,0:T(8,128)(2,1)S(1)}, bf16[512,256]{1,0:T(8,128)(2,1)S(1)}, u32[]{:S(2)}, u32[]{:S(2)}) collective-permute-start(bf16[512,256]{1,0:T(8,128)(2,1)S(1)} %slice.45), channel_id=1, source_target_pairs={{0,1},{1,0},{2,3},{3,2},{4,5},{5,4},{6,7},{7,6},{8,9},{9,8},{10,11... | collective-permute-start | bytes 786440 | tf_op jit(solution)/shard_map/ppermute | solution.py:25
  19.8 4.0 %collective-permute-start.12 = (bf16[512,256]{1,0:T(8,128)(2,1)S(1)}, bf16[512,256]{1,0:T(8,128)(2,1)S(1)}, u32[]{:S(2)}, u32[]{:S(2)}) collective-permute-start(bf16[512,256]{1,0:T(8,128)(2,1)S(1)} %collective-permute-done.10.refs_4_), channel_id=1, source_target_pairs={{0,1},{1,0},{2,3},{3,2},{4,5},{5,4},{6,7},{7,6},{8,9},{9,8},{10,11... | collective-permute-start | bytes 786440 | tf_op jit(solution)/shard_map/ppermute | solution.py:25
  21.9 1.5 %collective-permute-start.13 = (bf16[256,256]{1,0:T(8,128)(2,1)S(1)}, bf16[256,256]{1,0:T(8,128)(2,1)S(1)}, u32[]{:S(2)}, u32[]{:S(2)}) collective-permute-start(bf16[256,256]{1,0:T(8,128)(2,1)S(1)} %collective-permute-done.11.refs_5_), channel_id=1, source_target_pairs={{0,1},{1,0},{2,3},{3,2},{4,5},{5,4},{6,7},{7,6},{8,9},{9,8},{10,11... | collective-permute-start | bytes 393224 | tf_op jit(solution)/shard_map/ppermute | solution.py:25
  21.9 1.5 %collective-permute-start.8 = (bf16[256,256]{1,0:T(8,128)(2,1)S(1)}, bf16[256,256]{1,0:T(8,128)(2,1)S(1)}, u32[]{:S(2)}, u32[]{:S(2)}) collective-permute-start(bf16[256,256]{1,0:T(8,128)(2,1)S(1)} %get-tuple-element.34.refs_0_.seed_ref), channel_id=1, source_target_pairs={{0,1},{1,0},{2,3},{3,2},{4,5},{5,4},{6,7},{7,6},{8,9},{9,8},{10,11... | collective-permute-start | bytes 393224 | tf_op jit(solution)/shard_map/ppermute | solution.py:25
  22.5 1.3 %collective-permute-start.14 = (bf16[256,256]{1,0:T(8,128)(2,1)S(1)}, bf16[256,256]{1,0:T(8,128)(2,1)S(1)}, u32[]{:S(2)}, u32[]{:S(2)}) collective-permute-start(bf16[256,256]{1,0:T(8,128)(2,1)S(1)} %get-tuple-element.23.refs_11_), channel_id=1, source_target_pairs={{0,1},{1,0},{2,3},{3,2},{4,5},{5,4},{6,7},{7,6},{8,9},{9,8},{10,11... | collective-permute-start | bytes 393224 | tf_op jit(solution)/shard_map/ppermute | solution.py:25
  25.1 7.7 %collective-permute-start.17 = (bf16[256,256]{1,0:T(8,128)(2,1)S(1)}, bf16[256,256]{1,0:T(8,128)(2,1)S(1)}, u32[]{:S(2)}, u32[]{:S(2)}) collective-permute-start(bf16[256,256]{1,0:T(8,128)(2,1)S(1)} %get-tuple-element.25.refs_2_), channel_id=1, source_target_pairs={{4,0},{8,4},{12,8},{16,12},{20,16},{24,20},{28,24},{5,1},{9,5},{13... | collective-permute-start | bytes 393224 | tf_op jit(solution)/shard_map/ppermute | solution.py:30
  29.7 4.1 %collective-permute-start.15 = (bf16[256,256]{1,0:T(8,128)(2,1)S(1)}, bf16[256,256]{1,0:T(8,128)(2,1)S(1)}, u32[]{:S(2)}, u32[]{:S(2)}) collective-permute-start(bf16[256,256]{1,0:T(8,128)(2,1)S(1)} %get-tuple-element.25.refs_2_), channel_id=1, source_target_pairs={{0,1},{1,0},{2,3},{3,2},{4,5},{5,4},{6,7},{7,6},{8,9},{9,8},{10,11... | collective-permute-start | bytes 393224 | tf_op jit(solution)/shard_map/ppermute | solution.py:25
  31.7 2.1 %collective-permute-start.16 = (bf16[256,256]{1,0:T(8,128)(2,1)S(1)}, bf16[256,256]{1,0:T(8,128)(2,1)S(1)}, u32[]{:S(2)}, u32[]{:S(2)}) collective-permute-start(bf16[256,256]{1,0:T(8,128)(2,1)S(1)} %get-tuple-element.32.refs_3_), channel_id=1, source_target_pairs={{0,1},{1,0},{2,3},{3,2},{4,5},{5,4},{6,7},{7,6},{8,9},{9,8},{10,11... | collective-permute-start | bytes 393224 | tf_op jit(solution)/shard_map/ppermute | solution.py:25
  32.8 2.0 %collective-permute-start.18 = (bf16[256,256]{1,0:T(8,128)(2,1)S(1)}, bf16[256,256]{1,0:T(8,128)(2,1)S(1)}, u32[]{:S(2)}, u32[]{:S(2)}) collective-permute-start(bf16[256,256]{1,0:T(8,128)(2,1)S(1)} %collective-permute-done.17.labels_ref), channel_id=1, source_target_pairs={{0,1},{1,0},{2,3},{3,2},{4,5},{5,4},{6,7},{7,6},{8,9},{9,8},{10,11... | collective-permute-start | bytes 393224 | tf_op jit(solution)/shard_map/ppermute | solution.py:25

commit v7 on v6

--- a/solution.py
+++ b/solution.py
@@ -312,7 +312,9 @@
     near_second = [across(near[TILE:head_rows], 2 * m) for m in apart]
 
     first_far_other = [across(tile_in(f, 0), 1) for f in first_far]
-    rest_far_other = [(across(f[:TILE], 1), across(f[TILE:], 1)) for f in rest_far]
+    rest_far_other = [
+        (across(f[:TILE], 1), across(after(f[TILE:], first_far_other), 1)) for f in rest_far
+    ]
     seeds_other = across(seeds, 1)
     seeds_far_other = [across(f, 1) for f in seeds_far]
 

time: 35.9 us -> 35.9 us (level)
  no operation moved by 1% of the time
where the time goes in v7:
time: 35.9 us; the launch traced here: 35.6 us
  starting transfers between devices  21.1 us (59%)
  Pallas kernels  8.1 us (23%)
  waiting for transfers between devices  3.9 us (11%)
  other arithmetic  2.19 us (6%)
    ppermute x16, starting transfers between devices, across(): lax.ppermute(block, 'grp', [(i, i ^ distance) for i in range(groups)])  13.4 us
    ppermute x3, starting transfers between devices, from_next(): return lax.ppermute(block, 'shard', [(i + 1, i) for i in range(shards - 1)])  7.67 us
    ppermute x16, waiting for transfers between devices, across(): lax.ppermute(block, 'grp', [(i, i ^ distance) for i in range(groups)])  2.67 us
    pallas_call x2, Pallas kernels, affinity_of(): pl.pallas_call(functools.partial(affinity_kernel, groups, m, windows), ou...  2.58 us
    pallas_call x2, Pallas kernels, early_of(): pl.pallas_call(functools.partial(early_kernel, groups, m), out_shape=(jax...  2.36 us
    pallas_call x2, Pallas kernels, logits_of(): pl.pallas_call(functools.partial(logit_kernel, groups, m, own_windows), o...  1.79 us
    ppermute x3, waiting for transfers between devices, from_next(): return lax.ppermute(block, 'shard', [(i + 1, i) for i in range(shards - 1)])  1.23 us
    slice x1, other arithmetic, local(): head = jnp.concatenate([embeddings[:head_rows], head_c])  1.23 us
  transfers between devices with their start and end apart: 19, of which 6 were waited for; matrix products, arithmetic and copies ran while one was open for 3% of the time, Pallas kernels for 17%

profile of v7, /device:TPU:11, one launch (start us, length us, event | category | flops | bytes accessed | tf_op | source)
XLA Modules:
  0.0 35.6 jit_solution(10193122147064965178)
XLA Ops:
  0.0 0.0 copy-start
  0.0 0.0 copy-start.5
  0.0 0.0 copy-start.1
  0.0 0.0 copy-start.2
  0.0 0.0 copy-start.3
  0.0 1.2 %fusion.2 = (bf16[512,256]{1,0:T(8,128)(2,1)S(1)}, bf16[512,256]{1,0:T(8,128)(2,1)S(1)}) fusion(bf16[1024,256]{1,0:T(8,128)(2,1)} %own_ref.6, bf16[256,256]{1,0:T(8,128)(2,1)} %param.11, pred[512]{0:T(512)(128)(4,1)S(1)} %iota_compare_fusion.1), kind=kLoop, calls=%fused_computation.11 | loop fusion | flops 655360 | bytes 918016 | tf_op jit(solution)/shard_map/slice | solution.py:278
  1.3 0.0 copy-start.4
  1.3 1.3 %collective-permute-start.3 = (bf16[512,256]{1,0:T(8,128)(2,1)S(1)}, bf16[512,256]{1,0:T(8,128)(2,1)S(1)}, u32[]{:S(2)}, u32[]{:S(2)}) collective-permute-start(bf16[512,256]{1,0:T(8,128)(2,1)S(1)} %get-tuple-element.38), channel_id=1, source_target_pairs={{0,2},{1,3},{2,0},{3,1},{4,6},{5,7},{6,4},{7,5},{8,10},{9,11},{10,... | collective-permute-start | bytes 786440 | tf_op jit(solution)/shard_map/ppermute | solution.py:25
  2.6 0.2 collective-permute-start.9
  2.8 0.7 %convert.3 = bf16[1024]{0:T(1024)(128)(2,1)S(1)} convert(s32[1024]{0:T(1024)} %param.7) | non-fusion elementwise | flops 1024 | bytes 6144 | tf_op jit(solution)/shard_map/convert
  3.6 2.2 %collective-permute-start.1 = (bf16[528,256]{1,0:T(8,128)(2,1)S(1)}, bf16[528,256]{1,0:T(8,128)(2,1)S(1)}, u32[]{:S(2)}, u32[]{:S(2)}) collective-permute-start(bf16[528,256]{1,0:T(8,128)(2,1)S(1)} %fusion.1), channel_id=1, source_target_pairs={{4,0},{8,4},{12,8},{16,12},{20,16},{24,20},{28,24},{5,1},{9,5},{13... | collective-permute-start | bytes 811016 | tf_op jit(solution)/shard_map/ppermute | solution.py:30
  5.7 1.6 %collective-permute-start = (bf16[1024,256]{1,0:T(8,128)(2,1)}, bf16[1024,256]{1,0:T(8,128)(2,1)S(1)}, u32[]{:S(2)}, u32[]{:S(2)}) collective-permute-start(bf16[1024,256]{1,0:T(8,128)(2,1)} %own_ref.6), channel_id=1, source_target_pairs={{0,1},{1,0},{2,3},{3,2},{4,5},{5,4},{6,7},{7,6},{8,9},{9,8},{10,11... | collective-permute-start | bytes 1572872 | tf_op jit(solution)/shard_map/ppermute | solution.py:25
  7.3 0.0 copy-done
  7.3 1.3 %collective-permute-start.4 = (bf16[768,256]{1,0:T(8,128)(2,1)S(1)}, bf16[768,256]{1,0:T(8,128)(2,1)S(1)}, u32[]{:S(2)}, u32[]{:S(2)}) collective-permute-start(bf16[768,256]{1,0:T(8,128)(2,1)S(1)} %slice.37), channel_id=1, source_target_pairs={{0,2},{1,3},{2,0},{3,1},{4,6},{5,7},{6,4},{7,5},{8,10},{9,11},{10,... | collective-permute-start | bytes 1179656 | tf_op jit(solution)/shard_map/ppermute | solution.py:25
  8.7 0.0 copy-done.5
  8.7 0.0 collective-permute-done.9
  8.7 0.0 collective-permute-done.3.refs_0_.refs_2_
  8.7 0.1 fusion.3
  8.8 0.3 collective-permute-done.other_ref
  9.1 0.0 copy-done.1
  9.1 0.0 copy-done.2
  9.1 0.0 copy-done.3
  9.1 1.2 %early_0.1 = (f32[4,256,256]{2,1,0:T(8,128)S(1)}, f32[8,1536]{1,0:T(8,128)S(1)}, f32[256,256]{1,0:T(8,128)S(1)}) custom-call(s32[4,4]{1,0:T(4,128)S(1)} %copy-done.2, s32[4]{0:T(128)S(1)} %copy-done.3, s32[1,1024]{1,0:T(1,128)S(1)} %bitcast.1, bf16[1024,256]{1,0:T(8,128)(2,1)S(1)} %copy-done, bf16[1024,256]{1,0:T(8,128)(2,1)S(1)} %collective-permute-done.other_ref), custom_call_target="tpu_custom_call" | custom-call | flops 1 | bytes 1 | tf_op jit(solution)/shard_map/early_0/pallas_call | solution.py:286
  10.3 0.0 copy-done.4
  10.3 0.1 broadcast_select_fusion.1
  10.4 3.0 %collective-permute-start.10 = (bf16[512,256]{1,0:T(8,128)(2,1)S(1)}, bf16[512,256]{1,0:T(8,128)(2,1)S(1)}, u32[]{:S(2)}, u32[]{:S(2)}) collective-permute-start(bf16[512,256]{1,0:T(8,128)(2,1)S(1)} %pad_maximum_fusion), channel_id=1, source_target_pairs={{4,0},{8,4},{12,8},{16,12},{20,16},{24,20},{28,24},{5,1},{9,5},{13... | collective-permute-start | bytes 786440 | tf_op jit(solution)/shard_map/ppermute | solution.py:30
  13.4 0.0 collective-permute-done.1.near_ref
  13.4 1.8 %collective-permute-start.2 = (bf16[528,256]{1,0:T(8,128)(2,1)S(1)}, bf16[528,256]{1,0:T(8,128)(2,1)S(1)}, u32[]{:S(2)}, u32[]{:S(2)}) collective-permute-start(bf16[528,256]{1,0:T(8,128)(2,1)S(1)} %collective-permute-done.1.near_ref), channel_id=1, source_target_pairs={{0,1},{1,0},{2,3},{3,2},{4,5},{5,4},{6,7},{7,6},{8,9},{9,8},{10,11... | collective-permute-start | bytes 811016 | tf_op jit(solution)/shard_map/ppermute | solution.py:25
  15.3 0.0 collective-permute-start.5
  15.3 1.3 %collective-permute-start.11 = (bf16[256,256]{1,0:T(8,128)(2,1)S(1)}, bf16[256,256]{1,0:T(8,128)(2,1)S(1)}, u32[]{:S(2)}, u32[]{:S(2)}) collective-permute-start(bf16[256,256]{1,0:T(8,128)(2,1)S(1)} %slice.47), channel_id=1, source_target_pairs={{0,2},{1,3},{2,0},{3,1},{4,6},{5,7},{6,4},{7,5},{8,10},{9,11},{10,... | collective-permute-start | bytes 393224 | tf_op jit(solution)/shard_map/ppermute | solution.py:25
  16.6 1.6 %collective-permute-done.4.refs_1_.refs_3_ = bf16[768,256]{1,0:T(8,128)(2,1)S(1)} collective-permute-done((bf16[768,256]{1,0:T(8,128)(2,1)S(1)}, bf16[768,256]{1,0:T(8,128)(2,1)S(1)}, u32[]{:S(2)}, u32[]{:S(2)}) %collective-permute-start.4) | collective-permute-done | bytes 393248 | tf_op jit(solution)/shard_map/ppermute | solution.py:25
  18.1 1.3 %collective-permute-start.6 = (bf16[256,256]{1,0:T(8,128)(2,1)S(1)}, bf16[256,256]{1,0:T(8,128)(2,1)S(1)}, u32[]{:S(2)}, u32[]{:S(2)}) collective-permute-start(bf16[256,256]{1,0:T(8,128)(2,1)S(1)} %slice.44), channel_id=1, source_target_pairs={{0,1},{1,0},{2,3},{3,2},{4,5},{5,4},{6,7},{7,6},{8,9},{9,8},{10,11... | collective-permute-start | bytes 393224 | tf_op jit(solution)/shard_map/ppermute | solution.py:25
  19.5 0.0 collective-permute-done.5.refs_2_.refs_6_
  19.5 0.1 collective-permute-start.7
  19.6 0.2 collective-permute-done.10.refs_4_
  19.8 2.1 %collective-permute-start.12 = (bf16[512,256]{1,0:T(8,128)(2,1)S(1)}, bf16[512,256]{1,0:T(8,128)(2,1)S(1)}, u32[]{:S(2)}, u32[]{:S(2)}) collective-permute-start(bf16[512,256]{1,0:T(8,128)(2,1)S(1)} %collective-permute-done.10.refs_4_), channel_id=1, source_target_pairs={{0,1},{1,0},{2,3},{3,2},{4,5},{5,4},{6,7},{7,6},{8,9},{9,8},{10,11... | collective-permute-start | bytes 786440 | tf_op jit(solution)/shard_map/ppermute | solution.py:25
  21.9 0.0 collective-permute-done.11.refs_5_
  21.9 0.0 collective-permute-start.13
  21.9 0.0 collective-permute-done.6.refs_3_.refs_7_
  21.9 0.5 %collective-permute-start.8 = (bf16[256,256]{1,0:T(8,128)(2,1)S(1)}, bf16[256,256]{1,0:T(8,128)(2,1)S(1)}, u32[]{:S(2)}, u32[]{:S(2)}) collective-permute-start(bf16[256,256]{1,0:T(8,128)(2,1)S(1)} %get-tuple-element.36.refs_0_.seed_ref), channel_id=1, source_target_pairs={{0,1},{1,0},{2,3},{3,2},{4,5},{5,4},{6,7},{7,6},{8,9},{9,8},{10,11... | collective-permute-start | bytes 393224 | tf_op jit(solution)/shard_map/ppermute | solution.py:25
  22.5 0.0 collective-permute-done.2.near_other_ref
  22.5 0.1 collective-permute-start.14
  22.5 0.0 collective-permute-done.7.refs_4_.refs_8_
  22.5 0.9 %logits_0.1.logit_ref = f32[6,256,256]{2,1,0:T(8,128)S(1)} custom-call(f32[4,256,256]{2,1,0:T(8,128)S(1)} %get-tuple-element.21.part_ref, f32[8,1536]{1,0:T(8,128)S(1)} %get-tuple-element.22.factor_ref, f32[256,256]{1,0:T(8,128)S(1)} %get-tuple-element.23.row_ref, bf16[1024,256]{1,0:T(8,128)(2,1)S(1)} %copy-done, ...), custom_call_target="tpu_custom_call" | custom-call | flops 1 | bytes 1 | tf_op jit(solution)/shard_map/logits_0/pallas_call | solution.py:330
  23.4 0.0 collective-permute-done.13.refs_10_
  23.4 0.0 collective-permute-done.8.refs_1_
  23.5 0.3 collective-permute-done.14.refs_12_
  23.8 0.0 collective-permute-done.12.refs_9_
  23.8 1.3 %affinity_0.1 = (bf16[6,256,256]{2,1,0:T(8,128)(2,1)S(1)}, bf16[256,256]{1,0:T(8,128)(2,1)S(1)}) custom-call(f32[6,256,256]{2,1,0:T(8,128)S(1)} %logits_0.1.logit_ref, f32[8,1536]{1,0:T(8,128)S(1)} %get-tuple-element.22.factor_ref, bf16[256,256]{1,0:T(8,128)(2,1)S(1)} %get-tuple-element.36.refs_0_.seed_ref, ...), custom_call_target="tpu_custom_call" | custom-call | flops 1 | bytes 1 | tf_op jit(solution)/shard_map/affinity_0/pallas_call | solution.py:382
  25.1 2.5 %collective-permute-start.17 = (bf16[256,256]{1,0:T(8,128)(2,1)S(1)}, bf16[256,256]{1,0:T(8,128)(2,1)S(1)}, u32[]{:S(2)}, u32[]{:S(2)}) collective-permute-start(bf16[256,256]{1,0:T(8,128)(2,1)S(1)} %get-tuple-element.27.refs_2_), channel_id=1, source_target_pairs={{4,0},{8,4},{12,8},{16,12},{20,16},{24,20},{28,24},{5,1},{9,5},{13... | collective-permute-start | bytes 393224 | tf_op jit(solution)/shard_map/ppermute | solution.py:30
  27.6 1.2 %early_1.1 = (f32[4,256,256]{2,1,0:T(8,128)S(1)}, f32[8,1536]{1,0:T(8,128)S(1)}, f32[256,256]{1,0:T(8,128)S(1)}) custom-call(s32[4,4]{1,0:T(4,128)S(1)} %copy-done.2, s32[4]{0:T(128)S(1)} %copy-done.3, s32[1,1024]{1,0:T(1,128)S(1)} %bitcast.2, bf16[1024,256]{1,0:T(8,128)(2,1)S(1)} %copy-done, bf16[1024,256]{1,0:T(8,128)(2,1)S(1)} %collective-permute-done.other_ref), custom_call_target="tpu_custom_call" | custom-call | flops 1 | bytes 1 | tf_op jit(solution)/shard_map/early_1/pallas_call | solution.py:286
  28.8 0.9 %logits_1.1.logit_ref = f32[6,256,256]{2,1,0:T(8,128)S(1)} custom-call(f32[4,256,256]{2,1,0:T(8,128)S(1)} %get-tuple-element.30.part_ref, f32[8,1536]{1,0:T(8,128)S(1)} %get-tuple-element.31.factor_ref, f32[256,256]{1,0:T(8,128)S(1)} %get-tuple-element.32.row_ref, bf16[1024,256]{1,0:T(8,128)(2,1)S(1)} %copy-done, ...), custom_call_target="tpu_custom_call" | custom-call | flops 1 | bytes 1 | tf_op jit(solution)/shard_map/logits_1/pallas_call | solution.py:330
  29.7 0.7 %collective-permute-start.15 = (bf16[256,256]{1,0:T(8,128)(2,1)S(1)}, bf16[256,256]{1,0:T(8,128)(2,1)S(1)}, u32[]{:S(2)}, u32[]{:S(2)}) collective-permute-start(bf16[256,256]{1,0:T(8,128)(2,1)S(1)} %get-tuple-element.27.refs_2_), channel_id=1, source_target_pairs={{0,1},{1,0},{2,3},{3,2},{4,5},{5,4},{6,7},{7,6},{8,9},{9,8},{10,11... | collective-permute-start | bytes 393224 | tf_op jit(solution)/shard_map/ppermute | solution.py:25
  30.4 1.3 %affinity_1.1 = (bf16[6,256,256]{2,1,0:T(8,128)(2,1)S(1)}, bf16[256,256]{1,0:T(8,128)(2,1)S(1)}) custom-call(f32[6,256,256]{2,1,0:T(8,128)S(1)} %logits_1.1.logit_ref, f32[8,1536]{1,0:T(8,128)S(1)} %get-tuple-element.31.factor_ref, bf16[256,256]{1,0:T(8,128)(2,1)S(1)} %get-tuple-element.36.refs_0_.seed_ref, ...), custom_call_target="tpu_custom_call" | custom-call | flops 1 | bytes 1 | tf_op jit(solution)/shard_map/affinity_1/pallas_call | solution.py:382
  31.7 0.1 collective-permute-start.16
  31.8 1.0 %collective-permute-done.17.labels_ref = bf16[256,256]{1,0:T(8,128)(2,1)S(1)} collective-permute-done((bf16[256,256]{1,0:T(8,128)(2,1)S(1)}, bf16[256,256]{1,0:T(8,128)(2,1)S(1)}, u32[]{:S(2)}, u32[]{:S(2)}) %collective-permute-start.17) | collective-permute-done | bytes 131104 | tf_op jit(solution)/shard_map/ppermute | solution.py:30
  32.8 1.0 %collective-permute-start.18 = (bf16[256,256]{1,0:T(8,128)(2,1)S(1)}, bf16[256,256]{1,0:T(8,128)(2,1)S(1)}, u32[]{:S(2)}, u32[]{:S(2)}) collective-permute-start(bf16[256,256]{1,0:T(8,128)(2,1)S(1)} %collective-permute-done.17.labels_ref), channel_id=1, source_target_pairs={{0,1},{1,0},{2,3},{3,2},{4,5},{5,4},{6,7},{7,6},{8,9},{9,8},{10,11... | collective-permute-start | bytes 393224 | tf_op jit(solution)/shard_map/ppermute | solution.py:25
  33.8 0.0 collective-permute-done.15.refs_4_
  33.8 0.0 collective-permute-done.16.refs_5_
  33.8 0.3 spread_own.1.total_ref
  34.1 0.2 spread_near_0.1.total_ref
  34.3 0.5 %collective-permute-done.18.labels_ref = bf16[256,256]{1,0:T(8,128)(2,1)S(1)} collective-permute-done((bf16[256,256]{1,0:T(8,128)(2,1)S(1)}, bf16[256,256]{1,0:T(8,128)(2,1)S(1)}, u32[]{:S(2)}, u32[]{:S(2)}) %collective-permute-start.18) | collective-permute-done | bytes 131104 | tf_op jit(solution)/shard_map/ppermute | solution.py:25
  34.8 0.8 %spread_near_1.1 = bf16[256,256]{1,0:T(8,128)(2,1)} custom-call(f32[256,256]{1,0:T(8,128)S(1)} %spread_near_0.1.total_ref, bf16[256,256]{1,0:T(8,128)(2,1)S(1)} %collective-permute-done.18.labels_ref, bf16[6,256,256]{2,1,0:T(8,128)(2,1)S(1)} %get-tuple-element.26.refs_0_, bf16[6,256,256]{2,1,0:T(8,128)(2,1)S(1)} %get-tuple-element.33.refs_1_), custom_call_target="tpu_custom_call" | custom-call | flops 1 | bytes 1 | tf_op jit(solution)/shard_map/spread_near_1/pallas_call | solution.py:411
  (11 shorter events, 0.1 us)
Async XLA Ops:
  0.0 7.3 %copy-start = (bf16[1024,256]{1,0:T(8,128)(2,1)S(1)}, bf16[1024,256]{1,0:T(8,128)(2,1)}, u32[]{:S(2)}) copy-start(bf16[1024,256]{1,0:T(8,128)(2,1)} %own_ref.6) | copy-start | bytes 1572868
  0.0 8.7 %copy-start.5 = (s32[256]{0:T(256)S(1)}, s32[256]{0:T(256)}, u32[]{:S(2)}) copy-start(s32[256]{0:T(256)} %param.10) | copy-start | bytes 3076
  0.0 9.1 %copy-start.1 = (s32[1024]{0:T(1024)S(1)}, s32[1024]{0:T(1024)}, u32[]{:S(2)}) copy-start(s32[1024]{0:T(1024)} %param.7) | copy-start | bytes 12292
  0.0 9.1 %copy-start.2 = (s32[4,4]{1,0:T(4,128)S(1)}, s32[4,4]{1,0:T(4,128)}, u32[]{:S(2)}) copy-start(s32[4,4]{1,0:T(4,128)} %blocks_ref.3) | copy-start | bytes 196
  0.0 9.1 %copy-start.3 = (s32[4]{0:T(128)S(1)}, s32[4]{0:T(128)}, u32[]{:S(2)}) copy-start(s32[4]{0:T(128)} %counts_ref.3) | copy-start | bytes 52
  1.3 9.0 %copy-start.4 = (bf16[256,256]{1,0:T(8,128)(2,1)S(1)}, bf16[256,256]{1,0:T(8,128)(2,1)}, u32[]{:S(2)}) copy-start(bf16[256,256]{1,0:T(8,128)(2,1)} %param.11) | copy-start | bytes 393220
  1.3 7.4 %collective-permute-start.3 = (bf16[512,256]{1,0:T(8,128)(2,1)S(1)}, bf16[512,256]{1,0:T(8,128)(2,1)S(1)}, u32[]{:S(2)}, u32[]{:S(2)}) collective-permute-start(bf16[512,256]{1,0:T(8,128)(2,1)S(1)} %get-tuple-element.38), channel_id=1, source_target_pairs={{0,2},{1,3},{2,0},{3,1},{4,6},{5,7},{6,4},{7,5},{8,10},{9,11},{10,... | collective-permute-start | bytes 786440 | tf_op jit(solution)/shard_map/ppermute | solution.py:25
  2.6 6.1 %collective-permute-start.9 = (s32[256]{0:T(256)}, s32[256]{0:T(256)S(1)}, u32[]{:S(2)}, u32[]{:S(2)}) collective-permute-start(s32[256]{0:T(256)} %param.10), channel_id=1, source_target_pairs={{0,2},{1,3},{2,0},{3,1},{4,6},{5,7},{6,4},{7,5},{8,10},{9,11},{10,... | collective-permute-start | bytes 3080 | tf_op jit(solution)/shard_map/ppermute | solution.py:25
  3.6 9.9 %collective-permute-start.1 = (bf16[528,256]{1,0:T(8,128)(2,1)S(1)}, bf16[528,256]{1,0:T(8,128)(2,1)S(1)}, u32[]{:S(2)}, u32[]{:S(2)}) collective-permute-start(bf16[528,256]{1,0:T(8,128)(2,1)S(1)} %fusion.1), channel_id=1, source_target_pairs={{4,0},{8,4},{12,8},{16,12},{20,16},{24,20},{28,24},{5,1},{9,5},{13... | collective-permute-start | bytes 811016 | tf_op jit(solution)/shard_map/ppermute | solution.py:30
  5.7 3.3 %collective-permute-start = (bf16[1024,256]{1,0:T(8,128)(2,1)}, bf16[1024,256]{1,0:T(8,128)(2,1)S(1)}, u32[]{:S(2)}, u32[]{:S(2)}) collective-permute-start(bf16[1024,256]{1,0:T(8,128)(2,1)} %own_ref.6), channel_id=1, source_target_pairs={{0,1},{1,0},{2,3},{3,2},{4,5},{5,4},{6,7},{7,6},{8,9},{9,8},{10,11... | collective-permute-start | bytes 1572872 | tf_op jit(solution)/shard_map/ppermute | solution.py:25
  7.3 10.8 %collective-permute-start.4 = (bf16[768,256]{1,0:T(8,128)(2,1)S(1)}, bf16[768,256]{1,0:T(8,128)(2,1)S(1)}, u32[]{:S(2)}, u32[]{:S(2)}) collective-permute-start(bf16[768,256]{1,0:T(8,128)(2,1)S(1)} %slice.37), channel_id=1, source_target_pairs={{0,2},{1,3},{2,0},{3,1},{4,6},{5,7},{6,4},{7,5},{8,10},{9,11},{10,... | collective-permute-start | bytes 1179656 | tf_op jit(solution)/shard_map/ppermute | solution.py:25
  10.4 9.4 %collective-permute-start.10 = (bf16[512,256]{1,0:T(8,128)(2,1)S(1)}, bf16[512,256]{1,0:T(8,128)(2,1)S(1)}, u32[]{:S(2)}, u32[]{:S(2)}) collective-permute-start(bf16[512,256]{1,0:T(8,128)(2,1)S(1)} %pad_maximum_fusion), channel_id=1, source_target_pairs={{4,0},{8,4},{12,8},{16,12},{20,16},{24,20},{28,24},{5,1},{9,5},{13... | collective-permute-start | bytes 786440 | tf_op jit(solution)/shard_map/ppermute | solution.py:30
  13.4 9.0 %collective-permute-start.2 = (bf16[528,256]{1,0:T(8,128)(2,1)S(1)}, bf16[528,256]{1,0:T(8,128)(2,1)S(1)}, u32[]{:S(2)}, u32[]{:S(2)}) collective-permute-start(bf16[528,256]{1,0:T(8,128)(2,1)S(1)} %collective-permute-done.1.near_ref), channel_id=1, source_target_pairs={{0,1},{1,0},{2,3},{3,2},{4,5},{5,4},{6,7},{7,6},{8,9},{9,8},{10,11... | collective-permute-start | bytes 811016 | tf_op jit(solution)/shard_map/ppermute | solution.py:25
  15.3 4.2 %collective-permute-start.5 = (bf16[256,256]{1,0:T(8,128)(2,1)S(1)}, bf16[256,256]{1,0:T(8,128)(2,1)S(1)}, u32[]{:S(2)}, u32[]{:S(2)}) collective-permute-start(bf16[256,256]{1,0:T(8,128)(2,1)S(1)} %get-tuple-element.39), channel_id=1, source_target_pairs={{0,1},{1,0},{2,3},{3,2},{4,5},{5,4},{6,7},{7,6},{8,9},{9,8},{10,11... | collective-permute-start | bytes 393224 | tf_op jit(solution)/shard_map/ppermute | solution.py:25
  15.3 6.7 %collective-permute-start.11 = (bf16[256,256]{1,0:T(8,128)(2,1)S(1)}, bf16[256,256]{1,0:T(8,128)(2,1)S(1)}, u32[]{:S(2)}, u32[]{:S(2)}) collective-permute-start(bf16[256,256]{1,0:T(8,128)(2,1)S(1)} %slice.47), channel_id=1, source_target_pairs={{0,2},{1,3},{2,0},{3,1},{4,6},{5,7},{6,4},{7,5},{8,10},{9,11},{10,... | collective-permute-start | bytes 393224 | tf_op jit(solution)/shard_map/ppermute | solution.py:25
  18.1 3.8 %collective-permute-start.6 = (bf16[256,256]{1,0:T(8,128)(2,1)S(1)}, bf16[256,256]{1,0:T(8,128)(2,1)S(1)}, u32[]{:S(2)}, u32[]{:S(2)}) collective-permute-start(bf16[256,256]{1,0:T(8,128)(2,1)S(1)} %slice.44), channel_id=1, source_target_pairs={{0,1},{1,0},{2,3},{3,2},{4,5},{5,4},{6,7},{7,6},{8,9},{9,8},{10,11... | collective-permute-start | bytes 393224 | tf_op jit(solution)/shard_map/ppermute | solution.py:25
  19.5 3.1 %collective-permute-start.7 = (bf16[512,256]{1,0:T(8,128)(2,1)S(1)}, bf16[512,256]{1,0:T(8,128)(2,1)S(1)}, u32[]{:S(2)}, u32[]{:S(2)}) collective-permute-start(bf16[512,256]{1,0:T(8,128)(2,1)S(1)} %slice.45), channel_id=1, source_target_pairs={{0,1},{1,0},{2,3},{3,2},{4,5},{5,4},{6,7},{7,6},{8,9},{9,8},{10,11... | collective-permute-start | bytes 786440 | tf_op jit(solution)/shard_map/ppermute | solution.py:25
  19.8 4.0 %collective-permute-start.12 = (bf16[512,256]{1,0:T(8,128)(2,1)S(1)}, bf16[512,256]{1,0:T(8,128)(2,1)S(1)}, u32[]{:S(2)}, u32[]{:S(2)}) collective-permute-start(bf16[512,256]{1,0:T(8,128)(2,1)S(1)} %collective-permute-done.10.refs_4_), channel_id=1, source_target_pairs={{0,1},{1,0},{2,3},{3,2},{4,5},{5,4},{6,7},{7,6},{8,9},{9,8},{10,11... | collective-permute-start | bytes 786440 | tf_op jit(solution)/shard_map/ppermute | solution.py:25
  21.9 1.5 %collective-permute-start.13 = (bf16[256,256]{1,0:T(8,128)(2,1)S(1)}, bf16[256,256]{1,0:T(8,128)(2,1)S(1)}, u32[]{:S(2)}, u32[]{:S(2)}) collective-permute-start(bf16[256,256]{1,0:T(8,128)(2,1)S(1)} %collective-permute-done.11.refs_5_), channel_id=1, source_target_pairs={{0,1},{1,0},{2,3},{3,2},{4,5},{5,4},{6,7},{7,6},{8,9},{9,8},{10,11... | collective-permute-start | bytes 393224 | tf_op jit(solution)/shard_map/ppermute | solution.py:25
  21.9 1.5 %collective-permute-start.8 = (bf16[256,256]{1,0:T(8,128)(2,1)S(1)}, bf16[256,256]{1,0:T(8,128)(2,1)S(1)}, u32[]{:S(2)}, u32[]{:S(2)}) collective-permute-start(bf16[256,256]{1,0:T(8,128)(2,1)S(1)} %get-tuple-element.36.refs_0_.seed_ref), channel_id=1, source_target_pairs={{0,1},{1,0},{2,3},{3,2},{4,5},{5,4},{6,7},{7,6},{8,9},{9,8},{10,11... | collective-permute-start | bytes 393224 | tf_op jit(solution)/shard_map/ppermute | solution.py:25
  22.5 1.3 %collective-permute-start.14 = (bf16[256,256]{1,0:T(8,128)(2,1)S(1)}, bf16[256,256]{1,0:T(8,128)(2,1)S(1)}, u32[]{:S(2)}, u32[]{:S(2)}) collective-permute-start(bf16[256,256]{1,0:T(8,128)(2,1)S(1)} %get-tuple-element.25.refs_11_), channel_id=1, source_target_pairs={{0,1},{1,0},{2,3},{3,2},{4,5},{5,4},{6,7},{7,6},{8,9},{9,8},{10,11... | collective-permute-start | bytes 393224 | tf_op jit(solution)/shard_map/ppermute | solution.py:25
  25.1 7.7 %collective-permute-start.17 = (bf16[256,256]{1,0:T(8,128)(2,1)S(1)}, bf16[256,256]{1,0:T(8,128)(2,1)S(1)}, u32[]{:S(2)}, u32[]{:S(2)}) collective-permute-start(bf16[256,256]{1,0:T(8,128)(2,1)S(1)} %get-tuple-element.27.refs_2_), channel_id=1, source_target_pairs={{4,0},{8,4},{12,8},{16,12},{20,16},{24,20},{28,24},{5,1},{9,5},{13... | collective-permute-start | bytes 393224 | tf_op jit(solution)/shard_map/ppermute | solution.py:30
  29.7 4.1 %collective-permute-start.15 = (bf16[256,256]{1,0:T(8,128)(2,1)S(1)}, bf16[256,256]{1,0:T(8,128)(2,1)S(1)}, u32[]{:S(2)}, u32[]{:S(2)}) collective-permute-start(bf16[256,256]{1,0:T(8,128)(2,1)S(1)} %get-tuple-element.27.refs_2_), channel_id=1, source_target_pairs={{0,1},{1,0},{2,3},{3,2},{4,5},{5,4},{6,7},{7,6},{8,9},{9,8},{10,11... | collective-permute-start | bytes 393224 | tf_op jit(solution)/shard_map/ppermute | solution.py:25
  31.7 2.1 %collective-permute-start.16 = (bf16[256,256]{1,0:T(8,128)(2,1)S(1)}, bf16[256,256]{1,0:T(8,128)(2,1)S(1)}, u32[]{:S(2)}, u32[]{:S(2)}) collective-permute-start(bf16[256,256]{1,0:T(8,128)(2,1)S(1)} %get-tuple-element.34.refs_3_), channel_id=1, source_target_pairs={{0,1},{1,0},{2,3},{3,2},{4,5},{5,4},{6,7},{7,6},{8,9},{9,8},{10,11... | collective-permute-start | bytes 393224 | tf_op jit(solution)/shard_map/ppermute | solution.py:25
  32.8 2.0 %collective-permute-start.18 = (bf16[256,256]{1,0:T(8,128)(2,1)S(1)}, bf16[256,256]{1,0:T(8,128)(2,1)S(1)}, u32[]{:S(2)}, u32[]{:S(2)}) collective-permute-start(bf16[256,256]{1,0:T(8,128)(2,1)S(1)} %collective-permute-done.17.labels_ref), channel_id=1, source_target_pairs={{0,1},{1,0},{2,3},{3,2},{4,5},{5,4},{6,7},{7,6},{8,9},{9,8},{10,11... | collective-permute-start | bytes 393224 | tf_op jit(solution)/shard_map/ppermute | solution.py:25
